TPU v7x, 32 devices: a whole 2x2x4 slice. The times are simulated.
32 devices in a mesh: dp: 8 (over z, x), pix: 4 (over y, core).
Axes of the slice: x: 2, y: 2, z: 4, core: 2. Of those that a mesh axis runs over, the one named last changes fastest.
Arguments:
- images: bfloat16 [8, 32, 32, 1024], P('dp', 'pix'), may hold values from -6 to 6
- style_codes: bfloat16 [8, 512], P('dp'), may hold values from -6 to 6
- labels: int32 [8], P('dp'), may hold values from 0 to 999
- token_ids: int32 [8, 77], P('dp'), may hold values from 0 to 24703
- penalty_mask: int32 [8], P('dp'), may hold values 0 or 1
- class_table: bfloat16 [1000, 512], replicated, may hold values from -6 to 6
- text_table: bfloat16 [24704, 768], replicated, may hold values from -6 to 6
- conv_bank: bfloat16 [2, 3, 3, 1024, 1024], P(None, None, None, 'dp', 'pix'), may hold values from -0.0625 to 0.0625
- select_weight: bfloat16 [512, 2], replicated, may hold values from -0.25 to 0.25
- modulation: bfloat16 [512, 1024], replicated, may hold values from -0.125 to 0.125
- rgb_modulation: bfloat16 [512, 1024], replicated, may hold values from -0.125 to 0.125
- w_query: bfloat16 [1024, 1024], P('dp'), may hold values from -0.1875 to 0.1875
- w_key: bfloat16 [1024, 1024], P('dp'), may hold values from -0.1875 to 0.1875
- w_value: bfloat16 [1024, 1024], P('dp'), may hold values from -0.1875 to 0.1875
- w_out: bfloat16 [1024, 1024], P('dp'), may hold values from -0.375 to 0.375
- c_query: bfloat16 [1024, 1024], P('dp'), may hold values from -0.1875 to 0.1875
- c_key: bfloat16 [768, 1024], P('dp'), may hold values from -0.21875 to 0.21875
- c_value: bfloat16 [768, 1024], P('dp'), may hold values from -0.21875 to 0.21875
- c_out: bfloat16 [1024, 1024], P('dp'), may hold values from -0.75 to 0.75
- gain_self: float32 [1024], replicated, may hold values from 0.5 to 1.5
- gain_cross: float32 [1024], replicated, may hold values from 0.5 to 1.5
- rgb_weight: bfloat16 [1024, 3], replicated, may hold values from -0.1875 to 0.1875
- out_cotangent: bfloat16 [8, 32, 32, 1024], P('dp', 'pix'), may hold values from -6 to 6
- rgb_cotangent: float32 [8, 3, 32, 32], P('dp', None, 'pix'), may hold values from -6 to 6
Outputs:
- output: float32 [8, 32, 32, 1024], P('dp', 'pix')
- rgb_image: float32 [8, 3, 32, 32], P('dp', None, 'pix')
- grad_image: float32 [8, 32, 32, 1024], P('dp', 'pix')
- grad_style: float32 [8, 512], P('dp')
- grad_class_table: float32 [1000, 512], replicated
- grad_conv_bank: float32 [2, 3, 3, 1024, 1024], P(None, None, None, 'dp', 'pix')
- grad_select_weight: float32 [512, 2], replicated
- grad_modulation: float32 [512, 1024], replicated
- grad_rgb_modulation: float32 [512, 1024], replicated
- grad_w_query: float32 [1024, 1024], P('dp')
- grad_w_key: float32 [1024, 1024], P('dp')
- grad_w_value: float32 [1024, 1024], P('dp')
- grad_w_out: float32 [1024, 1024], P('dp')
- grad_c_query: float32 [1024, 1024], P('dp')
- grad_c_key: float32 [768, 1024], P('dp')
- grad_c_value: float32 [768, 1024], P('dp')
- grad_c_out: float32 [1024, 1024], P('dp')
- grad_gain_self: float32 [1024], replicated
- grad_gain_cross: float32 [1024], replicated
- grad_rgb_weight: float32 [1024, 3], replicated
All inputs are finite; a program needn't handle non-finite values. No bound on the sum of `penalty_mask` on one device may be relied on, other than what follows from the above.
Results may differ from a plain program's by a relative error of at most 0.025.
The roundings to bfloat16 on the way count: a program that leaves them out, or rounds other values in their place, can miss the bound.
Values may be sent and summed in bfloat16 or wider, within the bound.
A program may use at most 320 MiB of HBM per device.

v0:
```python
from functools import partial

import jax
import jax.numpy as jnp
from jax import lax
from jax.sharding import PartitionSpec as P

HEAD_DIM = 64


penalty_weight = 1.0
highest = lax.Precision.HIGHEST


def padded_2(shard, sides, width):
    for axis, dim in sides:
        count, length = (lax.axis_size(axis), shard.shape[dim])
        up = [(i, (i + 1) % count) for i in range(count - 1)]
        down = [(j, i) for i, j in up]
        last = lax.slice_in_dim(shard, length - width, length, axis=dim)
        initial = lax.slice_in_dim(shard, 0, width, axis=dim)
        before = lax.ppermute(last, axis, up)
        after = lax.ppermute(initial, axis, down)
        shard = jnp.concatenate([before, shard, after], axis=dim)
    return shard


def rms_norm(hidden, gain):
    return hidden * lax.rsqrt(jnp.mean(hidden * hidden, -1, keepdims=True) + 1e-06) * gain


def style_path(onehot, style_in, class_rows, select_mat, modul_mat, rgb_mod_mat):
    styled = style_in + jnp.dot(onehot, class_rows, precision=highest)
    mixing = jax.nn.softmax(jnp.dot(styled, select_mat, precision=highest), -1)
    scaling = jnp.dot(styled, modul_mat, precision=highest) + 1.0
    rgb_scale = jnp.dot(styled, rgb_mod_mat, precision=highest) + 1.0
    return (mixing, scaling, rgb_scale)


def bank_mix(bank_cols, mix_row):
    total = mix_row[0] * bank_cols[0].astype(jnp.float32)
    total = total + mix_row[1] * bank_cols[1].astype(jnp.float32)
    return total


def demodulate(selected, scale_row):
    modded = selected * scale_row[None, None, :, None]
    return modded * lax.rsqrt(jnp.sum(modded * modded, axis=(0, 1, 2)) + 1e-08)


def demodulate_back(selected, scale_row, kernel_grad):
    modded = selected * scale_row[None, None, :, None]
    inverse = lax.rsqrt(jnp.sum(modded * modded, axis=(0, 1, 2)) + 1e-08)
    inner = jnp.sum(kernel_grad * modded, axis=(0, 1, 2))
    grad_modded = inverse * kernel_grad - inverse**3 * inner * modded
    grad_selected = grad_modded * scale_row[None, None, :, None]
    return (grad_selected, jnp.sum(grad_modded * selected, axis=(0, 1, 3)))


def conv_rows(padded, kernel, height, width, flipped):
    channels = padded.shape[-1]
    out_width = kernel.shape[-2] if flipped else kernel.shape[-1]
    total = jnp.zeros((height * width, out_width), jnp.float32)
    for row_off in range(3):
        for col_off in range(3):
            window = padded[row_off : row_off + height, col_off : col_off + width].reshape(
                height * width, channels
            )
            if flipped:
                total = total + lax.dot_general(
                    window,
                    kernel[2 - row_off, 2 - col_off],
                    (((1,), (1,)), ((), ())),
                    preferred_element_type=jnp.float32,
                )
            else:
                total = total + jnp.dot(
                    window, kernel[row_off, col_off], preferred_element_type=jnp.float32
                )
    return total


def conv_weight_grad(padded, grad_rows, height, width):
    channels = padded.shape[-1]
    taps = []
    for row_off in range(3):
        line_taps = []
        for col_off in range(3):
            window = padded[row_off : row_off + height, col_off : col_off + width].reshape(
                height * width, channels
            )
            line_taps.append(
                lax.dot_general(
                    window, grad_rows, (((0,), (0,)), ((), ())), preferred_element_type=jnp.float32
                )
            )
        taps.append(jnp.stack(line_taps))
    return jnp.stack(taps)


def split_heads(source):
    samples_here, length, local_width = source.shape
    return source.reshape(samples_here, length, local_width // HEAD_DIM, HEAD_DIM)


def distance_scores(query_block, key_heads, key_norm):
    score_scale = HEAD_DIM ** (-0.5)
    inner = jnp.einsum(
        "bqhd,bkhd->bhqk", query_block, key_heads, preferred_element_type=jnp.float32
    )
    return score_scale * (2.0 * inner - key_norm[:, :, None, :])


def distance_attention(queries, keys, values):
    query_heads = split_heads(queries)
    key_heads = split_heads(keys)
    value_heads = split_heads(values)
    length = key_heads.shape[1]
    block_rows = min(512, length)
    key_norm = jnp.sum(jnp.square(key_heads.astype(jnp.float32)), -1).transpose(0, 2, 1)
    outputs = []
    totals = []
    for offset in range(0, length, block_rows):
        scores = distance_scores(query_heads[:, offset : offset + block_rows], key_heads, key_norm)
        largest = jnp.max(scores, -1, keepdims=True)
        expanded = jnp.exp(scores - largest)
        summed = jnp.sum(expanded, -1, keepdims=True)
        weights = (expanded / summed).astype(jnp.bfloat16)
        outputs.append(
            jnp.einsum("bhqk,bkhd->bqhd", weights, value_heads, preferred_element_type=jnp.float32)
        )
        totals.append(largest[..., 0] + jnp.log(summed[..., 0]))
    attended = jnp.concatenate(outputs, axis=1)
    return (attended.reshape(queries.shape), jnp.concatenate(totals, axis=2))


def distance_attention_back(queries, keys, values, log_totals, grad_out):
    score_scale = HEAD_DIM ** (-0.5)
    query_heads = split_heads(queries)
    key_heads = split_heads(keys)
    value_heads = split_heads(values)
    grad_heads = split_heads(grad_out)
    length = key_heads.shape[1]
    block_rows = min(512, length)
    key_float = key_heads.astype(jnp.float32)
    key_norm = jnp.sum(jnp.square(key_float), -1).transpose(0, 2, 1)
    grad_keys = jnp.zeros(key_heads.shape, jnp.float32)
    grad_values = jnp.zeros(value_heads.shape, jnp.float32)
    column_sum = jnp.zeros(key_norm.shape, jnp.float32)
    grad_queries = []
    for offset in range(0, length, block_rows):
        query_block = query_heads[:, offset : offset + block_rows]
        grad_block = grad_heads[:, offset : offset + block_rows]
        scores = distance_scores(query_block, key_heads, key_norm)
        probs = jnp.exp(scores - log_totals[:, :, offset : offset + block_rows, None])
        grad_probs = jnp.einsum(
            "bqhd,bkhd->bhqk", grad_block, value_heads, preferred_element_type=jnp.float32
        )
        grad_values = grad_values + jnp.einsum(
            "bhqk,bqhd->bkhd",
            probs.astype(jnp.bfloat16),
            grad_block,
            preferred_element_type=jnp.float32,
        )
        grad_scores = (
            probs * (grad_probs - jnp.sum(grad_probs * probs, -1, keepdims=True))
        ).astype(jnp.bfloat16)
        grad_queries.append(
            2.0
            * score_scale
            * jnp.einsum(
                "bhqk,bkhd->bqhd", grad_scores, key_heads, preferred_element_type=jnp.float32
            )
        )
        grad_keys = grad_keys + 2.0 * score_scale * jnp.einsum(
            "bhqk,bqhd->bkhd", grad_scores, query_block, preferred_element_type=jnp.float32
        )
        column_sum = column_sum + jnp.sum(grad_scores.astype(jnp.float32), axis=2)
    grad_keys = grad_keys - 2.0 * score_scale * key_float * column_sum.transpose(0, 2, 1)[..., None]
    grad_query_all = (
        jnp.concatenate(grad_queries, axis=1).reshape(queries.shape).astype(jnp.bfloat16)
    )
    return (
        grad_query_all,
        grad_keys.reshape(keys.shape).astype(jnp.bfloat16),
        grad_values.reshape(values.shape).astype(jnp.bfloat16),
    )


def cross_attention(cross_query, cross_key, cross_value):
    score_scale = HEAD_DIM ** (-0.5)
    scores = score_scale * jnp.einsum(
        "bqhd,bkhd->bhqk",
        split_heads(cross_query),
        split_heads(cross_key),
        preferred_element_type=jnp.float32,
    )
    probs = jax.nn.softmax(scores, -1)
    attended = jnp.einsum(
        "bhqk,bkhd->bqhd",
        probs.astype(jnp.bfloat16),
        split_heads(cross_value),
        preferred_element_type=jnp.float32,
    )
    return (attended.reshape(cross_query.shape), probs)


def cross_attention_back(cross_query, cross_key, cross_value, probs, grad_out):
    score_scale = HEAD_DIM ** (-0.5)
    grad_heads = split_heads(grad_out)
    value_heads = split_heads(cross_value)
    grad_probs = jnp.einsum(
        "bqhd,bkhd->bhqk", grad_heads, value_heads, preferred_element_type=jnp.float32
    )
    grad_value = jnp.einsum(
        "bhqk,bqhd->bkhd",
        probs.astype(jnp.bfloat16),
        grad_heads,
        preferred_element_type=jnp.float32,
    )
    grad_scores = (probs * (grad_probs - jnp.sum(grad_probs * probs, -1, keepdims=True))).astype(
        jnp.bfloat16
    )
    grad_query = score_scale * jnp.einsum(
        "bhqk,bkhd->bqhd", grad_scores, split_heads(cross_key), preferred_element_type=jnp.float32
    )
    grad_key = score_scale * jnp.einsum(
        "bhqk,bqhd->bkhd", grad_scores, split_heads(cross_query), preferred_element_type=jnp.float32
    )
    return (
        grad_query.reshape(cross_query.shape).astype(jnp.bfloat16),
        grad_key.reshape(cross_key.shape),
        grad_value.reshape(cross_value.shape),
    )


def on_device(
    images,
    style_codes,
    labels,
    token_ids,
    penalty_mask,
    class_table,
    text_table,
    conv_bank,
    select_weight,
    modulation,
    rgb_modulation,
    w_query,
    w_key,
    w_value,
    w_out,
    c_query,
    c_key,
    c_value,
    c_out,
    gain_self,
    gain_cross,
    rgb_weight,
    out_cotangent,
    rgb_cotangent,
):
    floats = jnp.float32
    halves = jnp.bfloat16
    samples_here, height, width, channels = images.shape
    tokens = height * width
    (
        bank_cols,
        query_full,
        key_full,
        value_full,
        out_full,
        cquery_full,
        ckey_full,
        cvalue_full,
        cout_full,
    ) = (
        lax.all_gather(conv_bank, "dp", axis=3, tiled=True),
        lax.all_gather(w_query, "dp", axis=0, tiled=True),
        lax.all_gather(w_key, "dp", axis=0, tiled=True),
        lax.all_gather(w_value, "dp", axis=0, tiled=True),
        lax.all_gather(w_out, "dp", axis=0, tiled=True),
        lax.all_gather(c_query, "dp", axis=0, tiled=True),
        lax.all_gather(c_key, "dp", axis=0, tiled=True),
        lax.all_gather(c_value, "dp", axis=0, tiled=True),
        lax.all_gather(c_out, "dp", axis=0, tiled=True),
    )
    onehot = (labels[:, None] == jnp.arange(class_table.shape[0], dtype=jnp.int32)[None, :]).astype(
        floats
    )
    (mixing, scaling, rgb_scale), style_back = jax.vjp(
        partial(style_path, onehot),
        style_codes.astype(floats),
        class_table.astype(floats),
        select_weight.astype(floats),
        modulation.astype(floats),
        rgb_modulation.astype(floats),
    )
    kernel_part = jnp.stack([demodulate(bank_mix(bank_cols, mixing[0]), scaling[0]).astype(halves)])
    kernels = lax.all_gather(kernel_part, "pix", axis=4, tiled=True)
    padded = padded_2(images, (("pix", 1),), 1)
    padded = jnp.pad(padded, ((0, 0), (0, 0), (1, 1), (0, 0)))
    conv_out = jnp.stack([conv_rows(padded[0], kernels[0], height, width, False)])
    hidden_one = images.reshape(samples_here, tokens, channels).astype(floats) + jax.nn.silu(
        conv_out
    )
    normed_one, norm_one_back = jax.vjp(rms_norm, hidden_one, gain_self)
    normed_one = normed_one.astype(halves)
    query = jnp.dot(normed_one, query_full, preferred_element_type=floats).astype(halves)
    key_proj = jnp.dot(normed_one, key_full, preferred_element_type=floats).astype(halves)
    value_proj = jnp.dot(normed_one, value_full, preferred_element_type=floats).astype(halves)
    query_heads, key_heads, value_heads = (
        lax.all_to_all(query, "pix", split_axis=2, concat_axis=1, tiled=True),
        lax.all_to_all(key_proj, "pix", split_axis=2, concat_axis=1, tiled=True),
        lax.all_to_all(value_proj, "pix", split_axis=2, concat_axis=1, tiled=True),
    )
    attended_heads, log_totals = distance_attention(query_heads, key_heads, value_heads)
    attended = lax.all_to_all(
        attended_heads.astype(halves), "pix", split_axis=1, concat_axis=2, tiled=True
    )
    hidden_two = hidden_one + jnp.dot(attended, out_full, preferred_element_type=floats)
    normed_two, norm_two_back = jax.vjp(rms_norm, hidden_two, gain_cross)
    normed_two = normed_two.astype(halves)
    cross_query = jnp.dot(normed_two, cquery_full, preferred_element_type=floats).astype(halves)
    text_rows = jnp.take(text_table, token_ids, axis=0)
    cross_key = jnp.dot(text_rows, ckey_full, preferred_element_type=floats).astype(halves)
    cross_value = jnp.dot(text_rows, cvalue_full, preferred_element_type=floats).astype(halves)
    cross_attended, cross_probs = cross_attention(cross_query, cross_key, cross_value)
    cross_attended = cross_attended.astype(halves)
    hidden_three = hidden_two + jnp.dot(cross_attended, cout_full, preferred_element_type=floats)
    output = hidden_three.reshape(samples_here, height, width, channels)
    mixed = (hidden_three * rgb_scale[:, None, :]).astype(halves)
    rgb_flat = jnp.dot(mixed, rgb_weight, preferred_element_type=floats)
    rgb_image = jnp.transpose(rgb_flat, (0, 2, 1)).reshape(samples_here, 3, height, width)
    rgb_grad = (
        rgb_cotangent
        + penalty_weight * penalty_mask.astype(floats)[:, None, None, None] * rgb_image
    )
    rgb_grad_flat = rgb_grad.reshape(samples_here, 3, tokens)
    mixed_float = mixed.astype(floats)
    grad_rgb_weight = jnp.einsum("bct,btd->dc", rgb_grad_flat, mixed_float, precision=highest)
    grad_mixed = jnp.einsum(
        "bct,dc->btd", rgb_grad_flat, rgb_weight.astype(floats), precision=highest
    )
    grad_three = (
        out_cotangent.reshape(samples_here, tokens, channels).astype(floats)
        + grad_mixed * rgb_scale[:, None, :]
    )
    grad_rgb_scale = jnp.sum(grad_mixed * hidden_three, axis=1)
    grad_cross_proj = grad_three.astype(halves)
    grad_c_out = jnp.einsum(
        "btc,btd->cd", cross_attended, grad_cross_proj, preferred_element_type=floats
    )
    grad_cross_out = jnp.einsum(
        "btd,cd->btc", grad_cross_proj, cout_full, preferred_element_type=floats
    ).astype(halves)
    grad_cross_query, grad_cross_key, grad_cross_value = cross_attention_back(
        cross_query, cross_key, cross_value, cross_probs, grad_cross_out
    )
    grad_c_query = jnp.einsum(
        "btc,btd->cd", normed_two, grad_cross_query, preferred_element_type=floats
    )
    text_float = text_rows.astype(floats)
    grad_c_key = jnp.einsum("btc,btd->cd", text_float, grad_cross_key, precision=highest)
    grad_c_value = jnp.einsum("btc,btd->cd", text_float, grad_cross_value, precision=highest)
    grad_normed_two = jnp.einsum(
        "btd,cd->btc", grad_cross_query, cquery_full, preferred_element_type=floats
    )
    grad_norm_two, grad_gain_cross = norm_two_back(grad_normed_two)
    grad_two = grad_three + grad_norm_two
    grad_attn_proj = grad_two.astype(halves)
    grad_w_out = jnp.einsum("btc,btd->cd", attended, grad_attn_proj, preferred_element_type=floats)
    grad_attended = jnp.einsum(
        "btd,cd->btc", grad_attn_proj, out_full, preferred_element_type=floats
    ).astype(halves)
    grad_heads = lax.all_to_all(grad_attended, "pix", split_axis=2, concat_axis=1, tiled=True)
    grad_query_heads, grad_key_heads, grad_value_heads = distance_attention_back(
        query_heads, key_heads, value_heads, log_totals, grad_heads
    )
    grad_query, grad_key, grad_value = (
        lax.all_to_all(grad_query_heads, "pix", split_axis=1, concat_axis=2, tiled=True),
        lax.all_to_all(grad_key_heads, "pix", split_axis=1, concat_axis=2, tiled=True),
        lax.all_to_all(grad_value_heads, "pix", split_axis=1, concat_axis=2, tiled=True),
    )
    grad_w_query = jnp.einsum("btc,btd->cd", normed_one, grad_query, preferred_element_type=floats)
    grad_w_key = jnp.einsum("btc,btd->cd", normed_one, grad_key, preferred_element_type=floats)
    grad_w_value = jnp.einsum("btc,btd->cd", normed_one, grad_value, preferred_element_type=floats)
    grad_normed_one = jnp.einsum(
        "btd,cd->btc", grad_query, query_full, preferred_element_type=floats
    )
    grad_normed_one = grad_normed_one + jnp.einsum(
        "btd,cd->btc", grad_key, key_full, preferred_element_type=floats
    )
    grad_normed_one = grad_normed_one + jnp.einsum(
        "btd,cd->btc", grad_value, value_full, preferred_element_type=floats
    )
    grad_norm_one, grad_gain_self = norm_one_back(grad_normed_one)
    grad_one = grad_two + grad_norm_one
    silu_values, silu_back = jax.vjp(jax.nn.silu, conv_out)
    grad_conv = silu_back(grad_one)[0].astype(halves)
    grad_padded = padded_2(
        grad_conv.reshape(samples_here, height, width, channels), (("pix", 1),), 1
    )
    grad_padded = jnp.pad(grad_padded, ((0, 0), (0, 0), (1, 1), (0, 0)))
    grad_through = jnp.stack([conv_rows(grad_padded[0], kernels[0], height, width, True)])
    grad_image = (grad_one + grad_through).reshape(samples_here, height, width, channels)
    kernel_grads = jnp.stack([conv_weight_grad(padded[0], grad_conv[0], height, width)])
    kernel_grad_part = lax.psum_scatter(kernel_grads, "pix", scatter_dimension=4, tiled=True)
    selected = bank_mix(bank_cols, mixing[0])
    grad_selected, grad_scale_row = demodulate_back(selected, scaling[0], kernel_grad_part[0])
    mixing_grads = [
        jnp.stack(
            [
                jnp.sum(grad_selected * bank_cols[index].astype(floats))
                for index in range(bank_cols.shape[0])
            ]
        )
    ]
    scaling_grads = [grad_scale_row]
    grad_bank = mixing[0][:, None, None, None, None] * grad_selected[None]
    grad_mixing = jnp.stack(mixing_grads)
    grad_scaling = jnp.stack(scaling_grads)
    grad_codes, grad_table, grad_select, grad_modulation, grad_rgb_mod = style_back(
        (grad_mixing, grad_scaling, grad_rgb_scale)
    )
    owned = (
        lax.psum_scatter(grad_bank, "dp", scatter_dimension=3, tiled=True),
        lax.psum_scatter(grad_w_query, "dp", scatter_dimension=0, tiled=True),
        lax.psum_scatter(grad_w_key, "dp", scatter_dimension=0, tiled=True),
        lax.psum_scatter(grad_w_value, "dp", scatter_dimension=0, tiled=True),
        lax.psum_scatter(grad_w_out, "dp", scatter_dimension=0, tiled=True),
        lax.psum_scatter(grad_c_query, "dp", scatter_dimension=0, tiled=True),
        lax.psum_scatter(grad_c_key, "dp", scatter_dimension=0, tiled=True),
        lax.psum_scatter(grad_c_value, "dp", scatter_dimension=0, tiled=True),
        lax.psum_scatter(grad_c_out, "dp", scatter_dimension=0, tiled=True),
    )
    summed = lax.psum(
        (
            owned[1],
            owned[2],
            owned[3],
            owned[4],
            owned[5],
            owned[6],
            owned[7],
            owned[8],
            grad_codes,
        ),
        "pix",
    )
    weight_sums = (owned[0],) + tuple(summed[:8])
    grad_style = summed[8]
    small = lax.psum(
        (
            grad_table,
            grad_select,
            grad_modulation,
            grad_rgb_mod,
            grad_gain_self,
            grad_gain_cross,
            grad_rgb_weight,
        ),
        ("dp", "pix"),
    )
    return (
        output,
        rgb_image,
        grad_image,
        grad_style,
        small[0],
        weight_sums[0],
        small[1],
        small[2],
        small[3],
        weight_sums[1],
        weight_sums[2],
        weight_sums[3],
        weight_sums[4],
        weight_sums[5],
        weight_sums[6],
        weight_sums[7],
        weight_sums[8],
        small[4],
        small[5],
        small[6],
    )


def solution(mesh):
    return jax.shard_map(
        on_device,
        mesh=mesh,
        in_specs=(
            P("dp", "pix", None, None),
            P("dp", None),
            P("dp"),
            P("dp", None),
            P("dp"),
            P(),
            P(),
            P(None, None, None, "dp", "pix"),
            P(),
            P(),
            P(),
            P("dp", None),
            P("dp", None),
            P("dp", None),
            P("dp", None),
            P("dp", None),
            P("dp", None),
            P("dp", None),
            P("dp", None),
            P(),
            P(),
            P(),
            P("dp", "pix", None, None),
            P("dp", None, "pix", None),
        ),
        out_specs=(
            P("dp", "pix", None, None),
            P("dp", None, "pix", None),
            P("dp", "pix", None, None),
            P("dp", None),
            P(),
            P(None, None, None, "dp", "pix"),
            P(),
            P(),
            P(),
            P("dp", None),
            P("dp", None),
            P("dp", None),
            P("dp", None),
            P("dp", None),
            P("dp", None),
            P("dp", None),
            P("dp", None),
            P(),
            P(),
            P(),
        ),
        check_vma=False,
    )
```

profile of v0, /device:TPU:0, one launch (start us, length us, event | category | flops | bytes accessed | tf_op | source)
XLA Modules:
  0.0 2252.7 jit_solution(14423813748432136753)
XLA Ops:
  16.4 134.6 %all-gather.11.cloned.1.call-done = bf16[2,3,3,1024,256]{4,3,2,1,0:T(8,128)(2,1)} async-done(((bf16[2,3,3,128,256]{4,3,2,1,0:T(8,128)(2,1)}), bf16[2,3,3,1024,256]{4,3,2,1,0:T(8,128)(2,1)}) %all-gather.11.cloned.1.call-update) | async-done | bytes 9437200 | tf_op jit(solution)/shard_map/all_gather | solution.py:278
  180.7 104.5 %all-gather.13.cloned.1.call-done = bf16[1,3,3,1024,1024]{4,3,2,1,0:T(8,128)(2,1)} async-done(((bf16[1,3,3,1024,256]{4,3,2,1,0:T(8,128)(2,1)}), bf16[1,3,3,1024,1024]{4,3,2,1,0:T(8,128)(2,1)}) %all-gather.13.cloned.1.call-update) | async-done | bytes 18874384 | tf_op jit(solution)/shard_map/all_gather | solution.py:300
  308.2 28.4 %all-gather.19.cloned.1.call-done = bf16[1024,1024]{1,0:T(8,128)(2,1)} async-done(((bf16[128,1024]{1,0:T(8,128)(2,1)}), bf16[1024,1024]{1,0:T(8,128)(2,1)}) %all-gather.19.cloned.1.call-update) | async-done | bytes 2097168 | tf_op jit(solution)/shard_map/all_gather | solution.py:280
  350.8 35.5 %all-gather.17.cloned.1.call-done = bf16[1024,1024]{1,0:T(8,128)(2,1)} async-done(((bf16[128,1024]{1,0:T(8,128)(2,1)}), bf16[1024,1024]{1,0:T(8,128)(2,1)}) %all-gather.17.cloned.1.call-update) | async-done | bytes 2097168 | tf_op jit(solution)/shard_map/all_gather | solution.py:279
  404.7 31.4 %all-gather.15.cloned.1.call-done = bf16[1024,1024]{1,0:T(8,128)(2,1)} async-done(((bf16[128,1024]{1,0:T(8,128)(2,1)}), bf16[1024,1024]{1,0:T(8,128)(2,1)}) %all-gather.15.cloned.1.call-update) | async-done | bytes 2097168 | tf_op jit(solution)/shard_map/all_gather | solution.py:281
  510.7 15.4 all-gather.27.cloned.1.call-done
  533.3 43.1 %all-gather.21.cloned.1.call-done = bf16[1024,1024]{1,0:T(8,128)(2,1)} async-done(((bf16[128,1024]{1,0:T(8,128)(2,1)}), bf16[1024,1024]{1,0:T(8,128)(2,1)}) %all-gather.21.cloned.1.call-update) | async-done | bytes 2097168 | tf_op jit(solution)/shard_map/all_gather | solution.py:282
  580.1 46.2 %all-gather.25.cloned.1.call-done = bf16[1024,1024]{1,0:T(8,128)(2,1)} async-done(((bf16[128,1024]{1,0:T(8,128)(2,1)}), bf16[1024,1024]{1,0:T(8,128)(2,1)}) %all-gather.25.cloned.1.call-update) | async-done | bytes 2097168 | tf_op jit(solution)/shard_map/all_gather | solution.py:283
  637.3 38.8 %all-gather.29.cloned.1.call-done = bf16[1024,1024]{1,0:T(8,128)(2,1)} async-done(((bf16[128,1024]{1,0:T(8,128)(2,1)}), bf16[1024,1024]{1,0:T(8,128)(2,1)}) %all-gather.29.cloned.1.call-update) | async-done | bytes 2097168 | tf_op jit(solution)/shard_map/all_gather | solution.py:286
  781.0 12.3 all_to_all.120
  816.3 12.3 all_to_all.121
  856.6 12.5 all_to_all.122
  905.6 10.7 maximum_bitcast_fusion.1
  916.3 17.8 maximum_bitcast_fusion
  940.8 91.6 %reduce-scatter.23.cloned.1.call-done = f32[128,1024]{1,0:T(8,128)} async-done(((f32[1024,1024]{1,0:T(8,128)}), f32[128,1024]{1,0:T(8,128)}) %reduce-scatter.23.cloned.1.call-update) | async-done | bytes 524304 | tf_op jit(solution)/shard_map/reduce_scatter | solution.py:432
  1032.4 91.3 %reduce-scatter.29.cloned.1.call-done = f32[128,1024]{1,0:T(8,128)} async-done(((f32[1024,1024]{1,0:T(8,128)}), f32[128,1024]{1,0:T(8,128)}) %reduce-scatter.29.cloned.1.call-update) | async-done | bytes 524304 | tf_op jit(solution)/shard_map/reduce_scatter | solution.py:435
  1123.7 91.6 %reduce-scatter.15.cloned.1.call-done = f32[128,1024]{1,0:T(8,128)} async-done(((f32[1024,1024]{1,0:T(8,128)}), f32[128,1024]{1,0:T(8,128)}) %reduce-scatter.15.cloned.1.call-update) | async-done | bytes 524304 | tf_op jit(solution)/shard_map/reduce_scatter | solution.py:428
  1215.4 91.3 %reduce-scatter.17.cloned.1.call-done = f32[128,1024]{1,0:T(8,128)} async-done(((f32[1024,1024]{1,0:T(8,128)}), f32[128,1024]{1,0:T(8,128)}) %reduce-scatter.17.cloned.1.call-update) | async-done | bytes 524304 | tf_op jit(solution)/shard_map/reduce_scatter | solution.py:429
  1306.7 91.7 %reduce-scatter.19.cloned.1.call-done = f32[128,1024]{1,0:T(8,128)} async-done(((f32[1024,1024]{1,0:T(8,128)}), f32[128,1024]{1,0:T(8,128)}) %reduce-scatter.19.cloned.1.call-update) | async-done | bytes 524304 | tf_op jit(solution)/shard_map/reduce_scatter | solution.py:430
  1398.4 263.8 %reduce-scatter.11.cloned.1.call-done = f32[1,3,3,1024,256]{4,3,2,1,0:T(8,128)} async-done(((f32[1,3,3,1024,1024]{4,3,2,1,0:T(8,128)}), f32[1,3,3,1024,256]{4,3,2,1,0:T(8,128)}) %reduce-scatter.11.cloned.1.call-update) | async-done | bytes 9437200 | tf_op jit(solution)/shard_map/reduce_scatter | solution.py:408
  1672.1 10.5 fusion.6
  1738.2 44.7 %all-reduce.2 = (f32[512,2]{0,1:T(2,128)}, f32[1024]{0:T(1024)}, f32[1024]{0:T(1024)}, f32[1024,3]{0,1:T(4,128)}) all-reduce(f32[512,2]{0,1:T(2,128)S(1)} %broadcast_multiply_fusion.4, f32[1024]{0:T(1024)S(1)} %get-tuple-element.105, f32[1024]{0:T(1024)S(1)} %copy-done.90, ...), channel_id=1, replica_groups=mesh['dp'=8,'pix'=4] {'dp','pix'}, use_global_device_ids=true, to_apply=%region_29.30 | all-reduce | flops 6144 | bytes 49152 | tf_op jit(solution)/shard_map/psum | solution.py:453
  1789.7 124.3 %all-reduce.8.cloned.1.call-done = (f32[1000,512]{1,0:T(8,128)}, f32[512,1024]{1,0:T(8,128)}, f32[512,1024]{1,0:T(8,128)}) async-done(((f32[1000,512]{1,0:T(8,128)}, f32[512,1024]{1,0:T(8,128)}, f32[512,1024]{1,0:T(8,128)}), (f32[1000,512]{1,0:T(8,128)}, f32[512,1024]{1,0:T(8,128)}, f32[512,1024]{1,0:T(8,128)})) %all-reduce.8.cloned.1.call-update) | async-done | bytes 6242320 | tf_op jit(solution)/shard_map/psum | solution.py:453
  1913.9 317.7 %reduce-scatter.13.cloned.1.call-done = f32[2,3,3,128,256]{4,3,2,1,0:T(8,128)} async-done(((f32[2,3,3,1024,256]{4,3,2,1,0:T(8,128)}), f32[2,3,3,128,256]{4,3,2,1,0:T(8,128)}) %reduce-scatter.13.cloned.1.call-update) | async-done | bytes 2359312 | tf_op jit(solution)/shard_map/reduce_scatter | solution.py:427
  (491 shorter events, 471.1 us)
Async XLA Ops:
  7.2 143.8 %all-gather.11.cloned.1.call-start = ((), (), s32[]{:S(2)}) async-start(), calls=%async_computation.18 | async-start | bytes 10616832 | tf_op jit(solution)/shard_map/all_gather | solution.py:278
  7.9 277.2 %all-gather.13.cloned.1.call-start = ((), (), s32[]{:S(2)}) async-start(), calls=%async_computation.19 | async-start | bytes 23592960 | tf_op jit(solution)/shard_map/all_gather | solution.py:300
  164.2 172.3 %all-gather.19.cloned.1.call-start = ((), (), s32[]{:S(2)}) async-start(), calls=%async_computation.22 | async-start | bytes 2359296 | tf_op jit(solution)/shard_map/all_gather | solution.py:280
  165.0 221.4 %all-gather.17.cloned.1.call-start = ((), (), s32[]{:S(2)}) async-start(), calls=%async_computation.21 | async-start | bytes 2359296 | tf_op jit(solution)/shard_map/all_gather | solution.py:279
  165.6 270.6 %all-gather.15.cloned.1.call-start = ((), (), s32[]{:S(2)}) async-start(), calls=%async_computation.20 | async-start | bytes 2359296 | tf_op jit(solution)/shard_map/all_gather | solution.py:281
  166.1 341.9 %all-gather.23.cloned.1.call-start = ((), (), s32[]{:S(2)}) async-start(), calls=%async_computation.24 | async-start | bytes 1769472 | tf_op jit(solution)/shard_map/all_gather | solution.py:285
  166.7 359.4 %all-gather.27.cloned.1.call-start = ((), (), s32[]{:S(2)}) async-start(), calls=%async_computation.26 | async-start | bytes 1769472 | tf_op jit(solution)/shard_map/all_gather | solution.py:284
  167.5 408.9 %all-gather.21.cloned.1.call-start = ((), (), s32[]{:S(2)}) async-start(), calls=%async_computation.23 | async-start | bytes 2359296 | tf_op jit(solution)/shard_map/all_gather | solution.py:282
  168.2 458.1 %all-gather.25.cloned.1.call-start = ((), (), s32[]{:S(2)}) async-start(), calls=%async_computation.25 | async-start | bytes 2359296 | tf_op jit(solution)/shard_map/all_gather | solution.py:283
  169.0 507.1 %all-gather.29.cloned.1.call-start = ((), (), s32[]{:S(2)}) async-start(), calls=%async_computation.27 | async-start | bytes 2359296 | tf_op jit(solution)/shard_map/all_gather | solution.py:286
  347.1 53.4 %all-to-all-start.2 = ((bf16[4,2,32768]{2,1,0:T(2,128)(2,1)}), bf16[4,2,32768]{2,1,0:T(2,128)(2,1)S(1)}, u32[]{:S(2)}, u32[]{:S(2)}) async-start(bf16[4,2,32768]{2,1,0:T(2,128)(2,1)} %reshape.1009), calls=%async_computation.2 | async-start | bytes 1048576 | tf_op jit(solution)/shard_map/all_to_all | solution.py:314
  400.5 56.0 %all-to-all-start.1 = ((bf16[4,2,32768]{2,1,0:T(2,128)(2,1)}), bf16[4,2,32768]{2,1,0:T(2,128)(2,1)}, u32[]{:S(2)}, u32[]{:S(2)}) async-start(bf16[4,2,32768]{2,1,0:T(2,128)(2,1)} %reshape.1013), calls=%async_computation.1 | async-start | bytes 1048576 | tf_op jit(solution)/shard_map/all_to_all | solution.py:313
  507.9 428.8 %reduce-scatter.25.cloned.1.call-start = ((), (), s32[]{:S(2)}) async-start(), calls=%async_computation.35 | async-start | bytes 3538944 | tf_op jit(solution)/shard_map/reduce_scatter | solution.py:433
  700.0 236.7 %reduce-scatter.27.cloned.1.call-start = ((), (), s32[]{:S(2)}) async-start(), calls=%async_computation.36 | async-start | bytes 3538944 | tf_op jit(solution)/shard_map/reduce_scatter | solution.py:434
  705.0 235.8 %reduce-scatter.21.cloned.1.call-start = ((), (), s32[]{:S(2)}) async-start(), calls=%async_computation.33 | async-start | bytes 4718592 | tf_op jit(solution)/shard_map/reduce_scatter | solution.py:431
  714.5 317.9 %reduce-scatter.23.cloned.1.call-start = ((), (), s32[]{:S(2)}) async-start(), calls=%async_computation.34 | async-start | bytes 4718592 | tf_op jit(solution)/shard_map/reduce_scatter | solution.py:432
  718.5 405.3 %reduce-scatter.29.cloned.1.call-start = ((), (), s32[]{:S(2)}) async-start(), calls=%async_computation.37 | async-start | bytes 4718592 | tf_op jit(solution)/shard_map/reduce_scatter | solution.py:435
  738.5 476.8 %reduce-scatter.15.cloned.1.call-start = ((), (), s32[]{:S(2)}) async-start(), calls=%async_computation.30 | async-start | bytes 4718592 | tf_op jit(solution)/shard_map/reduce_scatter | solution.py:428
  801.2 505.5 %reduce-scatter.17.cloned.1.call-start = ((), (), s32[]{:S(2)}) async-start(), calls=%async_computation.31 | async-start | bytes 4718592 | tf_op jit(solution)/shard_map/reduce_scatter | solution.py:429
  836.7 561.7 %reduce-scatter.19.cloned.1.call-start = ((), (), s32[]{:S(2)}) async-start(), calls=%async_computation.32 | async-start | bytes 4718592 | tf_op jit(solution)/shard_map/reduce_scatter | solution.py:430
  877.0 785.2 %reduce-scatter.11.cloned.1.call-start = ((), (), s32[]{:S(2)}) async-start(), calls=%async_computation.28 | async-start | bytes 47185920 | tf_op jit(solution)/shard_map/reduce_scatter | solution.py:408
  934.1 855.6 %all-reduce.10.cloned.1.call-start = ((), (), s32[]{:S(2)}) async-start(), calls=%async_computation.39 | async-start | bytes 7864320 | tf_op jit(solution)/shard_map/psum | solution.py:437
  1398.4 515.6 %all-reduce.8.cloned.1.call-start = ((), (), s32[]{:S(2)}) async-start(), calls=%async_computation.38 | async-start | bytes 12484608 | tf_op jit(solution)/shard_map/psum | solution.py:453
  1692.1 539.5 %reduce-scatter.13.cloned.1.call-start = ((), (), s32[]{:S(2)}) async-start(), calls=%async_computation.29 | async-start | bytes 21233664 | tf_op jit(solution)/shard_map/reduce_scatter | solution.py:427
  (117 other events, 4203.1 us)
Sparse Core Ops, SparseCore 0:
  10.2 140.7 all-gather.10
  164.4 120.7 all-gather.12
  287.3 49.2 all-gather.18
  338.6 47.7 all-gather.16
  388.3 47.7 all-gather.14
  438.2 42.6 all-gather.22
  483.1 42.9 all-gather.26
  528.2 48.0 all-gather.20
  578.5 47.7 all-gather.24
  628.3 47.7 all-gather.28
  700.1 72.9 reduce-scatter.24
  776.6 73.5 reduce-scatter.26
  853.7 86.9 reduce-scatter.20
  944.7 87.6 reduce-scatter.22
  1035.9 87.7 reduce-scatter.28
  1127.6 87.6 reduce-scatter.14
  1218.8 87.7 reduce-scatter.16
  1310.6 87.6 reduce-scatter.18
  1400.9 261.2 reduce-scatter.10
  1665.2 82.5 all-reduce.9
  1756.1 157.8 all-reduce.7
  1918.4 313.2 reduce-scatter.12
where the time goes:
time: 2260 us; the launch traced here: 2250 us
  waiting for transfers between devices  1660 us (73%)
  matrix products  186 us (8%)
  other arithmetic  152 us (7%)
  local copies, waits for them, and re-layouts  116 us (5%)
  blocking collectives  88.5 us (4%)
  starting transfers between devices  31.4 us (1%)
    reduce_scatter x1, waiting for transfers between devices, on_device(): lax.psum_scatter(grad_bank, 'dp', scatter_dimension=3, tiled=True)  318 us
    reduce_scatter x1, waiting for transfers between devices, on_device(): lax.psum_scatter(kernel_grads, 'pix', scatter_dimension=4, tiled=True)  264 us
    all_gather x1, waiting for transfers between devices, on_device(): lax.all_gather(conv_bank, 'dp', axis=3, tiled=True)  135 us
    psum x1, waiting for transfers between devices, on_device(): lax.psum((grad_table, grad_select, grad_modulation, grad_rgb_mod, grad_ga...  124 us
    all_gather x1, waiting for transfers between devices, on_device(): kernels = lax.all_gather(kernel_part, 'pix', axis=4, tiled=True)  104 us
    reduce_scatter x1, waiting for transfers between devices, on_device(): lax.psum_scatter(grad_w_value, 'dp', scatter_dimension=0, tiled=True)  91.7 us
    reduce_scatter x1, waiting for transfers between devices, on_device(): lax.psum_scatter(grad_w_query, 'dp', scatter_dimension=0, tiled=True)  91.6 us
    reduce_scatter x1, waiting for transfers between devices, on_device(): lax.psum_scatter(grad_c_query, 'dp', scatter_dimension=0, tiled=True)  91.6 us
  transfers between devices with their start and end apart: 31, of which 20 were waited for; matrix products, arithmetic and copies ran while one was open for 18% of the time, Pallas kernels for 0%

commit v1 on v0

v1 whole, which is shorter than its diff:
```python
from functools import partial

import jax
import jax.numpy as jnp
from jax import lax
from jax.experimental import pallas as pl
from jax.experimental.pallas import tpu as pltpu
from jax.sharding import PartitionSpec as P

HEAD_DIM = 64
PIX = 4
MESH = pl.DeviceIdType.MESH
VMEM_LIMIT = 60 * 1024 * 1024

penalty_weight = 1.0
highest = lax.Precision.HIGHEST
floats = jnp.float32
halves = jnp.bfloat16

ANY = pl.BlockSpec(memory_space=pl.ANY)
VMEM = pl.BlockSpec(memory_space=pltpu.VMEM)
DMA = pltpu.SemaphoreType.DMA


def params(collective_id):
    return pltpu.CompilerParams(
        collective_id=collective_id, has_side_effects=True, vmem_limit_bytes=VMEM_LIMIT
    )


def remote(src, dst, send_sem, recv_sem, where):
    return pltpu.make_async_remote_copy(
        src_ref=src,
        dst_ref=dst,
        send_sem=send_sem,
        recv_sem=recv_sem,
        device_id=where,
        device_id_type=MESH,
    )


def greet(count, others):
    row, col = lax.axis_index("dp"), lax.axis_index("pix")
    barrier = pltpu.get_barrier_semaphore()

    def one(step, carry):
        pl.semaphore_signal(
            barrier, inc=1, device_id=(lax.rem(row + step, count), col), device_id_type=MESH
        )
        return carry

    if count > 1:
        lax.fori_loop(1, count, one, 0)
    for other in others:
        pl.semaphore_signal(barrier, inc=1, device_id=other, device_id_type=MESH)
    pl.semaphore_wait(barrier, count - 1 + len(others))


def loop(count, body):
    def step(i, carry):
        body(i)
        return carry

    lax.fori_loop(0, count, step, 0)


def flip(index, bit):
    part = lax.rem(lax.div(index, bit), 2)
    return index + bit - 2 * bit * part


def gather_kernel(
    count,
    style_ref,
    bank_ref,
    parts_ref,
    images_ref,
    kernel_ref,
    styles_ref,
    inverse_ref,
    squares,
    squares_in,
    local_sem,
    style_send,
    style_recv,
    square_send,
    square_recv,
    part_send,
    part_recv,
    core_send,
    core_recv,
    line_send,
    line_recv,
    pass_send,
    pass_recv,
):
    row, col = lax.axis_index("dp"), lax.axis_index("pix")
    near, far = flip(col, 1), flip(col, 2)
    depth = bank_ref.shape[2]
    greet(count, [(row, near), (row, far)])

    def style_copy(step):
        other = lax.rem(row + step, count)
        return remote(
            style_ref.at[other], styles_ref.at[row], style_send.at[step], style_recv.at[step], (other, col)
        )

    def square_copy(step):
        other = lax.rem(row + step, count)
        return remote(
            squares, squares_in.at[row], square_send.at[step], square_recv.at[step], (other, col)
        )

    def part_copy(step):
        other = lax.rem(row + step, count)
        return remote(
            parts_ref.at[other], images_ref.at[row, col], part_send.at[step], part_recv.at[step], (other, col)
        )

    def part_arrives(step):
        origin = lax.rem(row - step + count, count)
        remote(
            parts_ref.at[0], images_ref.at[origin, col], part_send.at[step], part_recv.at[step], (row, near)
        ).wait_recv()

    def core_copy(step):
        origin = lax.rem(row - step + count, count)
        block = images_ref.at[origin, col]
        return remote(block, block, core_send.at[step], core_recv.at[step], (row, near))

    def line_copy(step):
        origin = lax.rem(row - step + count, count)
        block = images_ref.at[origin, col]
        return remote(block, block, line_send.at[step], line_recv.at[step], (row, far))

    def pass_copy(step):
        origin = lax.rem(row - step + count, count)
        block = images_ref.at[origin, far]
        return remote(block, block, pass_send.at[step], pass_recv.at[step], (row, near))

    def core_arrives(step):
        origin = lax.rem(row - step + count, count)
        block = images_ref.at[origin, near]
        remote(block, block, core_send.at[step], core_recv.at[step], (row, near)).wait_recv()

    def line_arrives(step):
        origin = lax.rem(row - step + count, count)
        block = images_ref.at[origin, far]
        remote(block, block, line_send.at[step], line_recv.at[step], (row, far)).wait_recv()

    def pass_arrives(step):
        origin = lax.rem(row - step + count, count)
        block = images_ref.at[origin, flip(near, 2)]
        remote(block, block, pass_send.at[step], pass_recv.at[step], (row, near)).wait_recv()

    own = pltpu.make_async_copy(parts_ref.at[row], images_ref.at[row, col], local_sem)
    own.start()

    def send_all(step):
        style_copy(step).start()

    lax.fori_loop(1, count, lambda i, c: (send_all(i), c)[1], 0)
    lax.fori_loop(1, count, lambda i, c: (part_copy(i).start(), c)[1], 0)
    styles_ref[row] = style_ref[row]
    own.wait()
    line_copy(0).start()
    core_copy(0).start()

    def style_wait(step):
        origin = lax.rem(row - step + count, count)
        remote(
            style_ref.at[0], styles_ref.at[origin], style_send.at[step], style_recv.at[step], (row, near)
        ).wait_recv()

    lax.fori_loop(1, count, lambda i, c: (style_wait(i), c)[1], 0)

    def mixed_tap(sample, tap, column, first, second):
        total = first * bank_ref[0, tap].astype(floats) + second * bank_ref[1, tap].astype(floats)
        return total * column

    def factors(sample):
        block = styles_ref[sample]
        column = jnp.transpose(block)[:depth, 0:1]
        return column, block[1:2, 0:1], block[2:3, 0:1]

    def square_sum(sample):
        column, first, second = factors(sample)
        total = jnp.zeros((depth, bank_ref.shape[3]), floats)
        for tap in range(9):
            modded = mixed_tap(sample, tap, column, first, second)
            total = total + modded * modded
        squares[pl.ds(sample, 1), :] = jnp.sum(total, axis=0, keepdims=True)

    loop(count, square_sum)
    lax.fori_loop(1, count, lambda i, c: (square_copy(i).start(), c)[1], 0)
    squares_in[row] = squares[...]

    def relay(step):
        part_arrives(step)
        line_copy(step).start()
        core_copy(step).start()

    lax.fori_loop(1, count, lambda i, c: (relay(i), c)[1], 0)

    def square_wait(step):
        origin = lax.rem(row - step + count, count)
        remote(
            squares, squares_in.at[origin], square_send.at[step], square_recv.at[step], (row, near)
        ).wait_recv()

    lax.fori_loop(1, count, lambda i, c: (square_wait(i), c)[1], 0)
    inverse_ref[...] = lax.rsqrt(jnp.sum(squares_in[...], axis=0) + 1e-08)

    def forward(step):
        line_arrives(step)
        pass_copy(step).start()

    def make_kernel(sample):
        column, first, second = factors(sample)
        scale = inverse_ref[pl.ds(sample, 1), :]
        for tap in range(9):
            modded = mixed_tap(sample, tap, column, first, second)
            kernel_ref[sample, tap] = (modded * scale).astype(halves)
        forward(sample)

    loop(count, make_kernel)
    loop(count, core_arrives)
    loop(count, pass_arrives)
    lax.fori_loop(
        1,
        count,
        lambda i, c: (
            style_copy(i).wait_send(),
            square_copy(i).wait_send(),
            part_copy(i).wait_send(),
            c,
        )[3],
        0,
    )
    loop(count, lambda i: core_copy(i).wait_send())
    loop(count, lambda i: line_copy(i).wait_send())
    loop(count, lambda i: pass_copy(i).wait_send())


def gather_inputs(style_rows, bank, parts):
    count, rows, depth = parts.shape
    width = bank.shape[-1]
    sems = [DMA((count,)) for _ in range(12)]
    return pl.pallas_call(
        partial(gather_kernel, count),
        out_shape=(
            jax.ShapeDtypeStruct((count, PIX, rows, depth), halves),
            jax.ShapeDtypeStruct((count, 9, depth, width), halves),
            jax.ShapeDtypeStruct((count, 8, 128), floats),
            jax.ShapeDtypeStruct((count, width), floats),
        ),
        in_specs=[VMEM, VMEM, ANY],
        out_specs=(ANY, VMEM, VMEM, VMEM),
        scratch_shapes=[
            pltpu.VMEM((count, width), floats),
            pltpu.VMEM((count, count, width), floats),
            DMA,
        ]
        + sems,
        compiler_params=params(0),
        name="gather_inputs",
    )(style_rows, bank, parts)


def conv_kernel(
    count,
    width,
    images_ref,
    kernel_ref,
    own_ref,
    gain_ref,
    conv_ref,
    conv_own_ref,
    hidden_ref,
    normed_ref,
    image_buf,
    padded,
    total,
    pair_out,
    pair_in,
    line_out,
    line_in,
    block_out,
    block_in,
    image_sem,
    pair_send,
    pair_recv,
    line_send,
    line_recv,
    block_send,
    block_recv,
    norm_send,
    norm_recv,
):
    row, col = lax.axis_index("dp"), lax.axis_index("pix")
    groups = count // 2
    slots = pair_out.shape[0]
    side = lax.rem(row, 2)
    level = lax.div(row, 2)
    partner = flip(row, 1)
    near, far = flip(col, 1), flip(col, 2)
    cross = flip(near, 2)
    tokens, depth = image_buf.shape[1], image_buf.shape[2]
    channels = total.shape[1]
    rows = tokens // PIX
    halo = width

    barrier = pltpu.get_barrier_semaphore()

    def hello(step, carry):
        other = 2 * lax.rem(level + step, groups) + side
        pl.semaphore_signal(barrier, inc=1, device_id=(other, col), device_id_type=MESH)
        return carry

    lax.fori_loop(1, groups, hello, 0)
    for other in ((partner, col), (row, near), (row, far), (row, cross)):
        pl.semaphore_signal(barrier, inc=1, device_id=other, device_id_type=MESH)
    pl.semaphore_wait(barrier, groups - 1 + 4)

    def group_of(step):
        return lax.rem(level + 1 + step, groups)

    def sample_of(index):
        mine = lax.div(index, groups)
        group = group_of(lax.rem(index, groups))
        return 2 * group + jnp.where(mine == 1, side, 1 - side)

    def fetch(index):
        slot = lax.rem(index, 2)
        return pltpu.make_async_copy(
            images_ref.at[sample_of(index)], image_buf.at[slot], image_sem.at[slot]
        )

    zeros = jnp.zeros((3, halo, depth), halves)
    padded[:, 0:halo, :] = zeros
    padded[:, halo + tokens : halo + tokens + halo, :] = zeros
    fetch(0).start()
    place = lax.rem(lax.broadcasted_iota(jnp.int32, (tokens, depth), 0), width)

    def stage(index):
        fetch(index).wait()

        @pl.when(index + 1 < count)
        def _():
            fetch(index + 1).start()

        source = image_buf[lax.rem(index, 2)]
        wide = source.astype(floats)
        padded[1, halo : halo + tokens, :] = source
        before = jnp.where(place == 0, 0.0, pltpu.roll(wide, 1, 0))
        padded[0, halo : halo + tokens, :] = before.astype(halves)
        after = jnp.where(place == width - 1, 0.0, pltpu.roll(wide, tokens - 1, 0))
        padded[2, halo : halo + tokens, :] = after.astype(halves)

    def rows_of(sample, start):
        acc = jnp.zeros((rows, channels), floats)
        for a in range(3):
            for b in range(3):
                window = padded[b, pl.ds(pl.multiple_of(start + a * width, 16), rows), :]
                acc = acc + jnp.dot(
                    window, kernel_ref[sample, 3 * a + b], preferred_element_type=floats
                )
        return acc

    def pair_copy(step):
        return remote(
            pair_out.at[lax.rem(step, slots)],
            pair_in.at[step],
            pair_send.at[step],
            pair_recv.at[step],
            (partner, col),
        )

    def line_copy(step):
        group = group_of(step)
        return remote(
            line_out.at[lax.rem(step, slots)],
            line_in.at[step],
            line_send.at[step],
            line_recv.at[step],
            (2 * group + side, col),
        )

    def give(step):
        @pl.when(step >= slots)
        def _():
            pair_copy(step - slots).wait_send()

        stage(step)
        sample = sample_of(step)

        def chunk(i):
            start = pl.multiple_of(i * rows, rows)
            pair_out[lax.rem(step, slots), pl.ds(start, rows), :] = rows_of(sample, start).astype(
                halves
            )

        loop(PIX, chunk)
        pair_copy(step).start()

    loop(groups, give)

    def keep(step):
        @pl.when(step >= slots)
        def _():
            line_copy(step - slots).wait_send()

        stage(groups + step)
        sample = sample_of(groups + step)
        pair_copy(step).wait_recv()

        def chunk(i):
            start = pl.multiple_of(i * rows, rows)
            here = pl.ds(start, rows)
            line_out[lax.rem(step, slots), here, :] = (
                rows_of(sample, start) + pair_in[step, here, :].astype(floats)
            ).astype(halves)

        loop(PIX, chunk)
        line_copy(step).start()

    loop(groups - 1, keep)
    last = groups - 1
    stage(count - 1)

    def own_chunk(i):
        start = pl.multiple_of(i * rows, rows)
        total[pl.ds(start, rows), :] = rows_of(row, start)

    loop(PIX, own_chunk)
    pair_copy(last).wait_recv()
    loop(groups - 1, lambda i: line_copy(i).wait_recv())

    def block_copy(turn):
        target = (far, cross, near)[turn]
        return remote(
            block_out.at[turn], block_in.at[col], block_send.at[turn], block_recv.at[turn], (row, target)
        )

    def block_arrives(turn):
        origin = (far, cross, near)[turn]
        remote(
            block_out.at[turn], block_in.at[origin], block_send.at[turn], block_recv.at[turn], (row, near)
        ).wait_recv()

    for turn, target in enumerate((far, cross, near, col)):
        here = pl.ds(pl.multiple_of(target * rows, rows), rows)
        value = total[here, :] + pair_in[last, here, :].astype(floats)
        for i in range(groups - 1):
            value = value + line_in[i, here, :].astype(floats)
        rounded = value.astype(halves)
        conv_own_ref[here, :] = rounded
        if turn < 3:
            block_out[turn] = rounded
            block_copy(turn).start()
        else:
            block_in[col] = rounded
    for turn in range(3):
        block_arrives(turn)

    part = rows // 4

    def norm_rows(i):
        here = pl.ds(pl.multiple_of(i * part, part), part)
        for j in range(PIX):
            conv_ref[here, j * channels : (j + 1) * channels] = block_in[j, here, :]
        conv = conv_ref[here, :].astype(floats)
        hidden = own_ref[here, :].astype(floats) + conv * jax.nn.sigmoid(conv)
        hidden_ref[here, :] = hidden
        mean = jnp.mean(hidden * hidden, -1, keepdims=True)
        normed_ref[col, here, :] = (hidden * lax.rsqrt(mean + 1e-06) * gain_ref[...]).astype(halves)

    loop(4, norm_rows)
    mine, theirs = normed_ref.at[col], normed_ref.at[far]
    to_far = remote(mine, mine, norm_send.at[0], norm_recv.at[0], (row, far))
    to_near = remote(mine, mine, norm_send.at[1], norm_recv.at[1], (row, near))
    to_far.start()
    to_near.start()
    remote(mine, theirs, norm_send.at[0], norm_recv.at[0], (row, far)).wait_recv()
    onward = remote(theirs, theirs, norm_send.at[2], norm_recv.at[2], (row, near))
    onward.start()
    remote(mine, normed_ref.at[near], norm_send.at[1], norm_recv.at[1], (row, near)).wait_recv()
    remote(mine, normed_ref.at[cross], norm_send.at[2], norm_recv.at[2], (row, near)).wait_recv()
    to_far.wait_send()
    to_near.wait_send()
    onward.wait_send()
    for turn in range(3):
        block_copy(turn).wait_send()
    for step in range(max(0, groups - slots), groups):
        pair_copy(step).wait_send()
    for step in range(max(0, groups - 1 - slots), groups - 1):
        line_copy(step).wait_send()


def conv_forward(images_all, kernels, own, gain, width):
    count, tokens, depth = images_all.shape
    channels = kernels.shape[-1]
    rows, full = own.shape
    groups = count // 2
    slots = min(groups, 4)
    block = (tokens, channels)
    return pl.pallas_call(
        partial(conv_kernel, count, width),
        out_shape=(
            jax.ShapeDtypeStruct((rows, full), halves),
            jax.ShapeDtypeStruct((tokens, channels), halves),
            jax.ShapeDtypeStruct((rows, full), floats),
            jax.ShapeDtypeStruct((PIX, rows, full), halves),
        ),
        in_specs=[ANY, VMEM, VMEM, VMEM],
        out_specs=(VMEM, VMEM, VMEM, VMEM),
        scratch_shapes=[
            pltpu.VMEM((2, tokens, depth), halves),
            pltpu.VMEM((3, tokens + 2 * width, depth), halves),
            pltpu.VMEM(block, floats),
            pltpu.VMEM((slots,) + block, halves),
            pltpu.VMEM((groups,) + block, halves),
            pltpu.VMEM((slots,) + block, halves),
            pltpu.VMEM((max(groups - 1, 1),) + block, halves),
            pltpu.VMEM((3, rows, channels), halves),
            pltpu.VMEM((PIX, rows, channels), halves),
            DMA((2,)),
            DMA((groups,)),
            DMA((groups,)),
            DMA((groups,)),
            DMA((groups,)),
            DMA((3,)),
            DMA((3,)),
            DMA((3,)),
            DMA((3,)),
        ],
        compiler_params=params(1),
        name="conv_forward",
    )(images_all, kernels, own, gain.reshape(1, -1))


def peers(col):
    near, far = flip(col, 1), flip(col, 2)
    return near, far, flip(near, 2)


def greet_pixels(row, others):
    barrier = pltpu.get_barrier_semaphore()
    for other in others:
        pl.semaphore_signal(barrier, inc=1, device_id=(row, other), device_id_type=MESH)
    pl.semaphore_wait(barrier, len(others))


NT = (((1,), (1,)), ((), ()))
TN = (((0,), (0,)), ((), ()))


def mul_nt(a, b, precision=None):
    return lax.dot_general(a, b, NT, preferred_element_type=floats, precision=precision)


def mul_tn(a, b, precision=None):
    return lax.dot_general(a, b, TN, preferred_element_type=floats, precision=precision)


def mul(a, b):
    return jnp.dot(a, b, preferred_element_type=floats)


def attend_kernel(
    normed_ref,
    weight_ref,
    text_ref,
    text_weight_ref,
    query_ref,
    key_ref,
    value_ref,
    total_ref,
    attended_ref,
    text_out_ref,
    block_out,
    key_norm,
    block_send,
    block_recv,
    text_send,
    text_recv,
):
    row, col = lax.axis_index("dp"), lax.axis_index("pix")
    near, far, cross = peers(col)
    targets = (far, cross, near)
    greet_pixels(row, targets)
    rows = normed_ref.shape[1]
    width = query_ref.shape[1]
    heads = width // HEAD_DIM
    score_scale = HEAD_DIM ** (-0.5)

    for j in range(2):
        here = slice(j * width, (j + 1) * width)
        text_out_ref[col, :, here] = mul(text_ref[...], text_weight_ref[:, here]).astype(halves)

    def text_copy(turn):
        block = text_out_ref.at[col]
        return remote(block, block, text_send.at[turn], text_recv.at[turn], (row, targets[turn]))

    for turn in range(3):
        text_copy(turn).start()

    def project(i):
        source = normed_ref[i]
        here = pl.ds(pl.multiple_of(i * rows, rows), rows)
        for j, out in enumerate((query_ref, key_ref, value_ref)):
            out[here, :] = mul(source, weight_ref[:, j * width : (j + 1) * width]).astype(halves)

    loop(PIX, project)
    ones = jnp.ones((8, HEAD_DIM), floats)
    for h in range(heads):
        key = key_ref[:, h * HEAD_DIM : (h + 1) * HEAD_DIM].astype(floats)
        key_norm[h] = mul_nt(ones, key * key, highest)

    def attend(target, store):
        here = pl.ds(pl.multiple_of(target * rows, rows), rows)
        for h in range(heads):
            lanes = slice(h * HEAD_DIM, (h + 1) * HEAD_DIM)
            inner = mul_nt(query_ref[here, lanes], key_ref[:, lanes])
            scores = score_scale * (2.0 * inner - key_norm[h, 0:1, :])
            largest = jnp.max(scores, -1, keepdims=True)
            expanded = jnp.exp(scores - largest)
            summed = jnp.sum(expanded, -1, keepdims=True)
            weights = (expanded * (1.0 / summed)).astype(halves)
            store(lanes, mul(weights, value_ref[:, lanes]).astype(halves))
            total_ref[here, h : h + 1] = largest + jnp.log(summed)

    def block_copy(turn):
        return remote(
            block_out.at[turn],
            attended_ref.at[col],
            block_send.at[turn],
            block_recv.at[turn],
            (row, targets[turn]),
        )

    def turn_body(turn):
        target = jnp.where(turn == 0, far, jnp.where(turn == 1, cross, jnp.where(turn == 2, near, col)))

        def store(lanes, result):
            block_out[turn, :, lanes] = result

        attend(target, store)
        for k in range(3):

            @pl.when(turn == k)
            def _(k=k):
                block_copy(k).start()

    loop(4, turn_body)
    attended_ref[col] = block_out[3]
    for turn in range(3):
        remote(
            block_out.at[turn],
            attended_ref.at[targets[turn]],
            block_send.at[turn],
            block_recv.at[turn],
            (row, near),
        ).wait_recv()
        block = text_out_ref.at[targets[turn]]
        remote(block, block, text_send.at[turn], text_recv.at[turn], (row, near)).wait_recv()
    for turn in range(3):
        block_copy(turn).wait_send()
        text_copy(turn).wait_send()


def attend_forward(normed, weights, text, text_weights):
    count, rows, full = normed.shape
    tokens, width = count * rows, weights.shape[1] // 3
    heads = width // HEAD_DIM
    flat = jax.ShapeDtypeStruct((tokens, width), halves)
    return pl.pallas_call(
        attend_kernel,
        out_shape=(
            flat,
            flat,
            flat,
            jax.ShapeDtypeStruct((tokens, 128), floats),
            jax.ShapeDtypeStruct((PIX, rows, width), halves),
            jax.ShapeDtypeStruct((PIX, text.shape[0], 2 * width), halves),
        ),
        in_specs=[VMEM] * 4,
        out_specs=(VMEM,) * 6,
        scratch_shapes=[
            pltpu.VMEM((4, rows, width), halves),
            pltpu.VMEM((heads, 8, tokens), floats),
            DMA((3,)),
            DMA((3,)),
            DMA((3,)),
            DMA((3,)),
        ],
        compiler_params=params(2),
        name="attend_forward",
    )(normed, weights, text, text_weights)


def cross_kernel(
    words,
    attended_ref,
    hidden_ref,
    weight_ref,
    text_ref,
    gain_ref,
    rgb_scale_ref,
    rgb_weight_ref,
    cotangent_ref,
    rgb_cotangent_ref,
    penalty_ref,
    output_ref,
    rgb_ref,
    weight_grad_ref,
    text_grad_ref,
    grad_two_ref,
    grad_attended_ref,
    small_ref,
    attended,
    two,
    normed,
    query,
    probs,
    crossed,
    mixed,
    grad_three,
    grad_proj,
    grad_crossed,
    grad_query,
    grad_norm,
    grad_attn,
):
    rows, full = hidden_ref.shape
    tile = full // PIX
    score_scale = HEAD_DIM ** (-0.5)
    W_OUT, C_QUERY, C_OUT = (slice(i * tile, (i + 1) * tile) for i in range(3))
    part = 64

    def cols(j):
        return pl.ds(pl.multiple_of(j * tile, tile), tile)

    for j in range(PIX):
        attended[:, j * tile : (j + 1) * tile] = attended_ref[j]

    def out_two(j):
        two[:, cols(j)] = hidden_ref[:, cols(j)] + mul(attended[...], weight_ref[j, :, W_OUT])

    loop(PIX, out_two)

    def norm_two(i):
        here = pl.ds(pl.multiple_of(i * part, part), part)
        hidden = two[here, :]
        mean = jnp.mean(hidden * hidden, -1, keepdims=True)
        normed[here, :] = (hidden * lax.rsqrt(mean + 1e-06) * gain_ref[...]).astype(halves)

    loop(rows // part, norm_two)

    def out_query(j):
        query[:, cols(j)] = mul(normed[...], weight_ref[j, :, C_QUERY]).astype(halves)

    loop(PIX, out_query)
    slots = text_ref.shape[1]
    known = lax.broadcasted_iota(jnp.int32, (rows, slots), 1) < words
    pairs = tile // 128

    def text_lanes(pair, side):
        return pl.ds(pl.multiple_of(side * tile + lax.rem(pair, pairs) * 128, 128), 128)

    def cross_pair(pair):
        here = pl.ds(pl.multiple_of(pair * 128, 128), 128)
        group = lax.div(pair, pairs)
        queries = query[:, here]
        keys = text_ref[group, :, text_lanes(pair, 0)]
        values = text_ref[group, :, text_lanes(pair, 1)]
        outs = []
        for h in range(2):
            lanes = slice(h * HEAD_DIM, (h + 1) * HEAD_DIM)
            scores = score_scale * mul_nt(queries[:, lanes], keys[:, lanes])
            scores = jnp.where(known, scores, -1e30)
            expanded = jnp.exp(scores - jnp.max(scores, -1, keepdims=True))
            prob = expanded / jnp.sum(expanded, -1, keepdims=True)
            probs[2 * pair + h] = prob
            outs.append(mul(prob.astype(halves), values[:, lanes]))
        crossed[:, here] = jnp.concatenate(outs, axis=1).astype(halves)

    loop(full // 128, cross_pair)
    rgb_ref[...] = jnp.zeros_like(rgb_ref)

    def out_three(j):
        three = two[:, cols(j)] + mul(crossed[...], weight_ref[j, :, C_OUT])
        output_ref[:, cols(j)] = three
        blend = (three * rgb_scale_ref[:, cols(j)]).astype(halves)
        mixed[:, cols(j)] = blend
        rgb_ref[...] += mul(blend, rgb_weight_ref[cols(j), :])

    loop(PIX, out_three)
    rgb_grad = rgb_cotangent_ref[...] + penalty_weight * penalty_ref[...] * rgb_ref[...]

    def back_three(j):
        color = mul_tn(rgb_grad, mixed[:, cols(j)].astype(floats), highest)
        small_ref[2:5, cols(j)] = color[0:3]
        grad_mixed = mul_nt(rgb_grad, rgb_weight_ref[cols(j), :].astype(floats), highest)
        small_ref[1:2, cols(j)] = jnp.sum(grad_mixed * output_ref[:, cols(j)], 0, keepdims=True)
        grad = cotangent_ref[:, cols(j)].astype(floats) + grad_mixed * rgb_scale_ref[:, cols(j)]
        grad_three[:, cols(j)] = grad
        grad_proj[:, cols(j)] = grad.astype(halves)

    loop(PIX, back_three)

    def times_transposed(source, j, which):
        acc = jnp.zeros((rows, tile), floats)
        for i in range(PIX):
            acc = acc + mul_nt(source[:, i * tile : (i + 1) * tile], weight_ref[i, cols(j), which])
        return acc

    def back_crossed(j):
        grad_crossed[:, cols(j)] = times_transposed(grad_proj, j, C_OUT).astype(halves)

    loop(PIX, back_crossed)

    def back_pair(pair):
        here = pl.ds(pl.multiple_of(pair * 128, 128), 128)
        group = lax.div(pair, pairs)
        queries, grads = query[:, here], grad_crossed[:, here]
        keys = text_ref[group, :, text_lanes(pair, 0)]
        values = text_ref[group, :, text_lanes(pair, 1)]
        grad_q, grad_k, grad_v = [], [], []
        for h in range(2):
            lanes = slice(h * HEAD_DIM, (h + 1) * HEAD_DIM)
            prob = probs[2 * pair + h]
            grad = grads[:, lanes]
            grad_prob = mul_nt(grad, values[:, lanes])
            grad_v.append(mul_tn(prob.astype(halves), grad))
            inner = jnp.sum(grad_prob * prob, -1, keepdims=True)
            score = (prob * (grad_prob - inner)).astype(halves)
            grad_q.append(score_scale * mul(score, keys[:, lanes]))
            grad_k.append(score_scale * mul_tn(score, queries[:, lanes]))
        grad_query[:, here] = jnp.concatenate(grad_q, axis=1).astype(halves)
        text_grad_ref[group, :, text_lanes(pair, 0)] = jnp.concatenate(grad_k, axis=1)
        text_grad_ref[group, :, text_lanes(pair, 1)] = jnp.concatenate(grad_v, axis=1)

    loop(full // 128, back_pair)

    def back_query(j):
        grad_norm[:, cols(j)] = times_transposed(grad_query, j, C_QUERY)

    loop(PIX, back_query)
    small_ref[0:1, :] = jnp.zeros((1, full), floats)

    def back_norm(i):
        here = pl.ds(pl.multiple_of(i * part, part), part)
        hidden, grad = two[here, :], grad_norm[here, :]
        inverse = lax.rsqrt(jnp.mean(hidden * hidden, -1, keepdims=True) + 1e-06)
        small_ref[0:1, :] += jnp.sum(grad * hidden * inverse, 0, keepdims=True)
        scaled = grad * gain_ref[...]
        mean = jnp.mean(scaled * hidden, -1, keepdims=True)
        total = grad_three[here, :] + inverse * scaled - hidden * (inverse * inverse * inverse * mean)
        grad_two_ref[here, :] = total
        grad_attn[here, :] = total.astype(halves)

    loop(rows // part, back_norm)

    def back_attended(j):
        grad_attended_ref[j] = times_transposed(grad_attn, j, W_OUT).astype(halves)

    loop(PIX, back_attended)

    def weight_grads(index):
        i, j = lax.div(index, PIX), lax.rem(index, PIX)
        for which, left, right in (
            (W_OUT, attended, grad_attn),
            (C_QUERY, normed, grad_query),
            (C_OUT, crossed, grad_proj),
        ):
            weight_grad_ref[j, cols(i), which] = mul_tn(left[:, cols(i)], right[:, cols(j)]).astype(
                halves
            )

    loop(PIX * PIX, weight_grads)
    small_ref[5:8, :] = jnp.zeros((3, full), floats)


def cross_part(
    words, attended, hidden, weights, text, gain, rgb_scale, rgb_weight, cotangent, rgb_cotangent, penalty
):
    rows, full = hidden.shape
    tile = full // PIX
    heads = full // HEAD_DIM
    wide = pltpu.VMEM((rows, full), floats)
    slim = pltpu.VMEM((rows, full), halves)
    return pl.pallas_call(
        partial(cross_kernel, words),
        out_shape=(
            jax.ShapeDtypeStruct((rows, full), floats),
            jax.ShapeDtypeStruct((rows, 128), floats),
            jax.ShapeDtypeStruct(weights.shape, halves),
            jax.ShapeDtypeStruct(text.shape, floats),
            jax.ShapeDtypeStruct((rows, full), floats),
            jax.ShapeDtypeStruct((PIX, rows, tile), halves),
            jax.ShapeDtypeStruct((8, full), floats),
        ),
        in_specs=[VMEM] * 10,
        out_specs=(VMEM,) * 7,
        scratch_shapes=[
            slim,
            wide,
            slim,
            slim,
            pltpu.VMEM((heads, rows, text.shape[1]), floats),
            slim,
            slim,
            wide,
            slim,
            slim,
            slim,
            wide,
            slim,
        ],
        compiler_params=pltpu.CompilerParams(vmem_limit_bytes=VMEM_LIMIT),
        name="cross_part",
    )(
        attended,
        hidden,
        weights,
        text,
        gain.reshape(1, -1),
        rgb_scale,
        rgb_weight,
        cotangent,
        rgb_cotangent,
        penalty,
    )


def attend_back_kernel(
    grad_ref,
    query_ref,
    key_ref,
    value_ref,
    total_ref,
    normed_ref,
    weight_ref,
    hidden_ref,
    conv_ref,
    grad_two_ref,
    gain_ref,
    weight_grad_ref,
    grad_one_ref,
    grad_conv_ref,
    small_ref,
    grads,
    grad_query,
    grad_key,
    grad_value,
    key_acc,
    value_acc,
    totals,
    pair_out,
    pair_in,
    line_out,
    line_in,
    own,
    conv_out,
    grad_send,
    grad_recv,
    pair_send,
    pair_recv,
    line_send,
    line_recv,
    conv_send,
    conv_recv,
):
    row, col = lax.axis_index("dp"), lax.axis_index("pix")
    near, far, cross = peers(col)
    targets = (far, cross, near)
    greet_pixels(row, targets)
    rows, full = hidden_ref.shape
    tokens, width = query_ref.shape
    heads = width // HEAD_DIM
    score_scale = HEAD_DIM ** (-0.5)

    def grad_copy(turn):
        return remote(
            grad_ref.at[targets[turn]],
            grads.at[col],
            grad_send.at[turn],
            grad_recv.at[turn],
            (row, targets[turn]),
        )

    for turn in range(3):
        grad_copy(turn).start()
    grads[col] = grad_ref[col]
    totals[...] = jnp.transpose(total_ref[...])
    for turn in range(3):
        remote(
            grad_ref.at[0],
            grads.at[targets[turn]],
            grad_send.at[turn],
            grad_recv.at[turn],
            (row, near),
        ).wait_recv()
    ones = jnp.ones((rows, HEAD_DIM), halves)
    for h in range(heads):
        lanes = slice(h * HEAD_DIM, (h + 1) * HEAD_DIM)
        keys, values = key_ref[:, lanes], value_ref[:, lanes]
        wide = keys.astype(floats)
        norm = score_scale * jnp.sum(wide * wide, -1, keepdims=True)
        key_acc[...] = jnp.zeros_like(key_acc)
        value_acc[...] = jnp.zeros_like(value_acc)

        def block(i, lanes=lanes, keys=keys, values=values, norm=norm, h=h):
            here = pl.ds(pl.multiple_of(i * rows, rows), rows)
            queries, grad = query_ref[here, lanes], grads[i, :, lanes]
            inner = mul_nt(keys, queries)
            prob = jnp.exp((2.0 * score_scale) * inner - norm - totals[h : h + 1, here])
            grad_prob = mul_nt(values, grad)
            value_acc[...] += mul(prob.astype(halves), grad)
            mean = jnp.sum(grad_prob * prob, 0, keepdims=True)
            score = (prob * (grad_prob - mean)).astype(halves)
            key_acc[...] += mul(score, jnp.concatenate([queries, ones], axis=1))
            grad_query[here, lanes] = (2.0 * score_scale * mul_tn(score, keys)).astype(halves)

        loop(PIX, block)
        acc = key_acc[...]
        grad_key[:, lanes] = (
            2.0 * score_scale * (acc[:, :HEAD_DIM] - wide * acc[:, HEAD_DIM : HEAD_DIM + 1])
        ).astype(halves)
        grad_value[:, lanes] = value_acc[...].astype(halves)

    def norm_grad(block, store):
        here = pl.ds(pl.multiple_of(block * rows, rows), rows)

        def tile(j):
            cols = pl.ds(pl.multiple_of(j * width, width), width)
            acc = jnp.zeros((rows, width), floats)
            for k, source in enumerate((grad_query, grad_key, grad_value)):
                acc = acc + mul_nt(source[here, :], weight_ref[cols, k * width : (k + 1) * width])
            store(cols, acc)

        loop(full // width, tile)

    def pair_copy(turn):
        return remote(
            pair_out.at[turn], pair_in.at[turn], pair_send.at[turn], pair_recv.at[turn], (row, near)
        )

    for turn, target in enumerate((cross, near)):

        def store(cols, value, turn=turn):
            pair_out[turn, :, cols] = value.astype(halves)

        norm_grad(target, store)
        pair_copy(turn).start()
    line = remote(line_out, line_in, line_send, line_recv, (row, far))

    def store_far(cols, value):
        line_out[:, cols] = (value + pair_in[0, :, cols].astype(floats)).astype(halves)

    pair_copy(0).wait_recv()
    norm_grad(far, store_far)
    line.start()

    def store_own(cols, value):
        own[:, cols] = value + pair_in[1, :, cols].astype(floats)

    pair_copy(1).wait_recv()
    norm_grad(col, store_own)

    def weight_grads(j):
        cols = pl.ds(pl.multiple_of(j * width, width), width)
        for k, right in enumerate((grad_query, grad_key, grad_value)):
            acc = jnp.zeros((width, width), floats)
            for i in range(PIX):
                acc = acc + mul_tn(normed_ref[i, :, cols], right[i * rows : (i + 1) * rows, :])
            weight_grad_ref[cols, k * width : (k + 1) * width] = acc.astype(halves)

    loop(full // width, weight_grads)
    line.wait_recv()
    small_ref[...] = jnp.zeros_like(small_ref)
    part = 64

    def back_norm(i):
        here = pl.ds(pl.multiple_of(i * part, part), part)
        hidden = hidden_ref[here, :]
        grad = own[here, :] + line_in[here, :].astype(floats)
        inverse = lax.rsqrt(jnp.mean(hidden * hidden, -1, keepdims=True) + 1e-06)
        small_ref[0:1, :] += jnp.sum(grad * hidden * inverse, 0, keepdims=True)
        scaled = grad * gain_ref[...]
        mean = jnp.mean(scaled * hidden, -1, keepdims=True)
        total = (
            grad_two_ref[here, :] + inverse * scaled - hidden * (inverse * inverse * inverse * mean)
        )
        grad_one_ref[here, :] = total
        conv = conv_ref[here, :].astype(floats)
        gate = jax.nn.sigmoid(conv)
        result = (total * gate * (1.0 + conv * (1.0 - gate))).astype(halves)
        for j in range(PIX):
            conv_out[j, here, :] = result[:, j * width : (j + 1) * width]

    loop(rows // part, back_norm)

    def conv_copy(turn):
        return remote(
            conv_out.at[targets[turn]],
            grad_conv_ref.at[col],
            conv_send.at[turn],
            conv_recv.at[turn],
            (row, targets[turn]),
        )

    for turn in range(3):
        conv_copy(turn).start()
    grad_conv_ref[col] = conv_out[col]
    for turn in range(3):
        remote(
            conv_out.at[0],
            grad_conv_ref.at[targets[turn]],
            conv_send.at[turn],
            conv_recv.at[turn],
            (row, near),
        ).wait_recv()
    for turn in range(3):
        conv_copy(turn).wait_send()
        grad_copy(turn).wait_send()
    pair_copy(0).wait_send()
    pair_copy(1).wait_send()
    line.wait_send()


def attend_backward(grad, query, key, value, totals, normed, weights, hidden, conv, grad_two, gain):
    rows, full = hidden.shape
    tokens, width = query.shape
    flat = pltpu.VMEM((tokens, width), halves)
    return pl.pallas_call(
        attend_back_kernel,
        out_shape=(
            jax.ShapeDtypeStruct(weights.shape, halves),
            jax.ShapeDtypeStruct((rows, full), floats),
            jax.ShapeDtypeStruct((PIX, rows, width), halves),
            jax.ShapeDtypeStruct((8, full), floats),
        ),
        in_specs=[VMEM] * 11,
        out_specs=(VMEM,) * 4,
        scratch_shapes=[
            pltpu.VMEM((PIX, rows, width), halves),
            flat,
            flat,
            flat,
            pltpu.VMEM((tokens, 2 * HEAD_DIM), floats),
            pltpu.VMEM((tokens, HEAD_DIM), floats),
            pltpu.VMEM((128, tokens), floats),
            pltpu.VMEM((2, rows, full), halves),
            pltpu.VMEM((2, rows, full), halves),
            pltpu.VMEM((rows, full), halves),
            pltpu.VMEM((rows, full), halves),
            pltpu.VMEM((rows, full), floats),
            pltpu.VMEM((PIX, rows, width), halves),
            DMA((3,)),
            DMA((3,)),
            DMA((2,)),
            DMA((2,)),
            DMA,
            DMA,
            DMA((3,)),
            DMA((3,)),
        ],
        compiler_params=params(3),
        name="attend_backward",
    )(
        grad,
        query,
        key,
        value,
        totals,
        normed,
        weights,
        hidden,
        conv,
        grad_two,
        gain.reshape(1, -1),
    )


def conv_back_kernel(
    count,
    width,
    images_ref,
    kernel_ref,
    bank_ref,
    styles_ref,
    inverse_ref,
    grad_ref,
    conv_ref,
    bank_grad_ref,
    stats_ref,
    image_grad_ref,
    grads_ref,
    image_buf,
    padded_image,
    padded_grad,
    turned,
    acc,
    sums_out,
    sums_in,
    kept,
    kept_own,
    pixel_out,
    pixel_in,
    line_out,
    line_in,
    owner_out,
    local_sem,
    image_sem,
    load_sem,
    sums_send,
    sums_recv,
    level_send,
    level_recv,
    pair_send,
    pair_recv,
    pixel_send,
    pixel_recv,
    line_send,
    line_recv,
    owner_send,
    owner_recv,
):
    row, col = lax.axis_index("dp"), lax.axis_index("pix")
    groups = count // 2
    side, level = lax.rem(row, 2), lax.div(row, 2)
    partner = flip(row, 1)
    near, far, cross = peers(col)
    tokens, channels = grad_ref.shape
    depth = image_buf.shape[2]
    rows = tokens // PIX
    halo = width
    greet(count, [(row, near), (row, far)])

    def sample_of(step):
        group = lax.rem(level - lax.div(step, 2) + groups, groups)
        return 2 * group + jnp.where(lax.rem(step, 2) == 0, side, 1 - side)

    def level_copy(k):
        target = 2 * lax.rem(level + k, groups) + side
        return remote(
            grad_ref, grads_ref.at[row], level_send.at[k], level_recv.at[k], (target, col)
        )

    def pair_copy(k):
        block = grads_ref.at[sample_of(2 * k)]
        return remote(block, block, pair_send.at[k], pair_recv.at[k], (partner, col))

    def sums_copy(k):
        return remote(
            sums_out,
            sums_in.at[row],
            sums_send.at[k],
            sums_recv.at[k],
            (lax.rem(row + k, count), col),
        )

    own = pltpu.make_async_copy(grad_ref, grads_ref.at[row], local_sem)
    own.start()
    lax.fori_loop(1, groups, lambda k, c: (level_copy(k).start(), c)[1], 0)
    own.wait()
    pair_copy(0).start()

    def fetch(step):
        slot = lax.rem(step, 2)
        return pltpu.make_async_copy(
            images_ref.at[sample_of(step)], image_buf.at[slot], image_sem.at[slot]
        )

    fetch(0).start()
    products = jnp.zeros((8, channels), floats)

    def add_product(i, total):
        here = pl.ds(pl.multiple_of(i * 64, 64), 64)
        product = grad_ref[here, :].astype(floats) * conv_ref[here, :].astype(floats)
        return total + jnp.sum(product.reshape(8, 8, channels), axis=0)

    products = lax.fori_loop(0, tokens // 64, add_product, products)
    sums_out[...] = jnp.broadcast_to(jnp.sum(products, 0, keepdims=True), (8, channels))
    lax.fori_loop(1, count, lambda k, c: (sums_copy(k).start(), c)[1], 0)
    sums_in[row] = sums_out[...]
    acc[...] = jnp.zeros_like(acc)
    stats_ref[...] = jnp.zeros_like(stats_ref)
    for buffer, lanes in ((padded_image, depth), (padded_grad, channels)):
        zeros = jnp.zeros((3, halo, lanes), halves)
        buffer[:, 0:halo, :] = zeros
        buffer[:, halo + tokens : halo + tokens + halo, :] = zeros

    def sums_arrive(k, carry):
        origin = lax.rem(row - k + count, count)
        remote(
            sums_out, sums_in.at[origin], sums_send.at[k], sums_recv.at[k], (partner, col)
        ).wait_recv()
        return carry

    def fill(buffer, source):
        wide = source.astype(floats)
        place = lax.rem(lax.broadcasted_iota(jnp.int32, wide.shape, 0), width)
        here = slice(halo, halo + tokens)
        buffer[0, here, :] = jnp.where(place == 0, 0.0, pltpu.roll(wide, 1, 0)).astype(halves)
        buffer[2, here, :] = jnp.where(
            place == width - 1, 0.0, pltpu.roll(wide, tokens - 1, 0)
        ).astype(halves)

    centre = pl.ds(halo, tokens)

    def pixel_copy(step):
        return remote(
            pixel_out.at[lax.rem(step, 2)],
            pixel_in.at[step],
            pixel_send.at[step],
            pixel_recv.at[step],
            (row, near),
        )

    def line_copy(step):
        return remote(
            line_out.at[lax.rem(step, 2)],
            line_in.at[step],
            line_send.at[step],
            line_recv.at[step],
            (row, far),
        )

    def owner_copy(step):
        return remote(
            owner_out.at[lax.rem(step, 2)],
            image_grad_ref.at[row],
            owner_send.at[step],
            owner_recv.at[row],
            (sample_of(step), col),
        )

    def work(step):
        k, odd = lax.div(step, 2), lax.rem(step, 2)
        sample = sample_of(step)

        @pl.when(odd == 1)
        def _():
            block = grads_ref.at[sample]
            remote(block, block, pair_send.at[k], pair_recv.at[k], (partner, col)).wait_recv()

        @pl.when((odd == 0) & (k > 0))
        def _():
            block = grads_ref.at[sample]
            remote(block, block, level_send.at[k], level_recv.at[k], (partner, col)).wait_recv()
            pair_copy(k).start()

        load = pltpu.make_async_copy(
            grads_ref.at[sample], padded_grad.at[1, centre, :], load_sem
        )
        load.start()
        fetch(step).wait()

        @pl.when(step + 1 < count)
        def _():
            fetch(step + 1).start()

        image = image_buf[lax.rem(step, 2)]
        padded_image[1, centre, :] = image
        fill(padded_image, image)
        load.wait()
        grad = padded_grad[1, centre, :]
        fill(padded_grad, grad)
        turned[...] = jnp.transpose(grad)
        slot = lax.rem(step, 2)

        @pl.when(step >= 2)
        def _():
            pixel_copy(step - 2).wait_send()

        def through(target):
            start = pl.multiple_of(target * rows, rows)
            total = jnp.zeros((rows, depth), floats)
            for a in range(3):
                for b in range(3):
                    window = padded_grad[
                        2 - b, pl.ds(pl.multiple_of(start + (2 - a) * width, 16), rows), :
                    ]
                    total = total + mul_nt(window, kernel_ref[sample, 3 * a + b])
            return total

        def give(i):
            pixel_out[slot, i] = through(jnp.where(i == 0, near, cross)).astype(halves)

        def keep(i):
            kept[slot, i] = through(jnp.where(i == 0, col, far))

        loop(2, give)
        pixel_copy(step).start()
        loop(2, keep)
        style = styles_ref[sample]
        scale = style[0:1, :depth]
        first, second = style[1:2, 0:1], style[2:3, 0:1]
        both = jnp.concatenate(
            [
                jnp.broadcast_to(inverse_ref[pl.ds(sample, 1), :], (8, channels)),
                sums_in[sample],
            ],
            axis=0,
        )
        columns = jnp.transpose(both)
        inverse, total = columns[:, 0:1], columns[:, 8:9]
        factor = inverse * inverse * total
        by_scale = jnp.zeros((1, depth), floats)
        by_first = jnp.zeros((1, depth), floats)
        by_second = jnp.zeros((1, depth), floats)
        for a in range(3):
            for b in range(3):
                tap = 3 * a + b
                found = mul(turned[...], padded_image[b, pl.ds(a * width, tokens), :])
                one, two = bank_ref[0, tap].astype(floats), bank_ref[1, tap].astype(floats)
                selected = first * one + second * two
                modded = inverse * found - factor * (selected * scale)
                by_scale = by_scale + jnp.sum(modded * selected, 0, keepdims=True)
                grad_selected = modded * scale
                acc[0, tap] += first * grad_selected
                acc[1, tap] += second * grad_selected
                by_first = by_first + jnp.sum(grad_selected * one, 0, keepdims=True)
                by_second = by_second + jnp.sum(grad_selected * two, 0, keepdims=True)
        stats_ref[sample, 0:1, :depth] = by_scale
        stats_ref[sample, 1:2, :depth] = by_first
        stats_ref[sample, 2:3, :depth] = by_second

    def across(step):
        slot = lax.rem(step, 2)
        pixel_copy(step).wait_recv()

        @pl.when(step >= 2)
        def _():
            line_copy(step - 2).wait_send()

        line_out[slot] = (kept[slot, 1] + pixel_in[step, 1].astype(floats)).astype(halves)
        line_copy(step).start()
        kept_own[slot] = kept[slot, 0] + pixel_in[step, 0].astype(floats)

    def home(step):
        slot = lax.rem(step, 2)
        line_copy(step).wait_recv()

        @pl.when(step >= 3)
        def _():
            owner_copy(step - 2).wait_send()

        owner_out[slot] = (kept_own[slot] + line_in[step].astype(floats)).astype(halves)

        @pl.when(step > 0)
        def _():
            owner_copy(step).start()

        @pl.when(step == 0)
        def _():
            mine = pltpu.make_async_copy(owner_out.at[slot], image_grad_ref.at[row], local_sem)
            mine.start()
            mine.wait()

    lax.fori_loop(1, count, sums_arrive, 0)

    def step_body(step):
        @pl.when(step < count)
        def _():
            work(step)

        @pl.when((step >= 1) & (step <= count))
        def _():
            across(step - 1)

        @pl.when(step >= 2)
        def _():
            home(step - 2)

    loop(count + 2, step_body)

    def write(index):
        bank_grad_ref[lax.div(index, 9), lax.rem(index, 9)] = jnp.transpose(
            acc[lax.div(index, 9), lax.rem(index, 9)]
        )

    loop(18, write)

    def owner_arrives(k, carry):
        origin = lax.rem(row - k + count, count)
        remote(
            owner_out.at[0],
            image_grad_ref.at[origin],
            owner_send.at[k],
            owner_recv.at[origin],
            (partner, col),
        ).wait_recv()
        return carry

    lax.fori_loop(1, count, owner_arrives, 0)
    for step in (count - 2, count - 1):
        pixel_copy(step).wait_send()
        line_copy(step).wait_send()
        owner_copy(step).wait_send()
    lax.fori_loop(1, groups, lambda k, c: (level_copy(k).wait_send(), c)[1], 0)
    loop(groups, lambda k: pair_copy(k).wait_send())
    lax.fori_loop(1, count, lambda k, c: (sums_copy(k).wait_send(), c)[1], 0)


def conv_backward(images_all, kernels, bank, styles, inverse, grad, conv, width):
    count, tokens, depth = images_all.shape
    channels = grad.shape[1]
    rows = tokens // PIX
    groups = count // 2
    piece = (rows, depth)
    return pl.pallas_call(
        partial(conv_back_kernel, count, width),
        out_shape=(
            jax.ShapeDtypeStruct((2, 9, depth, channels), floats),
            jax.ShapeDtypeStruct((count, 8, 128), floats),
            jax.ShapeDtypeStruct((count,) + piece, halves),
            jax.ShapeDtypeStruct((count, tokens, channels), halves),
        ),
        in_specs=[ANY] + [VMEM] * 6,
        out_specs=(VMEM, VMEM, ANY, ANY),
        scratch_shapes=[
            pltpu.VMEM((2, tokens, depth), halves),
            pltpu.VMEM((3, tokens + 2 * width, depth), halves),
            pltpu.VMEM((3, tokens + 2 * width, channels), halves),
            pltpu.VMEM((channels, tokens), halves),
            pltpu.VMEM((2, 9, channels, depth), floats),
            pltpu.VMEM((8, channels), floats),
            pltpu.VMEM((count, 8, channels), floats),
            pltpu.VMEM((2, 2) + piece, floats),
            pltpu.VMEM((2,) + piece, floats),
            pltpu.VMEM((2, 2) + piece, halves),
            pltpu.VMEM((count, 2) + piece, halves),
            pltpu.VMEM((2,) + piece, halves),
            pltpu.VMEM((count,) + piece, halves),
            pltpu.VMEM((2,) + piece, halves),
            DMA,
            DMA((2,)),
            DMA,
            DMA((count,)),
            DMA((count,)),
            DMA((groups,)),
            DMA((groups,)),
            DMA((groups,)),
            DMA((groups,)),
            DMA((count,)),
            DMA((count,)),
            DMA((count,)),
            DMA((count,)),
            DMA((count,)),
            DMA((count,)),
        ],
        compiler_params=params(4),
        name="conv_backward",
    )(images_all, kernels, bank, styles, inverse, grad, conv)


def small_kernel(
    count,
    small_ref,
    last_ref,
    stats_ref,
    rows_ref,
    stats_all_ref,
    rows_out,
    rows_in,
    stats_in,
    rows_send,
    rows_recv,
    stats_send,
    stats_recv,
    far_rows_send,
    far_rows_recv,
    far_stats_send,
    far_stats_recv,
):
    row, col = lax.axis_index("dp"), lax.axis_index("pix")
    near, far, cross = peers(col)
    targets = (far, cross, near)
    greet(count, [(row, near), (row, far), (row, cross)])
    rows_out[...] = small_ref[...]
    rows_out[5:6, :] = last_ref[0:1, :]

    def rows_copy(turn):
        return remote(
            rows_out, rows_in.at[turn], rows_send.at[turn], rows_recv.at[turn], (row, targets[turn])
        )

    def stats_copy(turn):
        return remote(
            stats_ref, stats_in.at[turn], stats_send.at[turn], stats_recv.at[turn], (row, targets[turn])
        )

    for turn in range(3):
        rows_copy(turn).start()
        stats_copy(turn).start()
    for turn in range(3):
        rows_copy(turn).wait()
        stats_copy(turn).wait()
    rows_in[3] = rows_out[...]
    stats_in[3] = stats_ref[...]

    def in_order(buffer):
        total = None
        for which in range(PIX):
            turn = jnp.where(
                which == col, 3, jnp.where(which == far, 0, jnp.where(which == cross, 1, 2))
            )
            total = buffer[turn] if total is None else total + buffer[turn]
        return total

    rows_ref[row] = in_order(rows_in)
    stats_all_ref[row] = in_order(stats_in)

    def far_rows(k):
        block = rows_ref.at[row]
        return remote(
            block, block, far_rows_send.at[k], far_rows_recv.at[k], (lax.rem(row + k, count), col)
        )

    def far_stats(k):
        block = stats_all_ref.at[row]
        return remote(
            block, block, far_stats_send.at[k], far_stats_recv.at[k], (lax.rem(row + k, count), col)
        )

    lax.fori_loop(1, count, lambda k, c: (far_rows(k).start(), far_stats(k).start(), c)[2], 0)

    def arrive(k, carry):
        origin = lax.rem(row - k + count, count)
        block = rows_ref.at[origin]
        remote(block, block, far_rows_send.at[k], far_rows_recv.at[k], (row, near)).wait_recv()
        block = stats_all_ref.at[origin]
        remote(block, block, far_stats_send.at[k], far_stats_recv.at[k], (row, near)).wait_recv()
        return carry

    lax.fori_loop(1, count, arrive, 0)
    lax.fori_loop(
        1, count, lambda k, c: (far_rows(k).wait_send(), far_stats(k).wait_send(), c)[2], 0
    )


def small_sums(small, last, stats):
    count = stats.shape[0]
    block = small.shape
    return pl.pallas_call(
        partial(small_kernel, count),
        out_shape=(
            jax.ShapeDtypeStruct((count,) + block, floats),
            jax.ShapeDtypeStruct((count,) + stats.shape, floats),
        ),
        in_specs=[VMEM] * 3,
        out_specs=(VMEM,) * 2,
        scratch_shapes=[
            pltpu.VMEM(block, floats),
            pltpu.VMEM((4,) + block, floats),
            pltpu.VMEM((4,) + stats.shape, floats),
            DMA((3,)),
            DMA((3,)),
            DMA((3,)),
            DMA((3,)),
            DMA((count,)),
            DMA((count,)),
            DMA((count,)),
            DMA((count,)),
        ],
        compiler_params=params(5),
        name="small_sums",
    )(small, last, stats)


def style_rows(style_codes, labels, class_table, select_weight, modulation, rgb_modulation):
    class_row = jnp.take(class_table, labels, axis=0).astype(floats)
    styled = style_codes.astype(floats) + class_row
    mixing = jax.nn.softmax(jnp.dot(styled, select_weight.astype(floats), precision=highest), -1)
    scaling = jnp.dot(styled, modulation.astype(floats), precision=highest) + 1.0
    rgb_scale = jnp.dot(styled, rgb_modulation.astype(floats), precision=highest) + 1.0
    return styled, mixing, scaling, rgb_scale


def pack_style(styled, labels, mixing, scaling, count):
    depth = scaling.shape[-1] // count
    pieces = jnp.pad(scaling.reshape(count, 1, depth), ((0, 0), (0, 0), (0, 128 - depth)))
    same = jnp.concatenate(
        [
            jnp.broadcast_to(mixing.reshape(2, 1), (2, 128)),
            styled.reshape(4, 128),
            jnp.broadcast_to(labels.astype(floats).reshape(1, 1), (1, 128)),
        ]
    )
    return jnp.concatenate([pieces, jnp.broadcast_to(same, (count, 7, 128))], axis=1)


def on_device(
    images,
    style_codes,
    labels,
    token_ids,
    penalty_mask,
    class_table,
    text_table,
    conv_bank,
    select_weight,
    modulation,
    rgb_modulation,
    w_query,
    w_key,
    w_value,
    w_out,
    c_query,
    c_key,
    c_value,
    c_out,
    gain_self,
    gain_cross,
    rgb_weight,
    out_cotangent,
    rgb_cotangent,
):
    count = lax.axis_size("dp")
    row, col = lax.axis_index("dp"), lax.axis_index("pix")
    _, height, width, channels = images.shape
    rows = height * width
    quarter = channels // PIX
    depth = channels // count

    def my_columns(*weights):
        return jnp.concatenate(
            [lax.dynamic_slice_in_dim(w, col * quarter, quarter, axis=1) for w in weights], axis=1
        )

    attention = lax.all_gather(my_columns(w_query, w_key, w_value), "dp", axis=0, tiled=True)
    text_weights = lax.all_gather(my_columns(c_key, c_value), "dp", axis=0, tiled=True)
    others = lax.all_gather(my_columns(w_out, c_query, c_out), "dp", axis=0, tiled=True)
    others = lax.all_gather(others, "pix", axis=0)

    styled, mixing, scaling, rgb_scale = style_rows(
        style_codes, labels, class_table, select_weight, modulation, rgb_modulation
    )
    own = images.reshape(rows, channels)
    parts = own.reshape(rows, count, depth).transpose(1, 0, 2)
    bank = conv_bank.reshape(2, 9, depth, quarter)
    bank_turned = bank.transpose(0, 1, 3, 2)
    words = token_ids.shape[1]
    text = jnp.take(text_table, token_ids[0], axis=0)
    text_padded = jnp.pad(text, ((0, 128 - words), (0, 0)))

    images_all, kernels, styles, inverse = gather_inputs(
        pack_style(styled, labels, mixing, scaling, count), bank, parts
    )
    images_all = images_all.reshape(count, PIX * rows, depth)
    conv, conv_own, hidden_one, normed_one = conv_forward(images_all, kernels, own, gain_self, width)
    query, key, value, totals, attended, text_all = attend_forward(
        normed_one, attention, text_padded, text_weights
    )
    rgb_rows = jnp.pad(rgb_cotangent.reshape(3, rows).T, ((0, 0), (0, 125)))
    penalty = jnp.broadcast_to(penalty_mask.astype(floats).reshape(1, 1), (1, 128))
    output, rgb, other_grads, text_grads, grad_two, grad_attended, small = cross_part(
        words,
        attended,
        hidden_one,
        others,
        text_all,
        gain_cross,
        rgb_scale,
        jnp.pad(rgb_weight, ((0, 0), (0, 125))),
        out_cotangent.reshape(rows, channels),
        rgb_rows,
        penalty,
    )
    other_owned = lax.psum_scatter(
        lax.psum_scatter(other_grads, "pix", scatter_dimension=0, tiled=False),
        "dp",
        scatter_dimension=0,
        tiled=True,
    )
    text_cols = lax.psum_scatter(text_grads, "pix", scatter_dimension=0, tiled=False)
    text_grad = lax.dot_general(
        text.astype(floats), text_cols[:words], TN, precision=highest, preferred_element_type=floats
    ).astype(halves)
    text_owned = lax.psum_scatter(text_grad, "dp", scatter_dimension=0, tiled=True)

    attention_grads, grad_one, grad_conv, last = attend_backward(
        grad_attended,
        query,
        key,
        value,
        totals,
        normed_one,
        attention,
        hidden_one,
        conv,
        grad_two,
        gain_self,
    )
    attention_owned = lax.psum_scatter(attention_grads, "dp", scatter_dimension=0, tiled=True)

    def whole(owned):
        full = lax.all_gather(owned, "pix", axis=0).astype(floats)
        pieces = owned.shape[1] // quarter
        full = full.reshape(PIX, owned.shape[0], pieces, quarter).transpose(2, 1, 0, 3)
        return full.reshape(pieces, owned.shape[0], channels)

    grad_w_query, grad_w_key, grad_w_value = whole(attention_owned)
    grad_w_out, grad_c_query, grad_c_out = whole(other_owned)
    grad_c_key, grad_c_value = whole(text_owned)

    bank_grad, stats, image_parts, _ = conv_backward(
        images_all,
        kernels,
        bank_turned,
        styles,
        inverse,
        grad_conv.reshape(PIX * rows, quarter),
        conv_own,
        width,
    )
    grad_image = grad_one + image_parts.transpose(1, 0, 2).reshape(rows, channels).astype(floats)
    all_rows, all_stats = small_sums(small, last, stats)

    styled_all = styles[:, 3:7, :].reshape(count, -1)
    mixing_all = styles[:, 1:3, 0]
    labels_all = styles[:, 7, 0].astype(jnp.int32)
    grad_scaling = all_stats[:, :, 0, :depth].transpose(1, 0, 2).reshape(count, channels)
    grad_mixing = jnp.sum(all_stats[:, :, 1:3, :], axis=(0, 3))
    grad_rgb_scale = all_rows[:, 1, :]
    inner = jnp.sum(grad_mixing * mixing_all, -1, keepdims=True)
    grad_logits = mixing_all * (grad_mixing - inner)

    def outer(right):
        return lax.dot_general(
            styled_all, right, TN, precision=highest, preferred_element_type=floats
        )

    def back(left, right):
        return lax.dot_general(
            left, right.astype(floats), NT, precision=highest, preferred_element_type=floats
        )

    grad_styles = (
        back(grad_logits, select_weight)
        + back(grad_scaling, modulation)
        + back(grad_rgb_scale, rgb_modulation)
    )
    classes = class_table.shape[0]
    chosen = (labels_all[:, None] == jnp.arange(classes, dtype=jnp.int32)[None, :]).astype(floats)
    grad_table = lax.dot_general(
        chosen, grad_styles, TN, precision=highest, preferred_element_type=floats
    )
    sums = jnp.sum(all_rows, axis=0)
    shape = images.shape
    return (
        output.reshape(shape),
        rgb[:, :3].T.reshape(1, 3, height, width),
        grad_image.reshape(shape),
        lax.dynamic_slice_in_dim(grad_styles, row, 1, axis=0),
        grad_table,
        bank_grad.reshape(conv_bank.shape),
        outer(grad_logits),
        outer(grad_scaling),
        outer(grad_rgb_scale),
        grad_w_query,
        grad_w_key,
        grad_w_value,
        grad_w_out,
        grad_c_query,
        grad_c_key,
        grad_c_value,
        grad_c_out,
        sums[5],
        sums[0],
        sums[2:5].T,
    )


def solution(mesh):
    return jax.shard_map(
        on_device,
        mesh=mesh,
        in_specs=(
            P("dp", "pix", None, None),
            P("dp", None),
            P("dp"),
            P("dp", None),
            P("dp"),
            P(),
            P(),
            P(None, None, None, "dp", "pix"),
            P(),
            P(),
            P(),
            P("dp", None),
            P("dp", None),
            P("dp", None),
            P("dp", None),
            P("dp", None),
            P("dp", None),
            P("dp", None),
            P("dp", None),
            P(),
            P(),
            P(),
            P("dp", "pix", None, None),
            P("dp", None, "pix", None),
        ),
        out_specs=(
            P("dp", "pix", None, None),
            P("dp", None, "pix", None),
            P("dp", "pix", None, None),
            P("dp", None),
            P(),
            P(None, None, None, "dp", "pix"),
            P(),
            P(),
            P(),
            P("dp", None),
            P("dp", None),
            P("dp", None),
            P("dp", None),
            P("dp", None),
            P("dp", None),
            P("dp", None),
            P("dp", None),
            P(),
            P(),
            P(),
        ),
        check_vma=False,
    )
```

time: 2260 us -> 643 us (0.28)
  waiting for transfers between devices: 1660 us -> 70 us
  Pallas kernels: 0 us -> 418 us
  matrix products: 186 us -> 15.9 us
  other arithmetic: 152 us -> 11.8 us
  local copies, waits for them, and re-layouts: 116 us -> 45.3 us
  starting transfers between devices: 31.4 us -> 0.71 us
  blocking collectives: 88.5 us -> 58.9 us
    reduce_scatter x10 -> x5, waiting for transfers between devices: 1040 us -> 24 us  [the longest x1 23.9 us: on_device(): lax.psum_scatter(lax.psum_scatter(other_grads, 'pix', scatter_dimension=0...]
    all_gather x10 -> x3, waiting for transfers between devices: 478 us -> 45.4 us  [the longest x1 45.3 us: on_device(): lax.all_gather(my_columns(w_out, c_query, c_out), 'dp', axis=0, tiled=True)]
    pallas_call x0 -> x7, Pallas kernels: none -> 418 us  [the longest x1 146 us: conv_backward(): pl.pallas_call(partial(conv_back_kernel, count, width), out_shape=(jax.Sh...]
    dot_general x76 -> x11, matrix products: 183 us -> 15.9 us  [the longest x3 7.05 us: outer(): lax.dot_general(styled_all, right, TN, precision=highest, preferred_eleme...]
    psum x2 -> x0, waiting for transfers between devices: 124 us -> none  [the longest x1 124 us: on_device(): lax.psum((grad_table, grad_select, grad_modulation, grad_rgb_mod, grad_ga...]
    all_gather x0 -> x4, blocking collectives: none -> 58.9 us  [the longest x1 35.4 us: on_device(): lax.all_gather(my_columns(c_key, c_value), 'dp', axis=0, tiled=True)]
    psum x2 -> x0, blocking collectives: 51.5 us -> none  [the longest x1 44.7 us: on_device(): lax.psum((grad_table, grad_select, grad_modulation, grad_rgb_mod, grad_ga...]
    unnamed x256 -> x43, local copies, waits for them, and re-layouts: 62 us -> 13.7 us
  transfers between devices with their start and end apart: 31 -> 8, of which waited for: 20 -> 2; matrix products, arithmetic and copies ran while one was open for 18% -> 9% of each run, Pallas kernels for 0% -> 60%
where the time goes in v1:
time: 643 us; the launch traced here: 637 us
  Pallas kernels  418 us (65%)
  waiting for transfers between devices  70 us (11%)
  blocking collectives  58.9 us (9%)
  local copies, waits for them, and re-layouts  45.3 us (7%)
  between operations  16.1 us (3%)
  matrix products  15.9 us (2%)
  other arithmetic  11.8 us (2%)
    pallas_call x1, Pallas kernels, conv_backward(): pl.pallas_call(partial(conv_back_kernel, count, width), out_shape=(jax.Sh...  146 us
    pallas_call x1, Pallas kernels, conv_forward(): pl.pallas_call(partial(conv_kernel, count, width), out_shape=(jax.ShapeDt...  95 us
    pallas_call x1, Pallas kernels, attend_backward(): pl.pallas_call(attend_back_kernel, out_shape=(jax.ShapeDtypeStruct(weight...  67.9 us
    all_gather x1, waiting for transfers between devices, on_device(): lax.all_gather(my_columns(w_out, c_query, c_out), 'dp', axis=0, tiled=True)  45.3 us
    pallas_call x1, Pallas kernels, cross_part(): pl.pallas_call(partial(cross_kernel, words), out_shape=(jax.ShapeDtypeStr...  38.3 us
    all_gather x1, blocking collectives, on_device(): lax.all_gather(my_columns(c_key, c_value), 'dp', axis=0, tiled=True)  35.4 us
    pallas_call x1, Pallas kernels, gather_inputs(): pl.pallas_call(partial(gather_kernel, count), out_shape=(jax.ShapeDtypeSt...  29.6 us
    reduce_scatter x1, waiting for transfers between devices, on_device(): lax.psum_scatter(lax.psum_scatter(other_grads, 'pix', scatter_dimension=0...  23.9 us
  transfers between devices with their start and end apart: 8, of which 2 were waited for; matrix products, arithmetic and copies ran while one was open for 9% of the time, Pallas kernels for 60%

profile of v1, /device:TPU:0, one launch (start us, length us, event | category | flops | bytes accessed | tf_op | source)
XLA Modules:
  0.0 637.0 jit_solution(2388109197825465800)
XLA Ops:
  12.4 45.3 %all-gather.10.cloned.1.call-done = bf16[1024,768]{1,0:T(8,128)(2,1)} async-done(((bf16[128,768]{1,0:T(8,128)(2,1)}), bf16[1024,768]{1,0:T(8,128)(2,1)}) %all-gather.10.cloned.1.call-update) | async-done | bytes 1572880 | tf_op jit(solution)/shard_map/all_gather | solution.py:1737
  63.8 3.5 gather_fusion
  71.5 29.6 %gather_inputs.1 = (bf16[8,4,256,128]{3,2,1,0:T(8,128)(2,1)}, bf16[8,9,128,256]{3,2,1,0:T(8,128)(2,1)}, f32[8,8,128]{2,1,0:T(8,128)}, f32[8,256]{1,0:T(8,128)}) custom-call(f32[8,8,128]{2,1,0:T(8,128)} %pad_maximum_fusion.3.style_ref, bf16[2,9,128,256]{3,2,1,0:T(8,128)(2,1)} %bitcast.126, bf16[8,256,128]{2,1,0:T(8,128)(2,1)} %bitcast.133), custom_call_target="tpu_custom_call" | custom-call | tf_op jit(solution)/shard_map/gather_inputs/pallas_call | solution.py:249
  101.2 95.0 %conv_forward.1 = (bf16[256,1024]{1,0:T(8,128)(2,1)}, bf16[1024,256]{1,0:T(8,128)(2,1)}, f32[256,1024]{1,0:T(8,128)}, bf16[4,256,1024]{2,1,0:T(8,128)(2,1)}) custom-call(bf16[8,1024,128]{2,1,0:T(8,128)(2,1)} %bitcast.121, bf16[8,9,128,256]{3,2,1,0:T(8,128)(2,1)} %get-tuple-element.51.kernel_ref, bf16[256,1024]{1,0:T(8,128)(2,1)} %bitcast.131, ...), custom_call_target="tpu_custom_call" | custom-call | tf_op jit(solution)/shard_map/conv_forward/pallas_call | solution.py:507
  198.2 35.4 %all_gather.34.text_weight_ref = bf16[768,512]{1,0:T(8,128)(2,1)} all-gather(bf16[96,512]{1,0:T(8,128)(2,1)S(1)} %pad_maximum_fusion.2), channel_id=1, replica_groups=mesh['dp'=8,'pix'=4] {'dp'}, dimensions={0}, use_global_device_ids=true | all-gather | bytes 884736 | tf_op jit(solution)/shard_map/all_gather | solution.py:1736
  233.6 21.0 %attend_forward.1 = (bf16[1024,256]{1,0:T(8,128)(2,1)}, bf16[1024,256]{1,0:T(8,128)(2,1)}, bf16[1024,256]{1,0:T(8,128)(2,1)}, f32[1024,128]{1,0:T(8,128)}, bf16[...) custom-call(bf16[4,256,1024]{2,1,0:T(8,128)(2,1)} %get-tuple-element.52.normed_ref, ...), custom_call_target="tpu_custom_call" | custom-call | tf_op jit(solution)/shard_map/attend_forward/pallas_call | solution.py:677
  255.1 38.3 %cross_part.1 = (f32[256,1024]{1,0:T(8,128)}, f32[256,128]{1,0:T(8,128)}, bf16[4,1024,768]{2,1,0:T(8,128)(2,1)}, f32[4,128,512]{2,1,0:T(8,128)}, f32[256,1024]{1...) custom-call(bf16[4,256,256]{2,1,0:T(8,128)(2,1)} %get-tuple-element.53.attended_ref, ...), custom_call_target="tpu_custom_call" | custom-call | tf_op jit(solution)/shard_map/cross_part/pallas_call | solution.py:893
  294.3 67.9 %attend_backward.1 = (bf16[1024,768]{1,0:T(8,128)(2,1)}, f32[256,1024]{1,0:T(8,128)}, bf16[4,256,256]{2,1,0:T(8,128)(2,1)}, f32[8,1024]{1,0:T(8,128)}) custom-call(bf16[4,256,256]{2,1,0:T(8,128)(2,1)} %get-tuple-element.58.grad_ref, bf16[1024,256]{1,0:T(8,128)(2,1)} %get-tuple-element.59.query_ref, bf16[1024,256]{1,0:T(8,128)(2,1)} %get-tuple-element.60.key_ref, ...), custom_call_target="tpu_custom_call" | custom-call | tf_op jit(solution)/shard_map/attend_backward/pallas_call | solution.py:1137
  362.3 2.7 convolution_convert_fusion
  367.1 146.2 %conv_backward.1 = (f32[2,9,128,256]{3,2,1,0:T(8,128)}, f32[8,8,128]{2,1,0:T(8,128)}, bf16[8,256,128]{2,1,0:T(8,128)(2,1)}, bf16[8,1024,256]{2,1,0:T(8,128)(2,1)}) custom-call(bf16[8,1024,128]{2,1,0:T(8,128)(2,1)} %bitcast.122, bf16[8,9,128,256]{3,2,1,0:T(8,128)(2,1)} %get-tuple-element.51.kernel_ref, bf16[2,9,256,128]{3,2,1,0:T(8,128)(2,1)} %bitcast.127, ...), custom_call_target="tpu_custom_call" | custom-call | tf_op jit(solution)/shard_map/conv_backward/pallas_call | solution.py:1515
  513.3 20.2 %small_sums.1 = (f32[8,8,1024]{2,1,0:T(8,128)}, f32[8,8,8,128]{3,2,1,0:T(8,128)}) custom-call(f32[8,1024]{1,0:T(8,128)} %get-tuple-element.71.small_ref, f32[8,1024]{1,0:T(8,128)} %get-tuple-element.72.last_ref, f32[8,8,128]{2,1,0:T(8,128)} %get-tuple-element.73.stats_ref), custom_call_target="tpu_custom_call" | custom-call | tf_op jit(solution)/shard_map/small_sums/pallas_call | solution.py:1649
  541.8 2.3 add.85
  548.5 2.4 fusion.3
  550.9 3.2 fusion
  554.1 3.2 fusion.7
  557.2 7.5 %all-gather.1 = bf16[512,768]{1,0:T(8,128)(2,1)S(1)} all-gather(bf16[128,768]{1,0:T(8,128)(2,1)} %reduce-scatter.6.cloned.1.call-done), channel_id=3, replica_groups=mesh['dp'=8,'pix'=4] {'pix'}, dimensions={0}, use_global_device_ids=true | all-gather | bytes 983040 | tf_op jit(solution)/shard_map/all_gather | solution.py:1802
  566.2 1.8 reshape.288
  572.0 7.2 %all-gather.3 = bf16[384,512]{1,0:T(8,128)(2,1)S(1)} all-gather(bf16[96,512]{1,0:T(8,128)(2,1)} %reduce-scatter.14.cloned.1.call-done), channel_id=5, replica_groups=mesh['dp'=8,'pix'=4] {'pix'}, dimensions={0}, use_global_device_ids=true | all-gather | bytes 491520 | tf_op jit(solution)/shard_map/all_gather | solution.py:1802
  582.5 23.9 %reduce-scatter.10.cloned.1.call-done = bf16[128,768]{1,0:T(8,128)(2,1)} async-done(((bf16[1024,768]{1,0:T(8,128)(2,1)}), bf16[128,768]{1,0:T(8,128)(2,1)}) %reduce-scatter.10.cloned.1.call-update) | async-done | bytes 196624 | tf_op jit(solution)/shard_map/reduce_scatter | solution.py:1774
  606.4 8.8 %all-gather.2 = bf16[512,768]{1,0:T(8,128)(2,1)S(1)} all-gather(bf16[128,768]{1,0:T(8,128)(2,1)} %reduce-scatter.10.cloned.1.call-done), channel_id=4, replica_groups=mesh['dp'=8,'pix'=4] {'pix'}, dimensions={0}, use_global_device_ids=true | all-gather | bytes 983040 | tf_op jit(solution)/shard_map/all_gather | solution.py:1802
  620.5 2.0 copy.152
  622.5 2.0 copy.161
  624.5 1.9 copy.155
  626.4 2.0 copy.162
  (128 shorter events, 47.5 us)
Async XLA Ops:
  7.2 63.2 %copy-start = (bf16[512,1024]{1,0:T(8,128)(2,1)S(1)}, bf16[512,1024]{1,0:T(8,128)(2,1)}, u32[]{:S(2)}) copy-start(bf16[512,1024]{1,0:T(8,128)(2,1)} %param.33) | copy-start | bytes 3145732
  7.2 51.3 %copy-start.11 = (bf16[1,512]{1,0:T(2,128)(2,1)S(1)}, bf16[1,512]{1,0:T(2,128)(2,1)}, u32[]{:S(2)}) copy-start(bf16[1,512]{1,0:T(2,128)(2,1)} %param.25) | copy-start | bytes 3076
  7.2 52.0 %copy-start.12 = (bf16[512,2]{0,1:T(2,128)(2,1)S(1)}, bf16[512,2]{0,1:T(2,128)(2,1)}, u32[]{:S(2)}) copy-start(bf16[512,2]{0,1:T(2,128)(2,1)} %param.32) | copy-start | bytes 6148
  7.2 55.3 %copy-start.4 = (bf16[1,8,32,1024]{3,2,1,0:T(8,128)(2,1)S(1)}, bf16[1,8,32,1024]{3,2,1,0:T(8,128)(2,1)}, u32[]{:S(2)}) copy-start(bf16[1,8,32,1024]{3,2,1,0:T(8,128)(2,1)} %param.24) | copy-start | bytes 1572868
  7.2 50.5 %all-gather.10.cloned.1.call-start = ((), (), s32[]{:S(2)}) async-start(), calls=%async_computation.6 | async-start | bytes 1769472 | tf_op jit(solution)/shard_map/all_gather | solution.py:1737
  9.8 223.7 %all-gather.8.cloned.1.call-start = ((), (), s32[]{:S(2)}) async-start(), calls=%async_computation.5 | async-start | bytes 1769472 | tf_op jit(solution)/shard_map/all_gather | solution.py:1735
  12.3 51.2 %copy-start.10 = (bf16[1024,3]{0,1:T(4,128)(2,1)S(1)}, bf16[1024,3]{0,1:T(4,128)(2,1)}, u32[]{:S(2)}) copy-start(bf16[1024,3]{0,1:T(4,128)(2,1)} %param.45) | copy-start | bytes 18436
  12.3 51.4 %copy-start.13 = (s32[1,77]{1,0:T(1,128)S(1)}, s32[1,77]{1,0:T(1,128)}, u32[]{:S(2)}) copy-start(s32[1,77]{1,0:T(1,128)} %param.27) | copy-start | bytes 928
  12.4 242.2 %all-gather.12.cloned.1.call-start = ((), (), s32[]{:S(2)}) async-start(), calls=%async_computation.12 | async-start | bytes 7864320 | tf_op jit(solution)/shard_map/all_gather | solution.py:1738
  57.8 304.5 %reduce-scatter.12.cloned.1.call-start = ((), (), s32[]{:S(2)}) async-start(), calls=%async_computation.10 | async-start | bytes 1310720 | tf_op jit(solution)/shard_map/reduce_scatter | solution.py:1780
  62.6 6.3 copy-start.9
  101.2 95.9 %copy-start.2 = (bf16[512,1024]{1,0:T(8,128)(2,1)S(1)}, bf16[512,1024]{1,0:T(8,128)(2,1)}, u32[]{:S(2)}) copy-start(bf16[512,1024]{1,0:T(8,128)(2,1)} %param.34) | copy-start | bytes 3145732
  293.5 243.4 %reduce-scatter.8.cloned.1.call-start = ((), (), s32[]{:S(2)}) async-start(), calls=%async_computation.8 | async-start | bytes 7864320 | tf_op jit(solution)/shard_map/reduce_scatter | solution.py:1775
  294.0 263.2 %reduce-scatter.6.cloned.1.call-start = ((), (), s32[]{:S(2)}) async-start(), calls=%async_computation.7 | async-start | bytes 1769472 | tf_op jit(solution)/shard_map/reduce_scatter | solution.py:1799
  362.1 3.1 copy-start.1
  362.2 4.5 copy-start.7
  362.2 209.8 %reduce-scatter.14.cloned.1.call-start = ((), (), s32[]{:S(2)}) async-start(), calls=%async_computation.11 | async-start | bytes 884736 | tf_op jit(solution)/shard_map/reduce_scatter | solution.py:1784
  365.0 241.4 %reduce-scatter.10.cloned.1.call-start = ((), (), s32[]{:S(2)}) async-start(), calls=%async_computation.9 | async-start | bytes 1769472 | tf_op jit(solution)/shard_map/reduce_scatter | solution.py:1774
  533.5 4.6 copy-start.6
  538.2 2.9 copy-start.8
  568.8 1.0 copy-start.5
  620.5 8.0 %copy-start.3 = (f32[2,9,128,256]{3,2,1,0:T(8,128)S(1)}, f32[2,9,128,256]{3,2,1,0:T(8,128)}, u32[]{:S(2)}) copy-start(f32[2,9,128,256]{3,2,1,0:T(8,128)} %get-tuple-element.76) | copy-start | bytes 7077892
Sparse Core Ops, SparseCore 0:
  10.8 46.8 all-gather.9
  60.5 47.7 all-gather.7
  109.9 45.3 all-gather.11
  293.6 24.1 reduce-scatter.11
  320.3 66.0 reduce-scatter.7
  389.6 77.3 reduce-scatter.5
  470.7 67.8 reduce-scatter.13
  542.0 64.3 reduce-scatter.9

commit v2 on v1

--- a/solution.py
+++ b/solution.py
@@ -67,6 +67,15 @@
 def flip(index, bit):
     part = lax.rem(lax.div(index, bit), 2)
     return index + bit - 2 * bit * part
+
+
+def level_at(level, groups, index):
+    both = jnp.minimum(level, groups - 1 - level)
+    step = lax.div(index + 1, 2)
+    near = jnp.where(lax.rem(index, 2) == 1, level - step, level + step)
+    rest = index - both
+    far = jnp.where(level > groups - 1 - level, level - rest, level + rest)
+    return jnp.where(index == 0, level, jnp.where(index <= 2 * both, near, far))
 
 
 def gather_kernel(
@@ -310,20 +319,22 @@
     rows = tokens // PIX
     halo = width
 
+    has_below, has_above = level > 0, level < groups - 1
+    below, above = jnp.maximum(row - 2, 0), jnp.minimum(row + 2, count - 1)
+
     barrier = pltpu.get_barrier_semaphore()
-
-    def hello(step, carry):
-        other = 2 * lax.rem(level + step, groups) + side
-        pl.semaphore_signal(barrier, inc=1, device_id=(other, col), device_id_type=MESH)
-        return carry
-
-    lax.fori_loop(1, groups, hello, 0)
+    for known, other in ((has_below, below), (has_above, above)):
+
+        @pl.when(known)
+        def _(other=other):
+            pl.semaphore_signal(barrier, inc=1, device_id=(other, col), device_id_type=MESH)
+
     for other in ((partner, col), (row, near), (row, far), (row, cross)):
         pl.semaphore_signal(barrier, inc=1, device_id=other, device_id_type=MESH)
-    pl.semaphore_wait(barrier, groups - 1 + 4)
+    pl.semaphore_wait(barrier, 4 + has_below.astype(jnp.int32) + has_above.astype(jnp.int32))
 
     def group_of(step):
-        return lax.rem(level + 1 + step, groups)
+        return level_at(level, groups, groups - 1 - step)
 
     def sample_of(index):
         mine = lax.div(index, groups)
@@ -376,15 +387,24 @@
             (partner, col),
         )
 
-    def line_copy(step):
+    def line_copy(step, upward):
         group = group_of(step)
+        if upward:
+            slot, target = group, above
+        else:
+            slot, target = jnp.where(group == level - 1, groups, group), below
         return remote(
             line_out.at[lax.rem(step, slots)],
-            line_in.at[step],
+            line_in.at[slot],
             line_send.at[step],
-            line_recv.at[step],
-            (2 * group + side, col),
-        )
+            line_recv.at[slot],
+            (target, col),
+        )
+
+    def line_arrives(slot):
+        remote(
+            line_out.at[0], line_in.at[slot], line_send.at[0], line_recv.at[slot], (partner, col)
+        ).wait_recv()
 
     def give(step):
         @pl.when(step >= slots)
@@ -408,21 +428,52 @@
     def keep(step):
         @pl.when(step >= slots)
         def _():
-            line_copy(step - slots).wait_send()
+            line_copy(step - slots, True).wait_send()
 
         stage(groups + step)
-        sample = sample_of(groups + step)
-        pair_copy(step).wait_recv()
+        group = group_of(step)
+        sample = 2 * group + side
+        out = lax.rem(step, slots)
 
         def chunk(i):
             start = pl.multiple_of(i * rows, rows)
-            here = pl.ds(start, rows)
-            line_out[lax.rem(step, slots), here, :] = (
-                rows_of(sample, start) + pair_in[step, here, :].astype(floats)
-            ).astype(halves)
+            total[pl.ds(start, rows), :] = rows_of(sample, start)
 
         loop(PIX, chunk)
-        line_copy(step).start()
+        pair_copy(step).wait_recv()
+        passing = jnp.where(group > level, has_below, has_above)
+
+        @pl.when(passing)
+        def _():
+            line_arrives(group)
+
+            def add(i):
+                here = pl.ds(pl.multiple_of(i * rows, rows), rows)
+                line_out[out, here, :] = (
+                    total[here, :]
+                    + pair_in[step, here, :].astype(floats)
+                    + line_in[group, here, :].astype(floats)
+                ).astype(halves)
+
+            loop(PIX, add)
+
+        @pl.when(jnp.logical_not(passing))
+        def _():
+            def add(i):
+                here = pl.ds(pl.multiple_of(i * rows, rows), rows)
+                line_out[out, here, :] = (
+                    total[here, :] + pair_in[step, here, :].astype(floats)
+                ).astype(halves)
+
+            loop(PIX, add)
+
+        @pl.when(group > level)
+        def _():
+            line_copy(step, True).start()
+
+        @pl.when(group < level)
+        def _():
+            line_copy(step, False).start()
 
     loop(groups - 1, keep)
     last = groups - 1
@@ -434,7 +485,17 @@
 
     loop(PIX, own_chunk)
     pair_copy(last).wait_recv()
-    loop(groups - 1, lambda i: line_copy(i).wait_recv())
+    for known, slot in ((has_below, level), (has_above, groups)):
+
+        @pl.when(known)
+        def _(slot=slot):
+            line_arrives(slot)
+
+            def add(i):
+                here = pl.ds(pl.multiple_of(i * rows, rows), rows)
+                total[here, :] += line_in[slot, here, :].astype(floats)
+
+            loop(PIX, add)
 
     def block_copy(turn):
         target = (far, cross, near)[turn]
@@ -451,8 +512,6 @@
     for turn, target in enumerate((far, cross, near, col)):
         here = pl.ds(pl.multiple_of(target * rows, rows), rows)
         value = total[here, :] + pair_in[last, here, :].astype(floats)
-        for i in range(groups - 1):
-            value = value + line_in[i, here, :].astype(floats)
         rounded = value.astype(halves)
         conv_own_ref[here, :] = rounded
         if turn < 3:
@@ -494,7 +553,7 @@
     for step in range(max(0, groups - slots), groups):
         pair_copy(step).wait_send()
     for step in range(max(0, groups - 1 - slots), groups - 1):
-        line_copy(step).wait_send()
+        line_copy(step, True).wait_send()
 
 
 def conv_forward(images_all, kernels, own, gain, width):
@@ -521,14 +580,14 @@
             pltpu.VMEM((slots,) + block, halves),
             pltpu.VMEM((groups,) + block, halves),
             pltpu.VMEM((slots,) + block, halves),
-            pltpu.VMEM((max(groups - 1, 1),) + block, halves),
+            pltpu.VMEM((groups + 1,) + block, halves),
             pltpu.VMEM((3, rows, channels), halves),
             pltpu.VMEM((PIX, rows, channels), halves),
             DMA((2,)),
             DMA((groups,)),
             DMA((groups,)),
             DMA((groups,)),
-            DMA((groups,)),
+            DMA((groups + 1,)),
             DMA((3,)),
             DMA((3,)),
             DMA((3,)),
@@ -571,7 +630,6 @@
     normed_ref,
     weight_ref,
     text_ref,
-    text_weight_ref,
     query_ref,
     key_ref,
     value_ref,
@@ -596,7 +654,8 @@
 
     for j in range(2):
         here = slice(j * width, (j + 1) * width)
-        text_out_ref[col, :, here] = mul(text_ref[...], text_weight_ref[:, here]).astype(halves)
+        weight = weight_ref[:, (3 + j) * width : (4 + j) * width]
+        text_out_ref[col, :, here] = mul(text_ref[...], weight).astype(halves)
 
     def text_copy(turn):
         block = text_out_ref.at[col]
@@ -669,9 +728,9 @@
         text_copy(turn).wait_send()
 
 
-def attend_forward(normed, weights, text, text_weights):
+def attend_forward(normed, weights, text):
     count, rows, full = normed.shape
-    tokens, width = count * rows, weights.shape[1] // 3
+    tokens, width = count * rows, weights.shape[1] // 5
     heads = width // HEAD_DIM
     flat = jax.ShapeDtypeStruct((tokens, width), halves)
     return pl.pallas_call(
@@ -684,7 +743,7 @@
             jax.ShapeDtypeStruct((PIX, rows, width), halves),
             jax.ShapeDtypeStruct((PIX, text.shape[0], 2 * width), halves),
         ),
-        in_specs=[VMEM] * 4,
+        in_specs=[VMEM] * 3,
         out_specs=(VMEM,) * 6,
         scratch_shapes=[
             pltpu.VMEM((4, rows, width), halves),
@@ -696,7 +755,7 @@
         ],
         compiler_params=params(2),
         name="attend_forward",
-    )(normed, weights, text, text_weights)
+    )(normed, weights, text)
 
 
 def cross_kernel(
@@ -713,12 +772,13 @@
     penalty_ref,
     output_ref,
     rgb_ref,
-    weight_grad_ref,
+    reduced_ref,
     text_grad_ref,
     grad_two_ref,
     grad_attended_ref,
     small_ref,
     attended,
+    grad_attn,
     two,
     normed,
     query,
@@ -730,8 +790,19 @@
     grad_crossed,
     grad_query,
     grad_norm,
-    grad_attn,
+    near_out,
+    near_in,
+    kept,
+    line_out,
+    line_in,
+    near_send,
+    near_recv,
+    line_send,
+    line_recv,
 ):
+    row, col = lax.axis_index("dp"), lax.axis_index("pix")
+    near, far, cross = peers(col)
+    greet_pixels(row, (near, far))
     rows, full = hidden_ref.shape
     tile = full // PIX
     score_scale = HEAD_DIM ** (-0.5)
@@ -740,6 +811,60 @@
 
     def cols(j):
         return pl.ds(pl.multiple_of(j * tile, tile), tile)
+
+    def near_copy(which):
+        return remote(
+            near_out.at[which], near_in.at[which], near_send.at[which], near_recv.at[which], (row, near)
+        )
+
+    def line_copy(which):
+        return remote(
+            line_out.at[which], line_in.at[which], line_send.at[which], line_recv.at[which], (row, far)
+        )
+
+    def start_grad(which, left, right):
+        def tile_of(index, targets):
+            i, b = lax.div(index, 2), lax.rem(index, 2)
+            return i, b, mul_tn(left[:, cols(i)], right[:, cols(jnp.where(b == 0, *targets))])
+
+        def give(index):
+            i, b, value = tile_of(index, (near, cross))
+            near_out[which, b, cols(i), :] = value.astype(halves)
+
+        def keep(index):
+            i, b, value = tile_of(index, (col, far))
+            kept[which, b, cols(i), :] = value
+
+        loop(2 * PIX, give)
+        near_copy(which).start()
+        loop(2 * PIX, keep)
+
+    def pass_grad(which):
+        near_copy(which).wait_recv()
+
+        def add(i):
+            here = cols(i)
+            line_out[which, here, :] = (
+                kept[which, 1, here, :] + near_in[which, 1, here, :].astype(floats)
+            ).astype(halves)
+
+        loop(PIX, add)
+        line_copy(which).start()
+
+    def end_grad(which):
+        line_copy(which).wait_recv()
+
+        def add(i):
+            here = cols(i)
+            reduced_ref[here, which * tile : (which + 1) * tile] = (
+                kept[which, 0, here, :]
+                + near_in[which, 0, here, :].astype(floats)
+                + line_in[which, here, :].astype(floats)
+            ).astype(halves)
+
+        loop(PIX, add)
+        near_copy(which).wait_send()
+        line_copy(which).wait_send()
 
     for j in range(PIX):
         attended[:, j * tile : (j + 1) * tile] = attended_ref[j]
@@ -808,6 +933,7 @@
         grad_proj[:, cols(j)] = grad.astype(halves)
 
     loop(PIX, back_three)
+    start_grad(1, crossed, grad_proj)
 
     def times_transposed(source, j, which):
         acc = jnp.zeros((rows, tile), floats)
@@ -838,15 +964,18 @@
             grad_q.append(score_scale * mul(score, keys[:, lanes]))
             grad_k.append(score_scale * mul_tn(score, queries[:, lanes]))
         grad_query[:, here] = jnp.concatenate(grad_q, axis=1).astype(halves)
-        text_grad_ref[group, :, text_lanes(pair, 0)] = jnp.concatenate(grad_k, axis=1)
-        text_grad_ref[group, :, text_lanes(pair, 1)] = jnp.concatenate(grad_v, axis=1)
+        text_grad_ref[group, :, text_lanes(pair, 0)] = jnp.concatenate(grad_k, axis=1).astype(halves)
+        text_grad_ref[group, :, text_lanes(pair, 1)] = jnp.concatenate(grad_v, axis=1).astype(halves)
 
     loop(full // 128, back_pair)
+    pass_grad(1)
+    start_grad(0, normed, grad_query)
 
     def back_query(j):
         grad_norm[:, cols(j)] = times_transposed(grad_query, j, C_QUERY)
 
     loop(PIX, back_query)
+    pass_grad(0)
     small_ref[0:1, :] = jnp.zeros((1, full), floats)
 
     def back_norm(i):
@@ -867,19 +996,9 @@
 
     loop(PIX, back_attended)
 
-    def weight_grads(index):
-        i, j = lax.div(index, PIX), lax.rem(index, PIX)
-        for which, left, right in (
-            (W_OUT, attended, grad_attn),
-            (C_QUERY, normed, grad_query),
-            (C_OUT, crossed, grad_proj),
-        ):
-            weight_grad_ref[j, cols(i), which] = mul_tn(left[:, cols(i)], right[:, cols(j)]).astype(
-                halves
-            )
-
-    loop(PIX * PIX, weight_grads)
     small_ref[5:8, :] = jnp.zeros((3, full), floats)
+    end_grad(1)
+    end_grad(0)
 
 
 def cross_part(
@@ -895,16 +1014,17 @@
         out_shape=(
             jax.ShapeDtypeStruct((rows, full), floats),
             jax.ShapeDtypeStruct((rows, 128), floats),
-            jax.ShapeDtypeStruct(weights.shape, halves),
-            jax.ShapeDtypeStruct(text.shape, floats),
+            jax.ShapeDtypeStruct((full, 2 * tile), halves),
+            jax.ShapeDtypeStruct(text.shape, halves),
             jax.ShapeDtypeStruct((rows, full), floats),
             jax.ShapeDtypeStruct((PIX, rows, tile), halves),
             jax.ShapeDtypeStruct((8, full), floats),
+            jax.ShapeDtypeStruct((rows, full), halves),
+            jax.ShapeDtypeStruct((rows, full), halves),
         ),
         in_specs=[VMEM] * 10,
-        out_specs=(VMEM,) * 7,
+        out_specs=(VMEM,) * 9,
         scratch_shapes=[
-            slim,
             wide,
             slim,
             slim,
@@ -916,9 +1036,17 @@
             slim,
             slim,
             wide,
-            slim,
+            pltpu.VMEM((2, 2, full, tile), halves),
+            pltpu.VMEM((2, 2, full, tile), halves),
+            pltpu.VMEM((2, 2, full, tile), floats),
+            pltpu.VMEM((2, full, tile), halves),
+            pltpu.VMEM((2, full, tile), halves),
+            DMA((2,)),
+            DMA((2,)),
+            DMA((2,)),
+            DMA((2,)),
         ],
-        compiler_params=pltpu.CompilerParams(vmem_limit_bytes=VMEM_LIMIT),
+        compiler_params=params(6),
         name="cross_part",
     )(
         attended,
@@ -946,7 +1074,13 @@
     conv_ref,
     grad_two_ref,
     gain_ref,
-    weight_grad_ref,
+    text_ref,
+    text_grad_ref,
+    reduced_ref,
+    attended_ref,
+    grad_attn_ref,
+    attention_ref,
+    others_ref,
     grad_one_ref,
     grad_conv_ref,
     small_ref,
@@ -963,19 +1097,63 @@
     line_in,
     own,
     conv_out,
+    text_in,
+    near_out,
+    near_in,
+    near_kept,
+    far_out,
+    far_in,
+    side_in,
+    level_out,
+    level_in,
+    out_grad,
+    out_side_in,
+    out_level_out,
+    out_level_in,
+    attention_grad,
+    attention_in,
     grad_send,
     grad_recv,
+    text_send,
+    text_recv,
     pair_send,
     pair_recv,
     line_send,
     line_recv,
     conv_send,
     conv_recv,
+    near_send,
+    near_recv,
+    far_send,
+    far_recv,
+    side_send,
+    side_recv,
+    level_send,
+    level_recv,
+    out_side_send,
+    out_side_recv,
+    out_level_send,
+    out_level_recv,
+    attention_send,
+    attention_recv,
 ):
     row, col = lax.axis_index("dp"), lax.axis_index("pix")
     near, far, cross = peers(col)
     targets = (far, cross, near)
-    greet_pixels(row, targets)
+    groups, _, owned, _ = attention_grad.shape
+    side, level = lax.rem(row, 2), lax.div(row, 2)
+    partner = flip(row, 1)
+    barrier = pltpu.get_barrier_semaphore()
+
+    def hello(step, carry):
+        other = 2 * lax.rem(level + step, groups) + side
+        pl.semaphore_signal(barrier, inc=1, device_id=(other, col), device_id_type=MESH)
+        return carry
+
+    lax.fori_loop(1, groups, hello, 0)
+    for other in ((partner, col), (row, near), (row, far), (row, cross)):
+        pl.semaphore_signal(barrier, inc=1, device_id=other, device_id_type=MESH)
+    pl.semaphore_wait(barrier, groups - 1 + 4)
     rows, full = hidden_ref.shape
     tokens, width = query_ref.shape
     heads = width // HEAD_DIM
@@ -990,8 +1168,125 @@
             (row, targets[turn]),
         )
 
+    used = text_in.shape[1]
+
+    def text_copy(turn):
+        return remote(
+            text_grad_ref.at[targets[turn], pl.ds(0, used), :],
+            text_in.at[turn],
+            text_send.at[turn],
+            text_recv.at[turn],
+            (row, targets[turn]),
+        )
+
     for turn in range(3):
         grad_copy(turn).start()
+    for turn in range(3):
+        text_copy(turn).start()
+
+    def side_copy():
+        return remote(
+            reduced_ref.at[:, 1 - side], side_in, side_send, side_recv, (partner, col)
+        )
+
+    def out_side_copy():
+        return remote(
+            out_grad.at[:, 1 - side], out_side_in, out_side_send, out_side_recv, (partner, col)
+        )
+
+    def level_copy(k):
+        group = lax.rem(level + k, groups)
+        return remote(
+            level_out.at[group], level_in.at[k], level_send.at[k], level_recv.at[k], (2 * group + side, col)
+        )
+
+    def out_level_copy(k):
+        group = lax.rem(level + k, groups)
+        return remote(
+            out_level_out.at[group],
+            out_level_in.at[k],
+            out_level_send.at[k],
+            out_level_recv.at[k],
+            (2 * group + side, col),
+        )
+
+    def level_sum(copy, source, arrived, out):
+        copy().wait_recv()
+
+        def add(group):
+            out[group] = (source[group, side].astype(floats) + arrived[group].astype(floats)).astype(
+                halves
+            )
+
+        loop(groups, add)
+
+    side_copy().start()
+
+    def near_copy():
+        return remote(near_out, near_in, near_send, near_recv, (row, near))
+
+    def far_copy():
+        return remote(far_out, far_in, far_send, far_recv, (row, far))
+
+    def row_tile(i):
+        return pl.ds(pl.multiple_of(i * width, width), width)
+
+    def out_tile(index, first, second):
+        i, b = lax.div(index, 2), lax.rem(index, 2)
+        right = grad_attn_ref[:, row_tile(jnp.where(b == 0, first, second))]
+        return i, b, mul_tn(attended_ref[:, row_tile(i)], right)
+
+    def out_give(index):
+        i, b, value = out_tile(index, near, cross)
+        near_out[b, row_tile(i), :] = value.astype(halves)
+
+    def out_keep(index):
+        i, b, value = out_tile(index, col, far)
+        near_kept[b, row_tile(i), :] = value
+
+    loop(2 * PIX, out_give)
+    near_copy().start()
+    loop(2 * PIX, out_keep)
+    per_tile = width // (2 * owned)
+
+    def out_pass():
+        near_copy().wait_recv()
+
+        def add(i):
+            here = row_tile(i)
+            far_out[here, :] = (
+                near_kept[1, here, :] + near_in[1, here, :].astype(floats)
+            ).astype(halves)
+
+        loop(PIX, add)
+        far_copy().start()
+
+    def out_end():
+        far_copy().wait_recv()
+
+        def add(i):
+            here = row_tile(i)
+            value = (
+                near_kept[0, here, :]
+                + near_in[0, here, :].astype(floats)
+                + far_in[here, :].astype(floats)
+            ).astype(halves)
+            out_grad[pl.ds(i * per_tile, per_tile)] = value.reshape(per_tile, 2, owned, width)
+
+        loop(PIX, add)
+        out_side_copy().start()
+
+    def between(h):
+        if h == 0:
+            out_pass()
+            level_sum(side_copy, reduced_ref, side_in, level_out)
+            lax.fori_loop(1, groups, lambda k, c: (level_copy(k).start(), c)[1], 0)
+        if h == 1:
+            out_end()
+        if h == 2:
+            level_sum(out_side_copy, out_grad, out_side_in, out_level_out)
+            lax.fori_loop(1, groups, lambda k, c: (out_level_copy(k).start(), c)[1], 0)
+
     grads[col] = grad_ref[col]
     totals[...] = jnp.transpose(total_ref[...])
     for turn in range(3):
@@ -1029,6 +1324,7 @@
             2.0 * score_scale * (acc[:, :HEAD_DIM] - wide * acc[:, HEAD_DIM : HEAD_DIM + 1])
         ).astype(halves)
         grad_value[:, lanes] = value_acc[...].astype(halves)
+        between(h)
 
     def norm_grad(block, store):
         here = pl.ds(pl.multiple_of(block * rows, rows), rows)
@@ -1069,13 +1365,42 @@
     pair_copy(1).wait_recv()
     norm_grad(col, store_own)
 
+    text_total = text_grad_ref[col, 0:used, :].astype(floats)
+    for turn in range(3):
+        text_copy(turn).wait_recv()
+        text_total = text_total + text_in[turn].astype(floats)
+    text_total = jnp.concatenate(
+        [text_total, jnp.zeros((text_ref.shape[0] - used, 2 * width), floats)], axis=0
+    )
+
+    def attention_copy(j):
+        here = pl.ds(j * per_tile, per_tile)
+        return remote(
+            attention_grad.at[here, 1 - side],
+            attention_in.at[here],
+            attention_send.at[j],
+            attention_recv.at[j],
+            (partner, col),
+        )
+
     def weight_grads(j):
-        cols = pl.ds(pl.multiple_of(j * width, width), width)
+        cols = row_tile(j)
+        here = pl.ds(j * per_tile, per_tile)
+
+        def put(k, value):
+            attention_grad[here, :, :, k * width : (k + 1) * width] = value.astype(halves).reshape(
+                per_tile, 2, owned, width
+            )
+
         for k, right in enumerate((grad_query, grad_key, grad_value)):
             acc = jnp.zeros((width, width), floats)
             for i in range(PIX):
                 acc = acc + mul_tn(normed_ref[i, :, cols], right[i * rows : (i + 1) * rows, :])
-            weight_grad_ref[cols, k * width : (k + 1) * width] = acc.astype(halves)
+            put(k, acc)
+        for k in range(2):
+            right = text_total[:, k * width : (k + 1) * width]
+            put(3 + k, mul_tn(text_ref[:, cols].astype(floats), right, highest))
+        attention_copy(j).start()
 
     loop(full // width, weight_grads)
     line.wait_recv()
@@ -1125,25 +1450,70 @@
     for turn in range(3):
         conv_copy(turn).wait_send()
         grad_copy(turn).wait_send()
+        text_copy(turn).wait_send()
+    total = level_out[level].astype(floats)
+    out_total = out_level_out[level].astype(floats)
+    for k in range(1, groups):
+        level_copy(k).wait()
+        out_level_copy(k).wait()
+        total = total + level_in[k].astype(floats)
+        out_total = out_total + out_level_in[k].astype(floats)
+    others_ref[:, 0:width] = out_total.astype(halves)
+    others_ref[:, width : 3 * width] = total.astype(halves)
+
+    def attention_sum(j):
+        attention_copy(j).wait_recv()
+        here = pl.ds(j * per_tile, per_tile)
+        attention_ref[here] = (
+            attention_grad[here, side].astype(floats) + attention_in[here].astype(floats)
+        ).astype(halves)
+
+    loop(full // width, attention_sum)
+    loop(full // width, lambda j: attention_copy(j).wait_send())
+    side_copy().wait_send()
+    out_side_copy().wait_send()
+    near_copy().wait_send()
+    far_copy().wait_send()
     pair_copy(0).wait_send()
     pair_copy(1).wait_send()
     line.wait_send()
 
 
-def attend_backward(grad, query, key, value, totals, normed, weights, hidden, conv, grad_two, gain):
+def attend_backward(
+    words,
+    grad,
+    query,
+    key,
+    value,
+    totals,
+    normed,
+    weights,
+    hidden,
+    conv,
+    grad_two,
+    gain,
+    text,
+    text_grads,
+    reduced,
+    attended,
+    grad_attn,
+):
     rows, full = hidden.shape
+    groups, _, owned, _ = reduced.shape
+    used = -(-words // 16) * 16
     tokens, width = query.shape
     flat = pltpu.VMEM((tokens, width), halves)
     return pl.pallas_call(
         attend_back_kernel,
         out_shape=(
-            jax.ShapeDtypeStruct(weights.shape, halves),
+            jax.ShapeDtypeStruct((groups, owned, 5 * width), halves),
+            jax.ShapeDtypeStruct((owned, 3 * width), halves),
             jax.ShapeDtypeStruct((rows, full), floats),
             jax.ShapeDtypeStruct((PIX, rows, width), halves),
             jax.ShapeDtypeStruct((8, full), floats),
         ),
-        in_specs=[VMEM] * 11,
-        out_specs=(VMEM,) * 4,
+        in_specs=[VMEM] * 16,
+        out_specs=(VMEM,) * 5,
         scratch_shapes=[
             pltpu.VMEM((PIX, rows, width), halves),
             flat,
@@ -1158,6 +1528,23 @@
             pltpu.VMEM((rows, full), halves),
             pltpu.VMEM((rows, full), floats),
             pltpu.VMEM((PIX, rows, width), halves),
+            pltpu.VMEM((3, used, 2 * width), halves),
+            pltpu.VMEM((2, full, width), halves),
+            pltpu.VMEM((2, full, width), halves),
+            pltpu.VMEM((2, full, width), floats),
+            pltpu.VMEM((full, width), halves),
+            pltpu.VMEM((full, width), halves),
+            pltpu.VMEM((groups, owned, 2 * width), halves),
+            pltpu.VMEM((groups, owned, 2 * width), halves),
+            pltpu.VMEM((groups, owned, 2 * width), halves),
+            pltpu.VMEM((groups, 2, owned, width), halves),
+            pltpu.VMEM((groups, owned, width), halves),
+            pltpu.VMEM((groups, owned, width), halves),
+            pltpu.VMEM((groups, owned, width), halves),
+            pltpu.VMEM((groups, 2, owned, 5 * width), halves),
+            pltpu.VMEM((groups, owned, 5 * width), halves),
+            DMA((3,)),
+            DMA((3,)),
             DMA((3,)),
             DMA((3,)),
             DMA((2,)),
@@ -1166,6 +1553,20 @@
             DMA,
             DMA((3,)),
             DMA((3,)),
+            DMA,
+            DMA,
+            DMA,
+            DMA,
+            DMA,
+            DMA,
+            DMA((groups,)),
+            DMA((groups,)),
+            DMA,
+            DMA,
+            DMA((groups,)),
+            DMA((groups,)),
+            DMA((PIX,)),
+            DMA((PIX,)),
         ],
         compiler_params=params(3),
         name="attend_backward",
@@ -1181,6 +1582,11 @@
         conv,
         grad_two,
         gain.reshape(1, -1),
+        text,
+        text_grads,
+        reduced,
+        attended,
+        grad_attn,
     )
 
 
@@ -1194,8 +1600,10 @@
     inverse_ref,
     grad_ref,
     conv_ref,
+    attention_ref,
     bank_grad_ref,
     stats_ref,
+    attention_sum_ref,
     image_grad_ref,
     grads_ref,
     image_buf,
@@ -1212,12 +1620,14 @@
     line_out,
     line_in,
     owner_out,
+    attention_in,
     local_sem,
     image_sem,
     load_sem,
     sums_send,
     sums_recv,
-    level_send,
+    up_send,
+    down_send,
     level_recv,
     pair_send,
     pair_recv,
@@ -1227,6 +1637,8 @@
     line_recv,
     owner_send,
     owner_recv,
+    attention_send,
+    attention_recv,
 ):
     row, col = lax.axis_index("dp"), lax.axis_index("pix")
     groups = count // 2
@@ -1234,23 +1646,61 @@
     partner = flip(row, 1)
     near, far, cross = peers(col)
     tokens, channels = grad_ref.shape
+
+    def attention_copy(k):
+        group = lax.rem(level + k, groups)
+        return remote(
+            attention_ref.at[group],
+            attention_in.at[k],
+            attention_send.at[k],
+            attention_recv.at[k],
+            (2 * group + side, col),
+        )
+
     depth = image_buf.shape[2]
     rows = tokens // PIX
     halo = width
     greet(count, [(row, near), (row, far)])
 
     def sample_of(step):
-        group = lax.rem(level - lax.div(step, 2) + groups, groups)
-        return 2 * group + jnp.where(lax.rem(step, 2) == 0, side, 1 - side)
-
-    def level_copy(k):
-        target = 2 * lax.rem(level + k, groups) + side
-        return remote(
-            grad_ref, grads_ref.at[row], level_send.at[k], level_recv.at[k], (target, col)
-        )
+        paired, k = turn_of(step)
+        return 2 * level_at(level, groups, k) + jnp.where(paired, 1 - side, side)
+
+    def turn_of(step):
+        final = step == count - 1
+        even = lax.rem(step, 2) == 0
+        paired = final | (even & (step > 0))
+        k = jnp.where(even, jnp.maximum(lax.div(step, 2) - 1, 0), lax.div(step + 1, 2))
+        return paired, jnp.where(final, groups - 1, k)
+
+    has_below, has_above = level > 0, level < groups - 1
+    reach = jnp.minimum(level, groups - 1 - level)
+
+    def line_block(origin, upward):
+        block = grads_ref.at[2 * origin + side]
+        sem = (up_send if upward else down_send).at[origin]
+        target = jnp.minimum(row + 2, count - 1) if upward else jnp.maximum(row - 2, 0)
+        return remote(block, block, sem, level_recv.at[origin], (target, col))
+
+    def relay(k):
+        origin = level_at(level, groups, k)
+        block = grads_ref.at[2 * origin + side]
+        remote(
+            block, block, up_send.at[origin], level_recv.at[origin], (partner, col)
+        ).wait_recv()
+
+        @pl.when((origin < level) & has_above)
+        def _():
+            line_block(origin, True).start()
+
+        @pl.when((origin > level) & has_below)
+        def _():
+            line_block(origin, False).start()
+
+        pair_copy(k).start()
 
     def pair_copy(k):
-        block = grads_ref.at[sample_of(2 * k)]
+        block = grads_ref.at[2 * level_at(level, groups, k) + side]
         return remote(block, block, pair_send.at[k], pair_recv.at[k], (partner, col))
 
     def sums_copy(k):
@@ -1264,8 +1714,16 @@
 
     own = pltpu.make_async_copy(grad_ref, grads_ref.at[row], local_sem)
     own.start()
-    lax.fori_loop(1, groups, lambda k, c: (level_copy(k).start(), c)[1], 0)
     own.wait()
+
+    @pl.when(has_above)
+    def _():
+        line_block(level, True).start()
+
+    @pl.when(has_below)
+    def _():
+        line_block(level, False).start()
+
     pair_copy(0).start()
 
     def fetch(step):
@@ -1339,19 +1797,24 @@
         )
 
     def work(step):
-        k, odd = lax.div(step, 2), lax.rem(step, 2)
+        paired, k = turn_of(step)
         sample = sample_of(step)
 
-        @pl.when(odd == 1)
+        @pl.when(paired)
         def _():
             block = grads_ref.at[sample]
             remote(block, block, pair_send.at[k], pair_recv.at[k], (partner, col)).wait_recv()
 
-        @pl.when((odd == 0) & (k > 0))
+        direct = jnp.logical_not(paired) & (step > 0)
+
+        @pl.when(direct & (k <= 2 * reach) & (lax.rem(k, 2) == 1))
         def _():
-            block = grads_ref.at[sample]
-            remote(block, block, level_send.at[k], level_recv.at[k], (partner, col)).wait_recv()
-            pair_copy(k).start()
+            relay(k)
+            relay(k + 1)
+
+        @pl.when(direct & (k > 2 * reach))
+        def _():
+            relay(k)
 
         load = pltpu.make_async_copy(
             grads_ref.at[sample], padded_grad.at[1, centre, :], load_sem
@@ -1464,6 +1927,10 @@
     lax.fori_loop(1, count, sums_arrive, 0)
 
     def step_body(step):
+        @pl.when(step == count - 2)
+        def _():
+            lax.fori_loop(1, groups, lambda k, c: (attention_copy(k).start(), c)[1], 0)
+
         @pl.when(step < count)
         def _():
             work(step)
@@ -1497,16 +1964,31 @@
         return carry
 
     lax.fori_loop(1, count, owner_arrives, 0)
+    lax.fori_loop(1, groups, lambda k, c: (attention_copy(k).wait(), c)[1], 0)
+    attention_total = attention_ref[level].astype(floats)
+    for k in range(1, groups):
+        attention_total = attention_total + attention_in[k].astype(floats)
+    attention_sum_ref[...] = attention_total.astype(halves)
     for step in (count - 2, count - 1):
         pixel_copy(step).wait_send()
         line_copy(step).wait_send()
         owner_copy(step).wait_send()
-    lax.fori_loop(1, groups, lambda k, c: (level_copy(k).wait_send(), c)[1], 0)
+
+    def sent(origin):
+        @pl.when((origin <= level) & has_above)
+        def _():
+            line_block(origin, True).wait_send()
+
+        @pl.when((origin >= level) & has_below)
+        def _():
+            line_block(origin, False).wait_send()
+
+    loop(groups, sent)
     loop(groups, lambda k: pair_copy(k).wait_send())
     lax.fori_loop(1, count, lambda k, c: (sums_copy(k).wait_send(), c)[1], 0)
 
 
-def conv_backward(images_all, kernels, bank, styles, inverse, grad, conv, width):
+def conv_backward(images_all, kernels, bank, styles, inverse, grad, conv, attention, width):
     count, tokens, depth = images_all.shape
     channels = grad.shape[1]
     rows = tokens // PIX
@@ -1517,11 +1999,12 @@
         out_shape=(
             jax.ShapeDtypeStruct((2, 9, depth, channels), floats),
             jax.ShapeDtypeStruct((count, 8, 128), floats),
+            jax.ShapeDtypeStruct(attention.shape[1:], halves),
             jax.ShapeDtypeStruct((count,) + piece, halves),
             jax.ShapeDtypeStruct((count, tokens, channels), halves),
         ),
-        in_specs=[ANY] + [VMEM] * 6,
-        out_specs=(VMEM, VMEM, ANY, ANY),
+        in_specs=[ANY] + [VMEM] * 7,
+        out_specs=(VMEM, VMEM, VMEM, ANY, ANY),
         scratch_shapes=[
             pltpu.VMEM((2, tokens, depth), halves),
             pltpu.VMEM((3, tokens + 2 * width, depth), halves),
@@ -1537,11 +2020,13 @@
             pltpu.VMEM((2,) + piece, halves),
             pltpu.VMEM((count,) + piece, halves),
             pltpu.VMEM((2,) + piece, halves),
+            pltpu.VMEM(attention.shape, halves),
             DMA,
             DMA((2,)),
             DMA,
             DMA((count,)),
             DMA((count,)),
+            DMA((groups,)),
             DMA((groups,)),
             DMA((groups,)),
             DMA((groups,)),
@@ -1552,22 +2037,36 @@
             DMA((count,)),
             DMA((count,)),
             DMA((count,)),
+            DMA((groups,)),
+            DMA((groups,)),
         ],
         compiler_params=params(4),
         name="conv_backward",
-    )(images_all, kernels, bank, styles, inverse, grad, conv)
-
-
-def small_kernel(
+    )(images_all, kernels, bank, styles, inverse, grad, conv, attention)
+
+
+def close_kernel(
     count,
     small_ref,
     last_ref,
     stats_ref,
+    attention_ref,
+    others_ref,
     rows_ref,
     stats_all_ref,
+    grad_query_ref,
+    grad_key_ref,
+    grad_value_ref,
+    grad_out_ref,
+    grad_cross_query_ref,
+    grad_cross_out_ref,
+    grad_text_key_ref,
+    grad_text_value_ref,
     rows_out,
     rows_in,
     stats_in,
+    attention_in,
+    others_in,
     rows_send,
     rows_recv,
     stats_send,
@@ -1576,6 +2075,8 @@
     far_rows_recv,
     far_stats_send,
     far_stats_recv,
+    weight_send,
+    weight_recv,
 ):
     row, col = lax.axis_index("dp"), lax.axis_index("pix")
     near, far, cross = peers(col)
@@ -1597,6 +2098,27 @@
     for turn in range(3):
         rows_copy(turn).start()
         stats_copy(turn).start()
+    attention_in[col] = attention_ref[...]
+    others_in[col] = others_ref[...]
+    buffers = (attention_in, others_in)
+
+    def weight_copy(which, hop):
+        block = buffers[which].at[far if hop == 2 else col]
+        index = 3 * which + hop
+        return remote(
+            block, block, weight_send.at[index], weight_recv.at[index], (row, far if hop == 0 else near)
+        )
+
+    def weight_arrives(which, hop):
+        block = buffers[which].at[(far, near, cross)[hop]]
+        index = 3 * which + hop
+        remote(
+            block, block, weight_send.at[index], weight_recv.at[index], (row, near)
+        ).wait_recv()
+
+    for which in range(2):
+        weight_copy(which, 0).start()
+        weight_copy(which, 1).start()
     for turn in range(3):
         rows_copy(turn).wait()
         stats_copy(turn).wait()
@@ -1628,6 +2150,27 @@
         )
 
     lax.fori_loop(1, count, lambda k, c: (far_rows(k).start(), far_stats(k).start(), c)[2], 0)
+    for which in range(2):
+        weight_arrives(which, 0)
+        weight_copy(which, 2).start()
+    width = attention_ref.shape[1] // 5
+    short = grad_text_key_ref.shape[0]
+    for which in range(2):
+        weight_arrives(which, 1)
+        weight_arrives(which, 2)
+    attention_outs = (
+        grad_query_ref,
+        grad_key_ref,
+        grad_value_ref,
+        grad_text_key_ref,
+        grad_text_value_ref,
+    )
+    other_outs = (grad_out_ref, grad_cross_query_ref, grad_cross_out_ref)
+    for buffer, outs in ((attention_in, attention_outs), (others_in, other_outs)):
+        for k, out in enumerate(outs):
+            for p in range(PIX):
+                block = buffer[p, :, k * width : (k + 1) * width].astype(floats)
+                out[:, p * width : (p + 1) * width] = block[: out.shape[0]]
 
     def arrive(k, carry):
         origin = lax.rem(row - k + count, count)
@@ -1641,23 +2184,33 @@
     lax.fori_loop(
         1, count, lambda k, c: (far_rows(k).wait_send(), far_stats(k).wait_send(), c)[2], 0
     )
-
-
-def small_sums(small, last, stats):
+    for which in range(2):
+        for hop in range(3):
+            weight_copy(which, hop).wait_send()
+
+
+def close(small, last, stats, attention, others, text_rows):
     count = stats.shape[0]
     block = small.shape
+    owned, full = attention.shape[0], small.shape[1]
+    weight = jax.ShapeDtypeStruct((owned, full), floats)
+    text = jax.ShapeDtypeStruct((text_rows, full), floats)
     return pl.pallas_call(
-        partial(small_kernel, count),
+        partial(close_kernel, count),
         out_shape=(
             jax.ShapeDtypeStruct((count,) + block, floats),
             jax.ShapeDtypeStruct((count,) + stats.shape, floats),
-        ),
-        in_specs=[VMEM] * 3,
-        out_specs=(VMEM,) * 2,
+        )
+        + (weight,) * 6
+        + (text,) * 2,
+        in_specs=[VMEM] * 5,
+        out_specs=(VMEM,) * 10,
         scratch_shapes=[
             pltpu.VMEM(block, floats),
             pltpu.VMEM((4,) + block, floats),
             pltpu.VMEM((4,) + stats.shape, floats),
+            pltpu.VMEM((PIX,) + attention.shape, halves),
+            pltpu.VMEM((PIX,) + others.shape, halves),
             DMA((3,)),
             DMA((3,)),
             DMA((3,)),
@@ -1666,10 +2219,12 @@
             DMA((count,)),
             DMA((count,)),
             DMA((count,)),
+            DMA((6,)),
+            DMA((6,)),
         ],
         compiler_params=params(5),
-        name="small_sums",
-    )(small, last, stats)
+        name="close",
+    )(small, last, stats, attention, others)
 
 
 def style_rows(style_codes, labels, class_table, select_weight, modulation, rgb_modulation):
@@ -1732,10 +2287,12 @@
             [lax.dynamic_slice_in_dim(w, col * quarter, quarter, axis=1) for w in weights], axis=1
         )
 
-    attention = lax.all_gather(my_columns(w_query, w_key, w_value), "dp", axis=0, tiled=True)
-    text_weights = lax.all_gather(my_columns(c_key, c_value), "dp", axis=0, tiled=True)
-    others = lax.all_gather(my_columns(w_out, c_query, c_out), "dp", axis=0, tiled=True)
-    others = lax.all_gather(others, "pix", axis=0)
+    owned, text_owned = w_query.shape[0], c_key.shape[0]
+    text_columns = jnp.pad(my_columns(c_key, c_value), ((0, owned - text_owned), (0, 0)))
+    attention = jnp.concatenate([my_columns(w_query, w_key, w_value), text_columns], axis=1)
+    attention = lax.all_gather(attention, "dp", axis=0, tiled=True)
+    others = lax.all_gather(my_columns(w_out, c_query, c_out), ("pix", "dp"), axis=0, tiled=True)
+    others = others.reshape(PIX, channels, 3 * quarter)
 
     styled, mixing, scaling, rgb_scale = style_rows(
         style_codes, labels, class_table, select_weight, modulation, rgb_modulation
@@ -1746,7 +2303,9 @@
     bank_turned = bank.transpose(0, 1, 3, 2)
     words = token_ids.shape[1]
     text = jnp.take(text_table, token_ids[0], axis=0)
-    text_padded = jnp.pad(text, ((0, 128 - words), (0, 0)))
+    text = text.reshape(words, count, text_owned)
+    text = jnp.pad(text, ((0, 128 - words), (0, 0), (0, owned - text_owned)))
+    text = text.reshape(128, channels)
 
     images_all, kernels, styles, inverse = gather_inputs(
         pack_style(styled, labels, mixing, scaling, count), bank, parts
@@ -1754,11 +2313,21 @@
     images_all = images_all.reshape(count, PIX * rows, depth)
     conv, conv_own, hidden_one, normed_one = conv_forward(images_all, kernels, own, gain_self, width)
     query, key, value, totals, attended, text_all = attend_forward(
-        normed_one, attention, text_padded, text_weights
+        normed_one, attention, text
     )
     rgb_rows = jnp.pad(rgb_cotangent.reshape(3, rows).T, ((0, 0), (0, 125)))
     penalty = jnp.broadcast_to(penalty_mask.astype(floats).reshape(1, 1), (1, 128))
-    output, rgb, other_grads, text_grads, grad_two, grad_attended, small = cross_part(
+    (
+        output,
+        rgb,
+        reduced,
+        text_grads,
+        grad_two,
+        grad_attended,
+        small,
+        attended_rows,
+        grad_attn,
+    ) = cross_part(
         words,
         attended,
         hidden_one,
@@ -1771,19 +2340,8 @@
         rgb_rows,
         penalty,
     )
-    other_owned = lax.psum_scatter(
-        lax.psum_scatter(other_grads, "pix", scatter_dimension=0, tiled=False),
-        "dp",
-        scatter_dimension=0,
-        tiled=True,
-    )
-    text_cols = lax.psum_scatter(text_grads, "pix", scatter_dimension=0, tiled=False)
-    text_grad = lax.dot_general(
-        text.astype(floats), text_cols[:words], TN, precision=highest, preferred_element_type=floats
-    ).astype(halves)
-    text_owned = lax.psum_scatter(text_grad, "dp", scatter_dimension=0, tiled=True)
-
-    attention_grads, grad_one, grad_conv, last = attend_backward(
+    attention_grads, others_owned, grad_one, grad_conv, last = attend_backward(
+        words,
         grad_attended,
         query,
         key,
@@ -1795,20 +2353,14 @@
         conv,
         grad_two,
         gain_self,
+        text,
+        text_grads,
+        reduced.reshape(count // 2, 2, owned, 2 * quarter),
+        attended_rows,
+        grad_attn,
     )
-    attention_owned = lax.psum_scatter(attention_grads, "dp", scatter_dimension=0, tiled=True)
-
-    def whole(owned):
-        full = lax.all_gather(owned, "pix", axis=0).astype(floats)
-        pieces = owned.shape[1] // quarter
-        full = full.reshape(PIX, owned.shape[0], pieces, quarter).transpose(2, 1, 0, 3)
-        return full.reshape(pieces, owned.shape[0], channels)
-
-    grad_w_query, grad_w_key, grad_w_value = whole(attention_owned)
-    grad_w_out, grad_c_query, grad_c_out = whole(other_owned)
-    grad_c_key, grad_c_value = whole(text_owned)
-
-    bank_grad, stats, image_parts, _ = conv_backward(
+
+    bank_grad, stats, attention_owned, image_parts, _ = conv_backward(
         images_all,
         kernels,
         bank_turned,
@@ -1816,10 +2368,22 @@
         inverse,
         grad_conv.reshape(PIX * rows, quarter),
         conv_own,
+        attention_grads,
         width,
     )
     grad_image = grad_one + image_parts.transpose(1, 0, 2).reshape(rows, channels).astype(floats)
-    all_rows, all_stats = small_sums(small, last, stats)
+    (
+        all_rows,
+        all_stats,
+        grad_w_query,
+        grad_w_key,
+        grad_w_value,
+        grad_w_out,
+        grad_c_query,
+        grad_c_out,
+        grad_c_key,
+        grad_c_value,
+    ) = close(small, last, stats, attention_owned, others_owned, text_owned)
 
     styled_all = styles[:, 3:7, :].reshape(count, -1)
     mixing_all = styles[:, 1:3, 0]

time: 643 us -> 507 us (0.79)
  waiting for transfers between devices: 70 us -> 0.06 us
  blocking collectives: 58.9 us -> 0 us
  local copies, waits for them, and re-layouts: 45.3 us -> 28.9 us
  Pallas kernels: 418 us -> 432 us
    all_gather x4 -> x0, blocking collectives: 58.9 us -> none  [the longest x1 35.4 us: on_device(): lax.all_gather(my_columns(c_key, c_value), 'dp', axis=0, tiled=True)]
    all_gather x3 -> x2, waiting for transfers between devices: 45.4 us -> 0.02 us  [the longest x1 0.02 us: on_device(): lax.all_gather(my_columns(w_out, c_query, c_out), ('pix', 'dp'), axis=0,...]
    pallas_call x1, Pallas kernels: 146 us -> 103 us  [conv_backward(): pl.pallas_call(partial(conv_back_kernel, count, width), out_shape=(jax.Sh...]
    pallas_call x2, Pallas kernels: 88.1 us -> 115 us  [the longest x1 92 us: attend_backward(): pl.pallas_call(attend_back_kernel, out_shape=(jax.ShapeDtypeStruct((group...]
    reduce_scatter x5 -> x0, waiting for transfers between devices: 24 us -> none  [the longest x1 23.9 us: on_device(): lax.psum_scatter(lax.psum_scatter(other_grads, 'pix', scatter_dimension=0...]
    pallas_call x1, Pallas kernels: 38.3 us -> 57.3 us  [cross_part(): pl.pallas_call(partial(cross_kernel, words), out_shape=(jax.ShapeDtypeStr...]
    another operation x11 -> x0, local copies, waits for them, and re-layouts: 7.11 us -> none  [the longest x4 4.99 us: on_device(): grad_w_out, grad_c_query, grad_c_out = whole(other_owned)]
    pallas_call x1, Pallas kernels: 95 us -> 102 us  [conv_forward(): pl.pallas_call(partial(conv_kernel, count, width), out_shape=(jax.ShapeDt...]
  transfers between devices with their start and end apart: 8 -> 2, of which waited for: 2 -> 0; matrix products, arithmetic and copies ran while one was open for 9% -> 4% of each run, Pallas kernels for 60% -> 31%
where the time goes in v2:
time: 507 us; the launch traced here: 502 us
  Pallas kernels  432 us (85%)
  local copies, waits for them, and re-layouts  28.9 us (6%)
  between operations  15.7 us (3%)
  matrix products  13.2 us (3%)
  other arithmetic  12 us (2%)
    pallas_call x1, Pallas kernels, conv_backward(): pl.pallas_call(partial(conv_back_kernel, count, width), out_shape=(jax.Sh...  103 us
    pallas_call x1, Pallas kernels, conv_forward(): pl.pallas_call(partial(conv_kernel, count, width), out_shape=(jax.ShapeDt...  102 us
    pallas_call x1, Pallas kernels, attend_backward(): pl.pallas_call(attend_back_kernel, out_shape=(jax.ShapeDtypeStruct((group...  92 us
    pallas_call x1, Pallas kernels, cross_part(): pl.pallas_call(partial(cross_kernel, words), out_shape=(jax.ShapeDtypeStr...  57.3 us
    pallas_call x1, Pallas kernels, gather_inputs(): pl.pallas_call(partial(gather_kernel, count), out_shape=(jax.ShapeDtypeSt...  32.8 us
    pallas_call x1, Pallas kernels, close(): pl.pallas_call(partial(close_kernel, count), out_shape=(jax.ShapeDtypeStr...  23.3 us
    pallas_call x1, Pallas kernels, attend_forward(): pl.pallas_call(attend_kernel, out_shape=(flat, flat, flat, jax.ShapeDtype...  22.3 us
    unnamed x61, local copies, waits for them, and re-layouts  12.2 us
  transfers between devices with their start and end apart: 2, of which 0 were waited for; matrix products, arithmetic and copies ran while one was open for 4% of the time, Pallas kernels for 31%

profile of v2, /device:TPU:0, one launch (start us, length us, event | category | flops | bytes accessed | tf_op | source)
XLA Modules:
  0.0 502.1 jit_solution(7507986032135384379)
XLA Ops:
  7.3 1.0 constant_dynamic-slice_fusion.9
  15.4 1.2 fusion.31
  16.6 1.3 broadcast_divide_fusion
  19.1 3.5 gather_fusion
  25.5 1.4 copy.77
  28.2 32.8 %gather_inputs.1 = (bf16[8,4,256,128]{3,2,1,0:T(8,128)(2,1)}, bf16[8,9,128,256]{3,2,1,0:T(8,128)(2,1)}, f32[8,8,128]{2,1,0:T(8,128)}, f32[8,256]{1,0:T(8,128)}) custom-call(f32[8,8,128]{2,1,0:T(8,128)} %pad_maximum_fusion.2.style_ref, bf16[2,9,128,256]{3,2,1,0:T(8,128)(2,1)} %bitcast.106, bf16[8,256,128]{2,1,0:T(8,128)(2,1)} %bitcast.113), custom_call_target="tpu_custom_call" | custom-call | tf_op jit(solution)/shard_map/gather_inputs/pallas_call | solution.py:258
  62.6 101.9 %conv_forward.1 = (bf16[256,1024]{1,0:T(8,128)(2,1)}, bf16[1024,256]{1,0:T(8,128)(2,1)}, f32[256,1024]{1,0:T(8,128)}, bf16[4,256,1024]{2,1,0:T(8,128)(2,1)}) custom-call(bf16[8,1024,128]{2,1,0:T(8,128)(2,1)} %bitcast.102, bf16[8,9,128,256]{3,2,1,0:T(8,128)(2,1)} %get-tuple-element.63.kernel_ref, bf16[256,1024]{1,0:T(8,128)(2,1)} %bitcast.111, ...), custom_call_target="tpu_custom_call" | custom-call | tf_op jit(solution)/shard_map/conv_forward/pallas_call | solution.py:566
  165.9 22.3 %attend_forward.1 = (bf16[1024,256]{1,0:T(8,128)(2,1)}, bf16[1024,256]{1,0:T(8,128)(2,1)}, bf16[1024,256]{1,0:T(8,128)(2,1)}, f32[1024,128]{1,0:T(8,128)}, bf16[...) custom-call(bf16[4,256,1024]{2,1,0:T(8,128)(2,1)} %get-tuple-element.64.normed_ref, ...), custom_call_target="tpu_custom_call" | custom-call | tf_op jit(solution)/shard_map/attend_forward/pallas_call | solution.py:736
  188.7 57.3 %cross_part.1 = (f32[256,1024]{1,0:T(8,128)}, f32[256,128]{1,0:T(8,128)}, bf16[1024,512]{1,0:T(8,128)(2,1)}, bf16[4,128,512]{2,1,0:T(8,128)(2,1)}, f32[256,1024]...) custom-call(bf16[4,256,256]{2,1,0:T(8,128)(2,1)} %get-tuple-element., ...), custom_call_target="tpu_custom_call" | custom-call | tf_op jit(solution)/shard_map/cross_part/pallas_call | solution.py:1012
  246.1 92.0 %attend_backward.1 = (bf16[4,128,1280]{2,1,0:T(8,128)(2,1)}, bf16[128,768]{1,0:T(8,128)(2,1)}, f32[256,1024]{1,0:T(8,128)}, bf16[4,256,256]{2,1,0:T(8,128)(2,1)}, f32[8,1024]{1,0:T(8,128)}) custom-call(bf16[4,256,256]{2,1,0:T(8,128)(2,1)} %get-tuple-element.70.grad_ref, bf16[1024,256]{1,0:T(8,128)(2,1)} %get-tuple-element.71.query_ref, ...), custom_call_target="tpu_custom_call" | custom-call | tf_op jit(solution)/shard_map/attend_backward/pallas_call | solution.py:1506
  338.0 102.7 %conv_backward.1 = (f32[2,9,128,256]{3,2,1,0:T(8,128)}, f32[8,8,128]{2,1,0:T(8,128)}, bf16[128,1280]{1,0:T(8,128)(2,1)}, bf16[8,256,128]{2,1,0:T(8,128)(2,1)}, bf16[8,1024,256]{2,1,0:T(8,128)(2,1)}) custom-call(bf16[8,1024,128]{2,1,0:T(8,128)(2,1)} %bitcast.103, bf16[8,9,128,256]{3,2,1,0:T(8,128)(2,1)} %get-tuple-element.63.kernel_ref, ...), custom_call_target="tpu_custom_call" | custom-call | tf_op jit(solution)/shard_map/conv_backward/pallas_call | solution.py:1997
  440.7 23.3 %close.1 = (f32[8,8,1024]{2,1,0:T(8,128)}, f32[8,8,8,128]{3,2,1,0:T(8,128)}, f32[128,1024]{1,0:T(8,128)}, f32[128,1024]{1,0:T(8,128)}, f32[128,1024]{1,0:T(8,128...) custom-call(f32[8,1024]{1,0:T(8,128)} %get-tuple-element.88.small_re, ...), custom_call_target="tpu_custom_call" | custom-call | tf_op jit(solution)/shard_map/close/pallas_call | solution.py:2198
  464.0 1.0 slice.33
  464.9 1.1 slice_reduce_fusion
  466.0 1.0 slice.34
  467.0 1.0 reduce_sum.42
  469.2 3.2 fusion.3
  472.3 3.2 fusion.10
  477.6 0.9 convolution_add_fusion.1
  478.5 0.9 convolution_add_fusion
  479.5 2.4 fusion.6
  484.1 2.5 add.77
  486.6 1.0 copy.135
  487.6 1.4 copy.136
  (108 shorter events, 26.4 us)
Async XLA Ops:
  7.2 19.8 %copy-start = (bf16[512,1024]{1,0:T(8,128)(2,1)S(1)}, bf16[512,1024]{1,0:T(8,128)(2,1)}, u32[]{:S(2)}) copy-start(bf16[512,1024]{1,0:T(8,128)(2,1)} %param.33) | copy-start | bytes 3145732
  7.2 6.7 %copy-start.19 = (bf16[1,512]{1,0:T(2,128)(2,1)S(1)}, bf16[1,512]{1,0:T(2,128)(2,1)}, u32[]{:S(2)}) copy-start(bf16[1,512]{1,0:T(2,128)(2,1)} %param.25) | copy-start | bytes 3076
  7.2 7.4 %copy-start.20 = (bf16[512,2]{0,1:T(2,128)(2,1)S(1)}, bf16[512,2]{0,1:T(2,128)(2,1)}, u32[]{:S(2)}) copy-start(bf16[512,2]{0,1:T(2,128)(2,1)} %param.32) | copy-start | bytes 6148
  7.2 10.8 %copy-start.4 = (bf16[1,8,32,1024]{3,2,1,0:T(8,128)(2,1)S(1)}, bf16[1,8,32,1024]{3,2,1,0:T(8,128)(2,1)}, u32[]{:S(2)}) copy-start(bf16[1,8,32,1024]{3,2,1,0:T(8,128)(2,1)} %param.24) | copy-start | bytes 1572868
  7.2 158.6 %all-gather.3.cloned.1.call-start = ((), (), s32[]{:S(2)}) async-start(), calls=%async_computation | async-start | bytes 2949120 | tf_op jit(solution)/shard_map/all_gather | solution.py:2293
  10.0 9.1 %copy-start.21 = (s32[1,77]{1,0:T(1,128)S(1)}, s32[1,77]{1,0:T(1,128)}, u32[]{:S(2)}) copy-start(s32[1,77]{1,0:T(1,128)} %param.27) | copy-start | bytes 928
  10.8 177.4 %all-gather.5.cloned.1.call-start = ((), (), s32[]{:S(2)}) async-start(), calls=%async_computation.1 | async-start | bytes 6488064 | tf_op jit(solution)/shard_map/all_gather | solution.py:2294
  18.1 5.6 %copy-start.18 = (bf16[1024,3]{0,1:T(4,128)(2,1)S(1)}, bf16[1024,3]{0,1:T(4,128)(2,1)}, u32[]{:S(2)}) copy-start(bf16[1024,3]{0,1:T(4,128)(2,1)} %param.45) | copy-start | bytes 18436
  18.1 6.6 %copy-start.17 = (f32[1,3,8,32]{3,2,1,0:T(8,128)S(1)}, f32[1,3,8,32]{3,2,1,0:T(8,128)}, u32[]{:S(2)}) copy-start(f32[1,3,8,32]{3,2,1,0:T(8,128)} %param.47) | copy-start | bytes 9220
  18.1 7.4 %copy-start.1 = (bf16[2,3,3,128,256]{4,3,2,1,0:T(8,128)(2,1)S(1)}, bf16[2,3,3,128,256]{4,3,2,1,0:T(8,128)(2,1)}, u32[]{:S(2)}) copy-start(bf16[2,3,3,128,256]{4,3,2,1,0:T(8,128)(2,1)} %param.31) | copy-start | bytes 3538948
  62.6 101.9 %copy-start.15 = (f32[8,8,128]{2,1,0:T(8,128)S(1)}, f32[8,8,128]{2,1,0:T(8,128)}, u32[]{:S(2)}) copy-start(f32[8,8,128]{2,1,0:T(8,128)} %get-tuple-element.82.styles_ref) | copy-start | bytes 98308
  62.6 102.2 %copy-start.2 = (bf16[512,1024]{1,0:T(8,128)(2,1)S(1)}, bf16[512,1024]{1,0:T(8,128)(2,1)}, u32[]{:S(2)}) copy-start(bf16[512,1024]{1,0:T(8,128)(2,1)} %param.34) | copy-start | bytes 3145732
  477.6 4.8 copy-start.6
  482.5 0.9 copy-start.16
  483.2 3.4 copy-start.5
  484.1 3.5 copy-start.3
  487.6 1.4 copy-start.12
  487.6 2.2 copy-start.11
  489.0 1.6 copy-start.10
  489.0 2.4 copy-start.9
  489.0 3.2 copy-start.8
  489.8 3.2 copy-start.14
  490.6 3.1 copy-start.13
  491.4 3.1 copy-start.7
Sparse Core Ops, SparseCore 0:
  10.9 61.4 all-gather.2
  75.9 80.1 all-gather.4

commit v3 on v2

--- a/solution.py
+++ b/solution.py
@@ -626,6 +626,28 @@
     return jnp.dot(a, b, preferred_element_type=floats)
 
 
+def split(value):
+    high = value.astype(halves)
+    rest = value - high.astype(floats)
+    middle = rest.astype(halves)
+    return high, middle, (rest - middle.astype(floats)).astype(halves)
+
+
+def exact(product, left, right):
+    count = left.shape[0]
+    found = product(jnp.concatenate(split(left), axis=0), right)
+    return found[2 * count :] + found[count : 2 * count] + found[:count]
+
+
+def outer_sum(left, right):
+    lefts, rights = split(left), split(right)
+    pairs = ((0, 2), (2, 0), (1, 1), (0, 1), (1, 0), (0, 0))
+    return mul_tn(
+        jnp.concatenate([lefts[i] for i, _ in pairs], axis=0),
+        jnp.concatenate([rights[j] for _, j in pairs], axis=0),
+    )
+
+
 def attend_kernel(
     normed_ref,
     weight_ref,
@@ -779,8 +801,9 @@
     small_ref,
     attended,
     grad_attn,
+    normed,
+    grad_query,
     two,
-    normed,
     query,
     probs,
     crossed,
@@ -788,7 +811,6 @@
     grad_three,
     grad_proj,
     grad_crossed,
-    grad_query,
     grad_norm,
     near_out,
     near_in,
@@ -910,7 +932,11 @@
             outs.append(mul(prob.astype(halves), values[:, lanes]))
         crossed[:, here] = jnp.concatenate(outs, axis=1).astype(halves)
 
-    loop(full // 128, cross_pair)
+    def cross_four(i):
+        cross_pair(2 * i)
+        cross_pair(2 * i + 1)
+
+    loop(full // 256, cross_four)
     rgb_ref[...] = jnp.zeros_like(rgb_ref)
 
     def out_three(j):
@@ -933,7 +959,7 @@
         grad_proj[:, cols(j)] = grad.astype(halves)
 
     loop(PIX, back_three)
-    start_grad(1, crossed, grad_proj)
+    start_grad(0, crossed, grad_proj)
 
     def times_transposed(source, j, which):
         acc = jnp.zeros((rows, tile), floats)
@@ -967,15 +993,17 @@
         text_grad_ref[group, :, text_lanes(pair, 0)] = jnp.concatenate(grad_k, axis=1).astype(halves)
         text_grad_ref[group, :, text_lanes(pair, 1)] = jnp.concatenate(grad_v, axis=1).astype(halves)
 
-    loop(full // 128, back_pair)
-    pass_grad(1)
-    start_grad(0, normed, grad_query)
+    def back_four(i):
+        back_pair(2 * i)
+        back_pair(2 * i + 1)
+
+    loop(full // 256, back_four)
+    pass_grad(0)
 
     def back_query(j):
         grad_norm[:, cols(j)] = times_transposed(grad_query, j, C_QUERY)
 
     loop(PIX, back_query)
-    pass_grad(0)
     small_ref[0:1, :] = jnp.zeros((1, full), floats)
 
     def back_norm(i):
@@ -997,7 +1025,6 @@
     loop(PIX, back_attended)
 
     small_ref[5:8, :] = jnp.zeros((3, full), floats)
-    end_grad(1)
     end_grad(0)
 
 
@@ -1014,19 +1041,17 @@
         out_shape=(
             jax.ShapeDtypeStruct((rows, full), floats),
             jax.ShapeDtypeStruct((rows, 128), floats),
-            jax.ShapeDtypeStruct((full, 2 * tile), halves),
+            jax.ShapeDtypeStruct((full, tile), halves),
             jax.ShapeDtypeStruct(text.shape, halves),
             jax.ShapeDtypeStruct((rows, full), floats),
             jax.ShapeDtypeStruct((PIX, rows, tile), halves),
             jax.ShapeDtypeStruct((8, full), floats),
-            jax.ShapeDtypeStruct((rows, full), halves),
-            jax.ShapeDtypeStruct((rows, full), halves),
-        ),
+        )
+        + (jax.ShapeDtypeStruct((rows, full), halves),) * 4,
         in_specs=[VMEM] * 10,
-        out_specs=(VMEM,) * 9,
+        out_specs=(VMEM,) * 11,
         scratch_shapes=[
             wide,
-            slim,
             slim,
             pltpu.VMEM((heads, rows, text.shape[1]), floats),
             slim,
@@ -1034,17 +1059,16 @@
             wide,
             slim,
             slim,
-            slim,
             wide,
-            pltpu.VMEM((2, 2, full, tile), halves),
-            pltpu.VMEM((2, 2, full, tile), halves),
-            pltpu.VMEM((2, 2, full, tile), floats),
-            pltpu.VMEM((2, full, tile), halves),
-            pltpu.VMEM((2, full, tile), halves),
-            DMA((2,)),
-            DMA((2,)),
-            DMA((2,)),
-            DMA((2,)),
+            pltpu.VMEM((1, 2, full, tile), halves),
+            pltpu.VMEM((1, 2, full, tile), halves),
+            pltpu.VMEM((1, 2, full, tile), floats),
+            pltpu.VMEM((1, full, tile), halves),
+            pltpu.VMEM((1, full, tile), halves),
+            DMA((1,)),
+            DMA((1,)),
+            DMA((1,)),
+            DMA((1,)),
         ],
         compiler_params=params(6),
         name="cross_part",
@@ -1068,22 +1092,31 @@
     key_ref,
     value_ref,
     total_ref,
-    normed_ref,
-    weight_ref,
-    hidden_ref,
-    conv_ref,
-    grad_two_ref,
+    normed_from,
+    weight_from,
+    hidden_from,
+    conv_from,
+    grad_two_from,
     gain_ref,
     text_ref,
     text_grad_ref,
     reduced_ref,
     attended_ref,
     grad_attn_ref,
+    normed_two_ref,
+    grad_cross_ref,
     attention_ref,
     others_ref,
+    text_owned_ref,
     grad_one_ref,
     grad_conv_ref,
     small_ref,
+    normed_ref,
+    weight_ref,
+    hidden_ref,
+    conv_ref,
+    grad_two_ref,
+    load_sem,
     grads,
     grad_query,
     grad_key,
@@ -1110,8 +1143,14 @@
     out_side_in,
     out_level_out,
     out_level_in,
+    words_grad,
+    words_side_in,
+    words_level_out,
+    words_level_in,
     attention_grad,
     attention_in,
+    attention_out,
+    attention_landed,
     grad_send,
     grad_recv,
     text_send,
@@ -1126,23 +1165,32 @@
     near_recv,
     far_send,
     far_recv,
-    side_send,
-    side_recv,
-    level_send,
-    level_recv,
-    out_side_send,
-    out_side_recv,
-    out_level_send,
-    out_level_recv,
     attention_send,
     attention_recv,
+    landed_send,
+    landed_recv,
+    *reduce_sems,
 ):
     row, col = lax.axis_index("dp"), lax.axis_index("pix")
     near, far, cross = peers(col)
     targets = (far, cross, near)
-    groups, _, owned, _ = attention_grad.shape
+    _, groups, _, owned, _ = attention_grad.shape
     side, level = lax.rem(row, 2), lax.div(row, 2)
     partner = flip(row, 1)
+    loads = [
+        pltpu.make_async_copy(source, buffer, load_sem.at[i])
+        for i, (source, buffer) in enumerate(
+            (
+                (normed_from, normed_ref),
+                (weight_from.at[:, pl.ds(0, weight_ref.shape[1])], weight_ref),
+                (hidden_from, hidden_ref),
+                (conv_from, conv_ref),
+                (grad_two_from, grad_two_ref),
+            )
+        )
+    ]
+    for load in loads:
+        load.start()
     barrier = pltpu.get_barrier_semaphore()
 
     def hello(step, carry):
@@ -1184,108 +1232,192 @@
     for turn in range(3):
         text_copy(turn).start()
 
-    def side_copy():
+    def reduction(which, source, arrived, out, landed):
+        side_send, side_recv, level_send, level_recv = reduce_sems[4 * which : 4 * which + 4]
+
+        def to_side():
+            return remote(source.at[:, 1 - side], arrived, side_send, side_recv, (partner, col))
+
+        def to_level(k):
+            group = lax.rem(level + k, groups)
+            return remote(
+                out.at[group], landed.at[k], level_send.at[k], level_recv.at[k], (2 * group + side, col)
+            )
+
+        def middle():
+            to_side().wait_recv()
+
+            def add(group):
+                out[group] = (
+                    source[group, side].astype(floats) + arrived[group].astype(floats)
+                ).astype(halves)
+
+            loop(groups, add)
+            lax.fori_loop(1, groups, lambda k, c: (to_level(k).start(), c)[1], 0)
+
+        def finish():
+            total = out[level].astype(floats)
+            for k in range(1, groups):
+                to_level(k).wait()
+                total = total + landed[k].astype(floats)
+            to_side().wait_send()
+            return total.astype(halves)
+
+        return to_side, middle, finish
+
+    sides = reduction(0, reduced_ref, side_in, level_out, level_in)
+    outs = reduction(1, out_grad, out_side_in, out_level_out, out_level_in)
+    word = reduction(2, words_grad, words_side_in, words_level_out, words_level_in)
+    sides[0]().start()
+
+    def near_copy(which):
         return remote(
-            reduced_ref.at[:, 1 - side], side_in, side_send, side_recv, (partner, col)
-        )
-
-    def out_side_copy():
+            near_out.at[which], near_in.at[which], near_send.at[which], near_recv.at[which], (row, near)
+        )
+
+    def far_copy(which):
         return remote(
-            out_grad.at[:, 1 - side], out_side_in, out_side_send, out_side_recv, (partner, col)
-        )
-
-    def level_copy(k):
+            far_out.at[which], far_in.at[which], far_send.at[which], far_recv.at[which], (row, far)
+        )
+
+    def row_tile(i):
+        return pl.ds(pl.multiple_of(i * width, width), width)
+
+    lefts, rights = (attended_ref, normed_two_ref), (grad_attn_ref, grad_cross_ref)
+    per_tile = width // (2 * owned)
+    for which in range(2):
+
+        def out_tile(index, first, second, which=which):
+            i, b = lax.div(index, 2), lax.rem(index, 2)
+            right = rights[which][:, row_tile(jnp.where(b == 0, first, second))]
+            return i, b, mul_tn(lefts[which][:, row_tile(i)], right)
+
+        def out_give(index, which=which, out_tile=out_tile):
+            i, b, value = out_tile(index, near, cross)
+            near_out[which, b, row_tile(i), :] = value.astype(halves)
+
+        def out_keep(index, which=which, out_tile=out_tile):
+            i, b, value = out_tile(index, col, far)
+            near_kept[which, b, row_tile(i), :] = value
+
+        loop(2 * PIX, out_give)
+        near_copy(which).start()
+        loop(2 * PIX, out_keep)
+
+    def out_pass():
+        for which in range(2):
+            near_copy(which).wait_recv()
+
+            def add(i, which=which):
+                here = row_tile(i)
+                far_out[which, here, :] = (
+                    near_kept[which, 1, here, :] + near_in[which, 1, here, :].astype(floats)
+                ).astype(halves)
+
+            loop(PIX, add)
+            far_copy(which).start()
+
+    def out_end():
+        for which in range(2):
+            far_copy(which).wait_recv()
+
+            def add(i, which=which):
+                here = row_tile(i)
+                value = (
+                    near_kept[which, 0, here, :]
+                    + near_in[which, 0, here, :].astype(floats)
+                    + far_in[which, here, :].astype(floats)
+                ).astype(halves)
+                out_grad[pl.ds(i * per_tile, per_tile), :, :, which * width : (which + 1) * width] = (
+                    value.reshape(per_tile, 2, owned, width)
+                )
+
+            loop(PIX, add)
+        outs[0]().start()
+
+    def words_grads():
+        text_total = text_grad_ref[col, 0:used, :].astype(floats)
+        for turn in range(3):
+            text_copy(turn).wait_recv()
+            text_total = text_total + text_in[turn].astype(floats)
+        text_total = jnp.concatenate(
+            [text_total, jnp.zeros((text_ref.shape[0] - used, 2 * width), floats)], axis=0
+        )
+
+        def put(j):
+            for k in range(2):
+                right = text_total[:, k * width : (k + 1) * width]
+                value = mul_tn(text_ref[:, row_tile(j)].astype(floats), right, highest)
+                words_grad[pl.ds(j * per_tile, per_tile), :, :, k * width : (k + 1) * width] = (
+                    value.astype(halves).reshape(per_tile, 2, owned, width)
+                )
+
+        loop(full // width, put)
+        word[0]().start()
+
+    def attention_copy(part, j):
+        here = pl.ds(j * per_tile, per_tile)
+        return remote(
+            attention_grad.at[part, here, 1 - side],
+            attention_in.at[part, here],
+            attention_send.at[part, j],
+            attention_recv.at[part, j],
+            (partner, col),
+        )
+
+    def weight_grads(part):
+        lanes = slice(part * 128, (part + 1) * 128)
+
+        def tile(j):
+            here = pl.ds(j * per_tile, per_tile)
+            for k, right in enumerate((grad_query, grad_key, grad_value)):
+                acc = jnp.zeros((width, 128), floats)
+                for i in range(PIX):
+                    acc = acc + mul_tn(
+                        normed_ref[i, :, row_tile(j)], right[i * rows : (i + 1) * rows, lanes]
+                    )
+                attention_grad[part, here, :, :, k * 128 : (k + 1) * 128] = acc.astype(
+                    halves
+                ).reshape(per_tile, 2, owned, 128)
+            attention_copy(part, j).start()
+
+        loop(full // width, tile)
+
+    def landed_copy(k):
         group = lax.rem(level + k, groups)
         return remote(
-            level_out.at[group], level_in.at[k], level_send.at[k], level_recv.at[k], (2 * group + side, col)
-        )
-
-    def out_level_copy(k):
-        group = lax.rem(level + k, groups)
-        return remote(
-            out_level_out.at[group],
-            out_level_in.at[k],
-            out_level_send.at[k],
-            out_level_recv.at[k],
+            attention_out.at[group],
+            attention_landed.at[k],
+            landed_send.at[k],
+            landed_recv.at[k],
             (2 * group + side, col),
         )
 
-    def level_sum(copy, source, arrived, out):
-        copy().wait_recv()
-
-        def add(group):
-            out[group] = (source[group, side].astype(floats) + arrived[group].astype(floats)).astype(
-                halves
-            )
-
-        loop(groups, add)
-
-    side_copy().start()
-
-    def near_copy():
-        return remote(near_out, near_in, near_send, near_recv, (row, near))
-
-    def far_copy():
-        return remote(far_out, far_in, far_send, far_recv, (row, far))
-
-    def row_tile(i):
-        return pl.ds(pl.multiple_of(i * width, width), width)
-
-    def out_tile(index, first, second):
-        i, b = lax.div(index, 2), lax.rem(index, 2)
-        right = grad_attn_ref[:, row_tile(jnp.where(b == 0, first, second))]
-        return i, b, mul_tn(attended_ref[:, row_tile(i)], right)
-
-    def out_give(index):
-        i, b, value = out_tile(index, near, cross)
-        near_out[b, row_tile(i), :] = value.astype(halves)
-
-    def out_keep(index):
-        i, b, value = out_tile(index, col, far)
-        near_kept[b, row_tile(i), :] = value
-
-    loop(2 * PIX, out_give)
-    near_copy().start()
-    loop(2 * PIX, out_keep)
-    per_tile = width // (2 * owned)
-
-    def out_pass():
-        near_copy().wait_recv()
-
-        def add(i):
-            here = row_tile(i)
-            far_out[here, :] = (
-                near_kept[1, here, :] + near_in[1, here, :].astype(floats)
+    def attention_sum(part, out):
+        def add(j):
+            attention_copy(part, j).wait_recv()
+            here = pl.ds(j * per_tile, per_tile)
+            out[here] = (
+                attention_grad[part, here, side].astype(floats)
+                + attention_in[part, here].astype(floats)
             ).astype(halves)
 
-        loop(PIX, add)
-        far_copy().start()
-
-    def out_end():
-        far_copy().wait_recv()
-
-        def add(i):
-            here = row_tile(i)
-            value = (
-                near_kept[0, here, :]
-                + near_in[0, here, :].astype(floats)
-                + far_in[here, :].astype(floats)
-            ).astype(halves)
-            out_grad[pl.ds(i * per_tile, per_tile)] = value.reshape(per_tile, 2, owned, width)
-
-        loop(PIX, add)
-        out_side_copy().start()
+        loop(full // width, add)
+
+    def attention_level():
+        attention_sum(0, attention_out)
+        lax.fori_loop(1, groups, lambda k, c: (landed_copy(k).start(), c)[1], 0)
 
     def between(h):
         if h == 0:
-            out_pass()
-            level_sum(side_copy, reduced_ref, side_in, level_out)
-            lax.fori_loop(1, groups, lambda k, c: (level_copy(k).start(), c)[1], 0)
+            words_grads()
+            sides[1]()
         if h == 1:
-            out_end()
+            for load in loads:
+                load.wait()
+            weight_grads(0)
         if h == 2:
-            level_sum(out_side_copy, out_grad, out_side_in, out_level_out)
-            lax.fori_loop(1, groups, lambda k, c: (out_level_copy(k).start(), c)[1], 0)
+            word[1]()
 
     grads[col] = grad_ref[col]
     totals[...] = jnp.transpose(total_ref[...])
@@ -1297,6 +1429,7 @@
             grad_recv.at[turn],
             (row, near),
         ).wait_recv()
+    out_pass()
     ones = jnp.ones((rows, HEAD_DIM), halves)
     for h in range(heads):
         lanes = slice(h * HEAD_DIM, (h + 1) * HEAD_DIM)
@@ -1350,14 +1483,21 @@
 
         norm_grad(target, store)
         pair_copy(turn).start()
-    line = remote(line_out, line_in, line_send, line_recv, (row, far))
+    half = rows // 2
+
+    def line_copy(i):
+        here = pl.ds(i * half, half)
+        return remote(
+            line_out.at[here], line_in.at[here], line_send.at[i], line_recv.at[i], (row, far)
+        )
 
     def store_far(cols, value):
         line_out[:, cols] = (value + pair_in[0, :, cols].astype(floats)).astype(halves)
 
     pair_copy(0).wait_recv()
     norm_grad(far, store_far)
-    line.start()
+    line_copy(0).start()
+    line_copy(1).start()
 
     def store_own(cols, value):
         own[:, cols] = value + pair_in[1, :, cols].astype(floats)
@@ -1365,45 +1505,10 @@
     pair_copy(1).wait_recv()
     norm_grad(col, store_own)
 
-    text_total = text_grad_ref[col, 0:used, :].astype(floats)
-    for turn in range(3):
-        text_copy(turn).wait_recv()
-        text_total = text_total + text_in[turn].astype(floats)
-    text_total = jnp.concatenate(
-        [text_total, jnp.zeros((text_ref.shape[0] - used, 2 * width), floats)], axis=0
-    )
-
-    def attention_copy(j):
-        here = pl.ds(j * per_tile, per_tile)
-        return remote(
-            attention_grad.at[here, 1 - side],
-            attention_in.at[here],
-            attention_send.at[j],
-            attention_recv.at[j],
-            (partner, col),
-        )
-
-    def weight_grads(j):
-        cols = row_tile(j)
-        here = pl.ds(j * per_tile, per_tile)
-
-        def put(k, value):
-            attention_grad[here, :, :, k * width : (k + 1) * width] = value.astype(halves).reshape(
-                per_tile, 2, owned, width
-            )
-
-        for k, right in enumerate((grad_query, grad_key, grad_value)):
-            acc = jnp.zeros((width, width), floats)
-            for i in range(PIX):
-                acc = acc + mul_tn(normed_ref[i, :, cols], right[i * rows : (i + 1) * rows, :])
-            put(k, acc)
-        for k in range(2):
-            right = text_total[:, k * width : (k + 1) * width]
-            put(3 + k, mul_tn(text_ref[:, cols].astype(floats), right, highest))
-        attention_copy(j).start()
-
-    loop(full // width, weight_grads)
-    line.wait_recv()
+    out_end()
+    weight_grads(1)
+    attention_level()
+    outs[1]()
     small_ref[...] = jnp.zeros_like(small_ref)
     part = 64
 
@@ -1425,58 +1530,50 @@
         for j in range(PIX):
             conv_out[j, here, :] = result[:, j * width : (j + 1) * width]
 
-    loop(rows // part, back_norm)
-
-    def conv_copy(turn):
+    def conv_copy(turn, i, block=None):
+        here = pl.ds(i * half, half)
         return remote(
-            conv_out.at[targets[turn]],
-            grad_conv_ref.at[col],
-            conv_send.at[turn],
-            conv_recv.at[turn],
+            conv_out.at[targets[turn], here],
+            grad_conv_ref.at[col if block is None else block, here],
+            conv_send.at[2 * turn + i],
+            conv_recv.at[2 * turn + i],
             (row, targets[turn]),
         )
 
+    per_half = half // part
+    for i in range(2):
+        line_copy(i).wait_recv()
+        lax.fori_loop(i * per_half, (i + 1) * per_half, lambda j, c: (back_norm(j), c)[1], 0)
+        for turn in range(3):
+            conv_copy(turn, i).start()
+    grad_conv_ref[col] = conv_out[col]
+    for i in range(2):
+        for turn in range(3):
+            conv_copy(turn, i, targets[turn]).wait_recv()
     for turn in range(3):
-        conv_copy(turn).start()
-    grad_conv_ref[col] = conv_out[col]
-    for turn in range(3):
-        remote(
-            conv_out.at[0],
-            grad_conv_ref.at[targets[turn]],
-            conv_send.at[turn],
-            conv_recv.at[turn],
-            (row, near),
-        ).wait_recv()
-    for turn in range(3):
-        conv_copy(turn).wait_send()
+        conv_copy(turn, 0).wait_send()
+        conv_copy(turn, 1).wait_send()
         grad_copy(turn).wait_send()
         text_copy(turn).wait_send()
-    total = level_out[level].astype(floats)
-    out_total = out_level_out[level].astype(floats)
+    others_ref[:, 0 : 2 * width] = outs[2]()
+    others_ref[:, 2 * width : 3 * width] = sides[2]()
+    total = attention_out[level].astype(floats)
     for k in range(1, groups):
-        level_copy(k).wait()
-        out_level_copy(k).wait()
-        total = total + level_in[k].astype(floats)
-        out_total = out_total + out_level_in[k].astype(floats)
-    others_ref[:, 0:width] = out_total.astype(halves)
-    others_ref[:, width : 3 * width] = total.astype(halves)
-
-    def attention_sum(j):
-        attention_copy(j).wait_recv()
-        here = pl.ds(j * per_tile, per_tile)
-        attention_ref[here] = (
-            attention_grad[here, side].astype(floats) + attention_in[here].astype(floats)
-        ).astype(halves)
-
-    loop(full // width, attention_sum)
-    loop(full // width, lambda j: attention_copy(j).wait_send())
-    side_copy().wait_send()
-    out_side_copy().wait_send()
-    near_copy().wait_send()
-    far_copy().wait_send()
+        landed_copy(k).wait()
+        total = total + attention_landed[k].astype(floats)
+    others_ref[:, 3 * width :] = total.astype(halves)
+    text_owned_ref[...] = word[2]()
+
+    attention_sum(1, attention_ref)
+    for p in range(2):
+        loop(full // width, lambda j, p=p: attention_copy(p, j).wait_send())
+    for which in range(2):
+        near_copy(which).wait_send()
+        far_copy(which).wait_send()
     pair_copy(0).wait_send()
     pair_copy(1).wait_send()
-    line.wait_send()
+    line_copy(0).wait_send()
+    line_copy(1).wait_send()
 
 
 def attend_backward(
@@ -1495,8 +1592,7 @@
     text,
     text_grads,
     reduced,
-    attended,
-    grad_attn,
+    *factors,
 ):
     rows, full = hidden.shape
     groups, _, owned, _ = reduced.shape
@@ -1506,15 +1602,22 @@
     return pl.pallas_call(
         attend_back_kernel,
         out_shape=(
-            jax.ShapeDtypeStruct((groups, owned, 5 * width), halves),
-            jax.ShapeDtypeStruct((owned, 3 * width), halves),
+            jax.ShapeDtypeStruct((groups, owned, 384), halves),
+            jax.ShapeDtypeStruct((owned, 3 * width + 384), halves),
+            jax.ShapeDtypeStruct((owned, 2 * width), halves),
             jax.ShapeDtypeStruct((rows, full), floats),
             jax.ShapeDtypeStruct((PIX, rows, width), halves),
             jax.ShapeDtypeStruct((8, full), floats),
         ),
-        in_specs=[VMEM] * 16,
-        out_specs=(VMEM,) * 5,
+        in_specs=[VMEM] * 5 + [ANY] * 5 + [VMEM] * 8,
+        out_specs=(VMEM,) * 6,
         scratch_shapes=[
+            pltpu.VMEM(normed.shape, halves),
+            pltpu.VMEM((full, 3 * width), halves),
+            pltpu.VMEM((rows, full), floats),
+            pltpu.VMEM((rows, full), halves),
+            pltpu.VMEM((rows, full), floats),
+            DMA((5,)),
             pltpu.VMEM((PIX, rows, width), halves),
             flat,
             flat,
@@ -1529,45 +1632,46 @@
             pltpu.VMEM((rows, full), floats),
             pltpu.VMEM((PIX, rows, width), halves),
             pltpu.VMEM((3, used, 2 * width), halves),
+            pltpu.VMEM((2, 2, full, width), halves),
+            pltpu.VMEM((2, 2, full, width), halves),
+            pltpu.VMEM((2, 2, full, width), floats),
             pltpu.VMEM((2, full, width), halves),
             pltpu.VMEM((2, full, width), halves),
-            pltpu.VMEM((2, full, width), floats),
-            pltpu.VMEM((full, width), halves),
-            pltpu.VMEM((full, width), halves),
+            pltpu.VMEM((groups, owned, width), halves),
+            pltpu.VMEM((groups, owned, width), halves),
+            pltpu.VMEM((groups, owned, width), halves),
+            pltpu.VMEM((groups, 2, owned, 2 * width), halves),
             pltpu.VMEM((groups, owned, 2 * width), halves),
             pltpu.VMEM((groups, owned, 2 * width), halves),
             pltpu.VMEM((groups, owned, 2 * width), halves),
-            pltpu.VMEM((groups, 2, owned, width), halves),
-            pltpu.VMEM((groups, owned, width), halves),
-            pltpu.VMEM((groups, owned, width), halves),
-            pltpu.VMEM((groups, owned, width), halves),
-            pltpu.VMEM((groups, 2, owned, 5 * width), halves),
-            pltpu.VMEM((groups, owned, 5 * width), halves),
+            pltpu.VMEM((groups, 2, owned, 2 * width), halves),
+            pltpu.VMEM((groups, owned, 2 * width), halves),
+            pltpu.VMEM((groups, owned, 2 * width), halves),
+            pltpu.VMEM((groups, owned, 2 * width), halves),
+            pltpu.VMEM((2, groups, 2, owned, 384), halves),
+            pltpu.VMEM((2, groups, owned, 384), halves),
+            pltpu.VMEM((groups, owned, 384), halves),
+            pltpu.VMEM((groups, owned, 384), halves),
             DMA((3,)),
             DMA((3,)),
             DMA((3,)),
             DMA((3,)),
             DMA((2,)),
             DMA((2,)),
-            DMA,
-            DMA,
-            DMA((3,)),
-            DMA((3,)),
-            DMA,
-            DMA,
-            DMA,
-            DMA,
-            DMA,
-            DMA,
+            DMA((2,)),
+            DMA((2,)),
+            DMA((6,)),
+            DMA((6,)),
+            DMA((2,)),
+            DMA((2,)),
+            DMA((2,)),
+            DMA((2,)),
+            DMA((2, PIX)),
+            DMA((2, PIX)),
             DMA((groups,)),
             DMA((groups,)),
-            DMA,
-            DMA,
-            DMA((groups,)),
-            DMA((groups,)),
-            DMA((PIX,)),
-            DMA((PIX,)),
-        ],
+        ]
+        + [DMA, DMA, DMA((groups,)), DMA((groups,))] * 3,
         compiler_params=params(3),
         name="attend_backward",
     )(
@@ -1585,8 +1689,7 @@
         text,
         text_grads,
         reduced,
-        attended,
-        grad_attn,
+        *factors,
     )
 
 
@@ -1594,18 +1697,34 @@
     count,
     width,
     images_ref,
-    kernel_ref,
-    bank_ref,
+    kernel_from,
+    bank_from,
     styles_ref,
     inverse_ref,
     grad_ref,
     conv_ref,
     attention_ref,
+    others_ref,
+    words_ref,
+    small_ref,
+    last_ref,
     bank_grad_ref,
-    stats_ref,
-    attention_sum_ref,
+    attention_all,
+    others_all,
+    words_all,
+    rows_all_ref,
+    stats_all_ref,
     image_grad_ref,
     grads_ref,
+    kernel_ref,
+    bank_ref,
+    table_sem,
+    stats_ref,
+    rows_out,
+    rows_in,
+    stats_in,
+    rows_sum,
+    stats_sum,
     image_buf,
     padded_image,
     padded_grad,
@@ -1639,13 +1758,98 @@
     owner_recv,
     attention_send,
     attention_recv,
+    weight_send,
+    weight_recv,
+    rows_send,
+    rows_recv,
+    stats_send,
+    stats_recv,
+    far_rows_send,
+    far_rows_recv,
+    far_stats_send,
+    far_stats_recv,
+    rows_sem,
+    stats_sem,
 ):
     row, col = lax.axis_index("dp"), lax.axis_index("pix")
     groups = count // 2
     side, level = lax.rem(row, 2), lax.div(row, 2)
     partner = flip(row, 1)
     near, far, cross = peers(col)
+    targets = (far, cross, near)
     tokens, channels = grad_ref.shape
+
+    buffers = (attention_all, others_all, words_all)
+
+    def weight_copy(which, hop):
+        block = buffers[which].at[far if hop == 2 else col]
+        index = 3 * which + hop
+        return remote(
+            block, block, weight_send.at[index], weight_recv.at[index], (row, far if hop == 0 else near)
+        )
+
+    def weight_arrives(which, hop):
+        block = buffers[which].at[(far, near, cross)[hop]]
+        index = 3 * which + hop
+        remote(block, block, weight_send.at[index], weight_recv.at[index], (row, near)).wait_recv()
+
+    def weight_start(which):
+        weight_copy(which, 0).start()
+        weight_copy(which, 1).start()
+
+    def weight_pass(which):
+        weight_arrives(which, 0)
+        weight_copy(which, 2).start()
+
+    def weight_end(which):
+        weight_arrives(which, 1)
+        weight_arrives(which, 2)
+        for hop in range(3):
+            weight_copy(which, hop).wait_send()
+
+    def group_copy(turn, source, landed, send, recv):
+        return remote(source, landed.at[turn], send.at[turn], recv.at[turn], (row, targets[turn]))
+
+    def group_sum(source, landed, send, recv):
+        for turn in range(3):
+            group_copy(turn, source, landed, send, recv).wait()
+        landed[3] = source[...]
+        total = None
+        for which in range(PIX):
+            turn = jnp.where(
+                which == col, 3, jnp.where(which == far, 0, jnp.where(which == cross, 1, 2))
+            )
+            total = landed[turn] if total is None else total + landed[turn]
+        return total
+
+    def far_copy(k, total, everyone, send, recv):
+        return remote(
+            total, everyone.at[row], send.at[k], recv.at[k], (lax.rem(row + k, count), col)
+        )
+
+    def far_start(total, everyone, send, recv, sem):
+        pltpu.make_async_copy(total, everyone.at[row], sem).start()
+        lax.fori_loop(
+            1, count, lambda k, c: (far_copy(k, total, everyone, send, recv).start(), c)[1], 0
+        )
+
+    def far_end(total, everyone, send, recv, sem):
+        pltpu.make_async_copy(total, everyone.at[row], sem).wait()
+
+        def arrive(k, carry):
+            origin = lax.rem(row - k + count, count)
+            remote(total, everyone.at[origin], send.at[k], recv.at[k], (row, near)).wait_recv()
+            return carry
+
+        lax.fori_loop(1, count, arrive, 0)
+        lax.fori_loop(
+            1, count, lambda k, c: (far_copy(k, total, everyone, send, recv).wait_send(), c)[1], 0
+        )
+
+    rows_group = (rows_out, rows_in, rows_send, rows_recv)
+    stats_group = (stats_ref, stats_in, stats_send, stats_recv)
+    rows_far = (rows_sum, rows_all_ref, far_rows_send, far_rows_recv, rows_sem)
+    stats_far = (stats_sum, stats_all_ref, far_stats_send, far_stats_recv, stats_sem)
 
     def attention_copy(k):
         group = lax.rem(level + k, groups)
@@ -1660,7 +1864,7 @@
     depth = image_buf.shape[2]
     rows = tokens // PIX
     halo = width
-    greet(count, [(row, near), (row, far)])
+    greet(count, [(row, near), (row, far), (row, cross)])
 
     def sample_of(step):
         paired, k = turn_of(step)
@@ -1712,8 +1916,14 @@
             (lax.rem(row + k, count), col),
         )
 
+    loads = [
+        pltpu.make_async_copy(kernel_from, kernel_ref, table_sem.at[0]),
+        pltpu.make_async_copy(bank_from, bank_ref, table_sem.at[1]),
+    ]
     own = pltpu.make_async_copy(grad_ref, grads_ref.at[row], local_sem)
     own.start()
+    for load in loads:
+        load.start()
     own.wait()
 
     @pl.when(has_above)
@@ -1733,6 +1943,14 @@
         )
 
     fetch(0).start()
+    others_all[col] = others_ref[...]
+    words_all[col] = words_ref[...]
+    rows_out[...] = small_ref[...]
+    rows_out[5:6, :] = last_ref[0:1, :]
+    for which in (1, 2):
+        weight_start(which)
+    for turn in range(3):
+        group_copy(turn, *rows_group).start()
     products = jnp.zeros((8, channels), floats)
 
     def add_product(i, total):
@@ -1805,16 +2023,17 @@
             block = grads_ref.at[sample]
             remote(block, block, pair_send.at[k], pair_recv.at[k], (partner, col)).wait_recv()
 
-        direct = jnp.logical_not(paired) & (step > 0)
-
-        @pl.when(direct & (k <= 2 * reach) & (lax.rem(k, 2) == 1))
+        distance = lax.div(step + 1, 2)
+        odd = lax.rem(step, 2) == 1
+
+        @pl.when(odd & (distance <= reach))
         def _():
-            relay(k)
-            relay(k + 1)
-
-        @pl.when(direct & (k > 2 * reach))
+            relay(2 * distance - 1)
+            relay(2 * distance)
+
+        @pl.when(odd & (distance > reach) & (distance <= groups - 1 - reach))
         def _():
-            relay(k)
+            relay(distance + reach)
 
         load = pltpu.make_async_copy(
             grads_ref.at[sample], padded_grad.at[1, centre, :], load_sem
@@ -1926,7 +2145,17 @@
 
     lax.fori_loop(1, count, sums_arrive, 0)
 
+    for load in loads:
+        load.wait()
+
     def step_body(step):
+        @pl.when(step == 2)
+        def _():
+            for which in (1, 2):
+                weight_pass(which)
+            rows_sum[...] = group_sum(*rows_group)
+            far_start(*rows_far)
+
         @pl.when(step == count - 2)
         def _():
             lax.fori_loop(1, groups, lambda k, c: (attention_copy(k).start(), c)[1], 0)
@@ -1935,6 +2164,11 @@
         def _():
             work(step)
 
+        @pl.when(step == count)
+        def _():
+            for turn in range(3):
+                group_copy(turn, *stats_group).start()
+
         @pl.when((step >= 1) & (step <= count))
         def _():
             across(step - 1)
@@ -1944,6 +2178,14 @@
             home(step - 2)
 
     loop(count + 2, step_body)
+    lax.fori_loop(1, groups, lambda k, c: (attention_copy(k).wait(), c)[1], 0)
+    attention_total = attention_ref[level].astype(floats)
+    for k in range(1, groups):
+        attention_total = attention_total + attention_in[k].astype(floats)
+    attention_all[col] = attention_total.astype(halves)
+    weight_start(0)
+    stats_sum[...] = group_sum(*stats_group)
+    far_start(*stats_far)
 
     def write(index):
         bank_grad_ref[lax.div(index, 9), lax.rem(index, 9)] = jnp.transpose(
@@ -1964,11 +2206,11 @@
         return carry
 
     lax.fori_loop(1, count, owner_arrives, 0)
-    lax.fori_loop(1, groups, lambda k, c: (attention_copy(k).wait(), c)[1], 0)
-    attention_total = attention_ref[level].astype(floats)
-    for k in range(1, groups):
-        attention_total = attention_total + attention_in[k].astype(floats)
-    attention_sum_ref[...] = attention_total.astype(halves)
+    weight_pass(0)
+    far_end(*rows_far)
+    far_end(*stats_far)
+    for which in (1, 2, 0):
+        weight_end(which)
     for step in (count - 2, count - 1):
         pixel_copy(step).wait_send()
         line_copy(step).wait_send()
@@ -1988,7 +2230,9 @@
     lax.fori_loop(1, count, lambda k, c: (sums_copy(k).wait_send(), c)[1], 0)
 
 
-def conv_backward(images_all, kernels, bank, styles, inverse, grad, conv, attention, width):
+def conv_backward(images_all, kernels, bank, styles, inverse, grad, conv, owned, rows_here, width):
+    attention, others, words = owned
+    small, last = rows_here
     count, tokens, depth = images_all.shape
     channels = grad.shape[1]
     rows = tokens // PIX
@@ -1998,14 +2242,26 @@
         partial(conv_back_kernel, count, width),
         out_shape=(
             jax.ShapeDtypeStruct((2, 9, depth, channels), floats),
-            jax.ShapeDtypeStruct((count, 8, 128), floats),
-            jax.ShapeDtypeStruct(attention.shape[1:], halves),
+            jax.ShapeDtypeStruct((PIX,) + attention.shape[1:], halves),
+            jax.ShapeDtypeStruct((PIX,) + others.shape, halves),
+            jax.ShapeDtypeStruct((PIX,) + words.shape, halves),
+            jax.ShapeDtypeStruct((count,) + small.shape, floats),
+            jax.ShapeDtypeStruct((count, count, 8, 128), floats),
             jax.ShapeDtypeStruct((count,) + piece, halves),
             jax.ShapeDtypeStruct((count, tokens, channels), halves),
         ),
-        in_specs=[ANY] + [VMEM] * 7,
-        out_specs=(VMEM, VMEM, VMEM, ANY, ANY),
+        in_specs=[ANY] * 3 + [VMEM] * 9,
+        out_specs=(VMEM,) * 4 + (ANY,) * 4,
         scratch_shapes=[
+            pltpu.VMEM(kernels.shape, halves),
+            pltpu.VMEM(bank.shape, halves),
+            DMA((2,)),
+            pltpu.VMEM((count, 8, 128), floats),
+            pltpu.VMEM(small.shape, floats),
+            pltpu.VMEM((4,) + small.shape, floats),
+            pltpu.VMEM((4, count, 8, 128), floats),
+            pltpu.VMEM(small.shape, floats),
+            pltpu.VMEM((count, 8, 128), floats),
             pltpu.VMEM((2, tokens, depth), halves),
             pltpu.VMEM((3, tokens + 2 * width, depth), halves),
             pltpu.VMEM((3, tokens + 2 * width, channels), halves),
@@ -2039,21 +2295,128 @@
             DMA((count,)),
             DMA((groups,)),
             DMA((groups,)),
+            DMA((9,)),
+            DMA((9,)),
+            DMA((3,)),
+            DMA((3,)),
+            DMA((3,)),
+            DMA((3,)),
+            DMA((count,)),
+            DMA((count,)),
+            DMA((count,)),
+            DMA((count,)),
+            DMA,
+            DMA,
         ],
         compiler_params=params(4),
         name="conv_backward",
-    )(images_all, kernels, bank, styles, inverse, grad, conv, attention)
-
-
-def close_kernel(
-    count,
-    small_ref,
-    last_ref,
-    stats_ref,
+    )(
+        images_all,
+        kernels,
+        bank,
+        styles,
+        inverse,
+        grad,
+        conv,
+        attention,
+        others,
+        words,
+        small,
+        last,
+    )
+
+
+def prepare_kernel(
+    styled_ref,
+    label_ref,
+    select_ref,
+    modulation_ref,
+    rgb_modulation_ref,
+    images_ref,
+    query_ref,
+    key_ref,
+    value_ref,
+    out_ref,
+    cross_query_ref,
+    cross_out_ref,
+    text_key_ref,
+    text_value_ref,
     attention_ref,
     others_ref,
+    style_ref,
+    rgb_scale_ref,
+    parts_ref,
+):
+    col = lax.axis_index("pix")
+    count, rows, depth = parts_ref.shape
+    width = attention_ref.shape[1] // 5
+    short = text_key_ref.shape[0]
+    mine = pl.ds(pl.multiple_of(col * width, width), width)
+    for k, source in enumerate((query_ref, key_ref, value_ref)):
+        attention_ref[:, k * width : (k + 1) * width] = source[:, mine]
+    attention_ref[:, 3 * width :] = jnp.zeros((attention_ref.shape[0], 2 * width), halves)
+    for k, source in enumerate((text_key_ref, text_value_ref)):
+        attention_ref[0:short, (3 + k) * width : (4 + k) * width] = source[:, mine]
+    for k, source in enumerate((out_ref, cross_query_ref, cross_out_ref)):
+        others_ref[:, k * width : (k + 1) * width] = source[:, mine]
+    styled = styled_ref[...]
+    logits = jnp.sum(styled * select_ref[...], -1, keepdims=True)
+    first, second = logits[0:1], logits[1:2]
+    largest = jnp.maximum(first, second)
+    first, second = jnp.exp(first - largest), jnp.exp(second - largest)
+    total = first + second
+    eight = jnp.broadcast_to(styled, (8, styled.shape[1]))
+
+    def through(matrix):
+        return exact(mul, eight, matrix[...]) + 1.0
+
+    scaling = through(modulation_ref)
+    rgb_scale_ref[...] = through(rgb_modulation_ref)[0:1]
+    same = jnp.concatenate(
+        [jnp.broadcast_to(first / total, (1, 128)), jnp.broadcast_to(second / total, (1, 128))]
+        + [styled[:, k * 128 : (k + 1) * 128] for k in range(4)]
+        + [label_ref[...]],
+        axis=0,
+    )
+    for d in range(count):
+        lanes = slice(d * depth, (d + 1) * depth)
+        style_ref[d, 0:1, :] = jnp.zeros((1, 128), floats)
+        style_ref[d, 0:1, 0:depth] = scaling[0:1, lanes]
+        style_ref[d, 1:8, :] = same
+        parts_ref[d] = images_ref[:, lanes]
+
+
+def prepare(styled, label, select_rows, modulation, rgb_modulation, images, weights, count):
+    rows, channels = images.shape
+    owned, quarter = weights[0].shape[0], channels // PIX
+    return pl.pallas_call(
+        prepare_kernel,
+        out_shape=(
+            jax.ShapeDtypeStruct((owned, 5 * quarter), halves),
+            jax.ShapeDtypeStruct((owned, 3 * quarter), halves),
+            jax.ShapeDtypeStruct((count, 8, 128), floats),
+            jax.ShapeDtypeStruct((1, channels), floats),
+            jax.ShapeDtypeStruct((count, rows, channels // count), halves),
+        ),
+        in_specs=[VMEM] * 14,
+        out_specs=(VMEM,) * 5,
+        compiler_params=pltpu.CompilerParams(vmem_limit_bytes=VMEM_LIMIT),
+        name="prepare",
+    )(styled, label, select_rows, modulation, rgb_modulation, images, *weights)
+
+
+def finish_kernel(
     rows_ref,
-    stats_all_ref,
+    stats_ref,
+    styles_ref,
+    select_ref,
+    modulation_ref,
+    rgb_modulation_ref,
+    attention_ref,
+    others_ref,
+    words_ref,
+    grad_one_ref,
+    image_parts_ref,
     grad_query_ref,
     grad_key_ref,
     grad_value_ref,
@@ -2062,191 +2425,130 @@
     grad_cross_out_ref,
     grad_text_key_ref,
     grad_text_value_ref,
-    rows_out,
-    rows_in,
-    stats_in,
-    attention_in,
-    others_in,
-    rows_send,
-    rows_recv,
-    stats_send,
-    stats_recv,
-    far_rows_send,
-    far_rows_recv,
-    far_stats_send,
-    far_stats_recv,
-    weight_send,
-    weight_recv,
+    grad_image_ref,
+    grad_style_ref,
+    grad_table_ref,
+    grad_select_ref,
+    grad_modulation_ref,
+    grad_rgb_ref,
+    gain_self_ref,
+    gain_cross_ref,
+    rgb_weight_ref,
+    scaling,
+    styles_grad,
 ):
-    row, col = lax.axis_index("dp"), lax.axis_index("pix")
-    near, far, cross = peers(col)
-    targets = (far, cross, near)
-    greet(count, [(row, near), (row, far), (row, cross)])
-    rows_out[...] = small_ref[...]
-    rows_out[5:6, :] = last_ref[0:1, :]
-
-    def rows_copy(turn):
-        return remote(
-            rows_out, rows_in.at[turn], rows_send.at[turn], rows_recv.at[turn], (row, targets[turn])
-        )
-
-    def stats_copy(turn):
-        return remote(
-            stats_ref, stats_in.at[turn], stats_send.at[turn], stats_recv.at[turn], (row, targets[turn])
-        )
-
-    for turn in range(3):
-        rows_copy(turn).start()
-        stats_copy(turn).start()
-    attention_in[col] = attention_ref[...]
-    others_in[col] = others_ref[...]
-    buffers = (attention_in, others_in)
-
-    def weight_copy(which, hop):
-        block = buffers[which].at[far if hop == 2 else col]
-        index = 3 * which + hop
-        return remote(
-            block, block, weight_send.at[index], weight_recv.at[index], (row, far if hop == 0 else near)
-        )
-
-    def weight_arrives(which, hop):
-        block = buffers[which].at[(far, near, cross)[hop]]
-        index = 3 * which + hop
-        remote(
-            block, block, weight_send.at[index], weight_recv.at[index], (row, near)
-        ).wait_recv()
-
-    for which in range(2):
-        weight_copy(which, 0).start()
-        weight_copy(which, 1).start()
-    for turn in range(3):
-        rows_copy(turn).wait()
-        stats_copy(turn).wait()
-    rows_in[3] = rows_out[...]
-    stats_in[3] = stats_ref[...]
-
-    def in_order(buffer):
-        total = None
-        for which in range(PIX):
-            turn = jnp.where(
-                which == col, 3, jnp.where(which == far, 0, jnp.where(which == cross, 1, 2))
-            )
-            total = buffer[turn] if total is None else total + buffer[turn]
-        return total
-
-    rows_ref[row] = in_order(rows_in)
-    stats_all_ref[row] = in_order(stats_in)
-
-    def far_rows(k):
-        block = rows_ref.at[row]
-        return remote(
-            block, block, far_rows_send.at[k], far_rows_recv.at[k], (lax.rem(row + k, count), col)
-        )
-
-    def far_stats(k):
-        block = stats_all_ref.at[row]
-        return remote(
-            block, block, far_stats_send.at[k], far_stats_recv.at[k], (lax.rem(row + k, count), col)
-        )
-
-    lax.fori_loop(1, count, lambda k, c: (far_rows(k).start(), far_stats(k).start(), c)[2], 0)
-    for which in range(2):
-        weight_arrives(which, 0)
-        weight_copy(which, 2).start()
-    width = attention_ref.shape[1] // 5
-    short = grad_text_key_ref.shape[0]
-    for which in range(2):
-        weight_arrives(which, 1)
-        weight_arrives(which, 2)
-    attention_outs = (
-        grad_query_ref,
-        grad_key_ref,
-        grad_value_ref,
-        grad_text_key_ref,
-        grad_text_value_ref,
-    )
-    other_outs = (grad_out_ref, grad_cross_query_ref, grad_cross_out_ref)
-    for buffer, outs in ((attention_in, attention_outs), (others_in, other_outs)):
+    row = lax.axis_index("dp")
+    count, rows, depth = image_parts_ref.shape
+    width = words_ref.shape[2] // 2
+    for d in range(count):
+        lanes = slice(d * depth, (d + 1) * depth)
+        grad_image_ref[:, lanes] = grad_one_ref[:, lanes] + image_parts_ref[d].astype(floats)
+        scaling[:, lanes] = stats_ref[d, :, 0, :][:, :depth]
+    for k, out in enumerate((grad_query_ref, grad_key_ref, grad_value_ref)):
+        for p in range(2 * PIX):
+            first = 3 * width + k * 128 if p % 2 == 0 else k * 128
+            source = others_ref if p % 2 == 0 else attention_ref
+            out[:, p * 128 : (p + 1) * 128] = source[p // 2, :, first : first + 128].astype(floats)
+    for buffer, outs in (
+        (others_ref, (grad_out_ref, grad_cross_query_ref, grad_cross_out_ref)),
+        (words_ref, (grad_text_key_ref, grad_text_value_ref)),
+    ):
         for k, out in enumerate(outs):
             for p in range(PIX):
                 block = buffer[p, :, k * width : (k + 1) * width].astype(floats)
                 out[:, p * width : (p + 1) * width] = block[: out.shape[0]]
-
-    def arrive(k, carry):
-        origin = lax.rem(row - k + count, count)
-        block = rows_ref.at[origin]
-        remote(block, block, far_rows_send.at[k], far_rows_recv.at[k], (row, near)).wait_recv()
-        block = stats_all_ref.at[origin]
-        remote(block, block, far_stats_send.at[k], far_stats_recv.at[k], (row, near)).wait_recv()
-        return carry
-
-    lax.fori_loop(1, count, arrive, 0)
-    lax.fori_loop(
-        1, count, lambda k, c: (far_rows(k).wait_send(), far_stats(k).wait_send(), c)[2], 0
+    sums = rows_ref[0]
+    for d in range(1, count):
+        sums = sums + rows_ref[d]
+    gain_self_ref[...] = sums[5:6]
+    gain_cross_ref[...] = sums[0:1]
+    rgb_weight_ref[...] = sums[2:5]
+    mixing, grads = [], []
+    for k in (1, 2):
+        total = stats_ref[0, :, k, :]
+        for d in range(1, count):
+            total = total + stats_ref[d, :, k, :]
+        grads.append(jnp.sum(total, -1, keepdims=True))
+        mixing.append(styles_ref[:, k, :][:, 0:1])
+    inner = grads[0] * mixing[0] + grads[1] * mixing[1]
+    logits = [m * (g - inner) for m, g in zip(mixing, grads)]
+    styled = jnp.concatenate([styles_ref[:, 3 + k, :] for k in range(4)], axis=1)
+    rgb = rows_ref[:, 1, :]
+    grad_modulation_ref[...] = outer_sum(styled, scaling[...])
+    grad_rgb_ref[...] = outer_sum(styled, rgb)
+    place = lax.broadcasted_iota(jnp.int32, (count, 128), 1)
+    both = jnp.where(place == 0, logits[0], jnp.where(place == 1, logits[1], 0.0))
+    grad_select_ref[...] = outer_sum(both, styled)[0:2]
+    grad_styles = (
+        exact(mul_nt, scaling[...], modulation_ref[...])
+        + exact(mul_nt, rgb, rgb_modulation_ref[...])
+        + logits[0] * select_ref[0:1, :]
+        + logits[1] * select_ref[1:2, :]
     )
-    for which in range(2):
-        for hop in range(3):
-            weight_copy(which, hop).wait_send()
-
-
-def close(small, last, stats, attention, others, text_rows):
-    count = stats.shape[0]
-    block = small.shape
-    owned, full = attention.shape[0], small.shape[1]
-    weight = jax.ShapeDtypeStruct((owned, full), floats)
-    text = jax.ShapeDtypeStruct((text_rows, full), floats)
+    styles_grad[...] = grad_styles
+    grad_style_ref[...] = styles_grad[pl.ds(row, 1), :]
+    label = styles_ref[:, 7, :][:, 0:1].astype(jnp.int32)
+    classes = grad_table_ref.shape[0]
+    chosen = lax.broadcasted_iota(jnp.int32, (count, classes), 1) == label
+    chosen = chosen.astype(floats).astype(halves)
+    grad_table_ref[...] = mul_tn(
+        jnp.concatenate([chosen] * 3, axis=0),
+        jnp.concatenate(split(grad_styles)[::-1], axis=0),
+    )
+
+
+def finish(
+    all_rows,
+    all_stats,
+    styles,
+    select_rows,
+    modulation,
+    rgb_modulation,
+    gathered,
+    grad_one,
+    image_parts,
+    classes,
+    text_rows,
+):
+    count = styles.shape[0]
+    rows, channels = grad_one.shape
+    owned = gathered[0].shape[1]
+    wide = modulation.shape[0]
+
+    def out(*shape):
+        return jax.ShapeDtypeStruct(shape, floats)
+
     return pl.pallas_call(
-        partial(close_kernel, count),
-        out_shape=(
-            jax.ShapeDtypeStruct((count,) + block, floats),
-            jax.ShapeDtypeStruct((count,) + stats.shape, floats),
-        )
-        + (weight,) * 6
-        + (text,) * 2,
-        in_specs=[VMEM] * 5,
-        out_specs=(VMEM,) * 10,
-        scratch_shapes=[
-            pltpu.VMEM(block, floats),
-            pltpu.VMEM((4,) + block, floats),
-            pltpu.VMEM((4,) + stats.shape, floats),
-            pltpu.VMEM((PIX,) + attention.shape, halves),
-            pltpu.VMEM((PIX,) + others.shape, halves),
-            DMA((3,)),
-            DMA((3,)),
-            DMA((3,)),
-            DMA((3,)),
-            DMA((count,)),
-            DMA((count,)),
-            DMA((count,)),
-            DMA((count,)),
-            DMA((6,)),
-            DMA((6,)),
-        ],
-        compiler_params=params(5),
-        name="close",
-    )(small, last, stats, attention, others)
-
-
-def style_rows(style_codes, labels, class_table, select_weight, modulation, rgb_modulation):
-    class_row = jnp.take(class_table, labels, axis=0).astype(floats)
-    styled = style_codes.astype(floats) + class_row
-    mixing = jax.nn.softmax(jnp.dot(styled, select_weight.astype(floats), precision=highest), -1)
-    scaling = jnp.dot(styled, modulation.astype(floats), precision=highest) + 1.0
-    rgb_scale = jnp.dot(styled, rgb_modulation.astype(floats), precision=highest) + 1.0
-    return styled, mixing, scaling, rgb_scale
-
-
-def pack_style(styled, labels, mixing, scaling, count):
-    depth = scaling.shape[-1] // count
-    pieces = jnp.pad(scaling.reshape(count, 1, depth), ((0, 0), (0, 0), (0, 128 - depth)))
-    same = jnp.concatenate(
-        [
-            jnp.broadcast_to(mixing.reshape(2, 1), (2, 128)),
-            styled.reshape(4, 128),
-            jnp.broadcast_to(labels.astype(floats).reshape(1, 1), (1, 128)),
-        ]
+        finish_kernel,
+        out_shape=(out(owned, channels),) * 6
+        + (out(text_rows, channels),) * 2
+        + (
+            out(rows, channels),
+            out(1, wide),
+            out(classes, wide),
+            out(2, wide),
+            out(wide, channels),
+            out(wide, channels),
+            out(1, channels),
+            out(1, channels),
+            out(3, channels),
+        ),
+        in_specs=[VMEM] * 11,
+        out_specs=(VMEM,) * 17,
+        scratch_shapes=[pltpu.VMEM((count, channels), floats), pltpu.VMEM((count, wide), floats)],
+        compiler_params=pltpu.CompilerParams(vmem_limit_bytes=VMEM_LIMIT),
+        name="finish",
+    )(
+        all_rows,
+        all_stats,
+        styles,
+        select_rows,
+        modulation,
+        rgb_modulation,
+        *gathered,
+        grad_one,
+        image_parts,
     )
-    return jnp.concatenate([pieces, jnp.broadcast_to(same, (count, 7, 128))], axis=1)
 
 
 def on_device(
@@ -2276,29 +2578,30 @@
     rgb_cotangent,
 ):
     count = lax.axis_size("dp")
-    row, col = lax.axis_index("dp"), lax.axis_index("pix")
     _, height, width, channels = images.shape
     rows = height * width
     quarter = channels // PIX
     depth = channels // count
 
-    def my_columns(*weights):
-        return jnp.concatenate(
-            [lax.dynamic_slice_in_dim(w, col * quarter, quarter, axis=1) for w in weights], axis=1
-        )
-
     owned, text_owned = w_query.shape[0], c_key.shape[0]
-    text_columns = jnp.pad(my_columns(c_key, c_value), ((0, owned - text_owned), (0, 0)))
-    attention = jnp.concatenate([my_columns(w_query, w_key, w_value), text_columns], axis=1)
+    class_row = jnp.take(class_table, labels, axis=0).astype(floats)
+    styled = style_codes.astype(floats) + class_row
+    label = jnp.broadcast_to(labels.astype(floats).reshape(1, 1), (1, 128))
+    select_rows = jnp.pad(select_weight.T, ((0, 6), (0, 0))).astype(floats)
+    own = images.reshape(rows, channels)
+    attention, others, style, rgb_scale, parts = prepare(
+        styled,
+        label,
+        select_rows,
+        modulation,
+        rgb_modulation,
+        own,
+        (w_query, w_key, w_value, w_out, c_query, c_out, c_key, c_value),
+        count,
+    )
     attention = lax.all_gather(attention, "dp", axis=0, tiled=True)
-    others = lax.all_gather(my_columns(w_out, c_query, c_out), ("pix", "dp"), axis=0, tiled=True)
+    others = lax.all_gather(others, ("pix", "dp"), axis=0, tiled=True)
     others = others.reshape(PIX, channels, 3 * quarter)
-
-    styled, mixing, scaling, rgb_scale = style_rows(
-        style_codes, labels, class_table, select_weight, modulation, rgb_modulation
-    )
-    own = images.reshape(rows, channels)
-    parts = own.reshape(rows, count, depth).transpose(1, 0, 2)
     bank = conv_bank.reshape(2, 9, depth, quarter)
     bank_turned = bank.transpose(0, 1, 3, 2)
     words = token_ids.shape[1]
@@ -2307,9 +2610,7 @@
     text = jnp.pad(text, ((0, 128 - words), (0, 0), (0, owned - text_owned)))
     text = text.reshape(128, channels)
 
-    images_all, kernels, styles, inverse = gather_inputs(
-        pack_style(styled, labels, mixing, scaling, count), bank, parts
-    )
+    images_all, kernels, styles, inverse = gather_inputs(style, bank, parts)
     images_all = images_all.reshape(count, PIX * rows, depth)
     conv, conv_own, hidden_one, normed_one = conv_forward(images_all, kernels, own, gain_self, width)
     query, key, value, totals, attended, text_all = attend_forward(
@@ -2325,8 +2626,7 @@
         grad_two,
         grad_attended,
         small,
-        attended_rows,
-        grad_attn,
+        *factors,
     ) = cross_part(
         words,
         attended,
@@ -2340,7 +2640,7 @@
         rgb_rows,
         penalty,
     )
-    attention_grads, others_owned, grad_one, grad_conv, last = attend_backward(
+    attention_grads, others_owned, words_owned, grad_one, grad_conv, last = attend_backward(
         words,
         grad_attended,
         query,
@@ -2355,12 +2655,11 @@
         gain_self,
         text,
         text_grads,
-        reduced.reshape(count // 2, 2, owned, 2 * quarter),
-        attended_rows,
-        grad_attn,
+        reduced.reshape(count // 2, 2, owned, quarter),
+        *factors,
     )
 
-    bank_grad, stats, attention_owned, image_parts, _ = conv_backward(
+    bank_grad, *gathered, all_rows, all_stats, image_parts, _ = conv_backward(
         images_all,
         kernels,
         bank_turned,
@@ -2368,13 +2667,11 @@
         inverse,
         grad_conv.reshape(PIX * rows, quarter),
         conv_own,
-        attention_grads,
+        (attention_grads, others_owned, words_owned),
+        (small, last),
         width,
     )
-    grad_image = grad_one + image_parts.transpose(1, 0, 2).reshape(rows, channels).astype(floats)
     (
-        all_rows,
-        all_stats,
         grad_w_query,
         grad_w_key,
         grad_w_value,
@@ -2383,49 +2680,39 @@
         grad_c_out,
         grad_c_key,
         grad_c_value,
-    ) = close(small, last, stats, attention_owned, others_owned, text_owned)
-
-    styled_all = styles[:, 3:7, :].reshape(count, -1)
-    mixing_all = styles[:, 1:3, 0]
-    labels_all = styles[:, 7, 0].astype(jnp.int32)
-    grad_scaling = all_stats[:, :, 0, :depth].transpose(1, 0, 2).reshape(count, channels)
-    grad_mixing = jnp.sum(all_stats[:, :, 1:3, :], axis=(0, 3))
-    grad_rgb_scale = all_rows[:, 1, :]
-    inner = jnp.sum(grad_mixing * mixing_all, -1, keepdims=True)
-    grad_logits = mixing_all * (grad_mixing - inner)
-
-    def outer(right):
-        return lax.dot_general(
-            styled_all, right, TN, precision=highest, preferred_element_type=floats
-        )
-
-    def back(left, right):
-        return lax.dot_general(
-            left, right.astype(floats), NT, precision=highest, preferred_element_type=floats
-        )
-
-    grad_styles = (
-        back(grad_logits, select_weight)
-        + back(grad_scaling, modulation)
-        + back(grad_rgb_scale, rgb_modulation)
+        grad_image,
+        grad_style,
+        grad_table,
+        grad_select,
+        grad_modulation,
+        grad_rgb_modulation,
+        grad_gain_self,
+        grad_gain_cross,
+        grad_rgb_weight,
+    ) = finish(
+        all_rows,
+        all_stats,
+        styles,
+        select_rows,
+        modulation,
+        rgb_modulation,
+        gathered,
+        grad_one,
+        image_parts,
+        class_table.shape[0],
+        text_owned,
     )
-    classes = class_table.shape[0]
-    chosen = (labels_all[:, None] == jnp.arange(classes, dtype=jnp.int32)[None, :]).astype(floats)
-    grad_table = lax.dot_general(
-        chosen, grad_styles, TN, precision=highest, preferred_element_type=floats
-    )
-    sums = jnp.sum(all_rows, axis=0)
     shape = images.shape
     return (
         output.reshape(shape),
         rgb[:, :3].T.reshape(1, 3, height, width),
         grad_image.reshape(shape),
-        lax.dynamic_slice_in_dim(grad_styles, row, 1, axis=0),
+        grad_style,
         grad_table,
         bank_grad.reshape(conv_bank.shape),
-        outer(grad_logits),
-        outer(grad_scaling),
-        outer(grad_rgb_scale),
+        grad_select.T,
+        grad_modulation,
+        grad_rgb_modulation,
         grad_w_query,
         grad_w_key,
         grad_w_value,
@@ -2434,9 +2721,9 @@
         grad_c_key,
         grad_c_value,
         grad_c_out,
-        sums[5],
-        sums[0],
-        sums[2:5].T,
+        grad_gain_self.reshape(-1),
+        grad_gain_cross.reshape(-1),
+        grad_rgb_weight.T,
     )
 
 

time: 507 us -> 413 us (0.81)
  Pallas kernels: 432 us -> 381 us
  local copies, waits for them, and re-layouts: 28.9 us -> 11.8 us
  matrix products: 13.2 us -> 0 us
  other arithmetic: 12 us -> 2.74 us
    pallas_call x1, Pallas kernels: 92 us -> 73 us  [attend_backward(): pl.pallas_call(attend_back_kernel, out_shape=(jax.ShapeDtypeStruct((group...]
    pallas_call x1, Pallas kernels: 57.3 us -> 41.9 us  [cross_part(): pl.pallas_call(partial(cross_kernel, words), out_shape=(jax.ShapeDtypeStr...]
    pallas_call x1, Pallas kernels: 103 us -> 87.3 us  [conv_backward(): pl.pallas_call(partial(conv_back_kernel, count, width), out_shape=(jax.Sh...]
    dot_general x10 -> x0, matrix products: 13.2 us -> none  [the longest x3 7.05 us: outer(): lax.dot_general(styled_all, right, TN, precision=highest, preferred_eleme...]
    pallas_call x1 -> x2, Pallas kernels: 23.3 us -> 12 us  [the longest x1 8.29 us: finish(): pl.pallas_call(finish_kernel, out_shape=(out(owned, channels),) * 6 + (ou...]
    unnamed x61 -> x21, local copies, waits for them, and re-layouts: 12.2 us -> 5.62 us
    pallas_call x1, Pallas kernels: 102 us -> 108 us  [conv_forward(): pl.pallas_call(partial(conv_kernel, count, width), out_shape=(jax.ShapeDt...]
  transfers between devices with their start and end apart: 2 -> 2, of which waited for: 0 -> 0; matrix products, arithmetic and copies ran while one was open for 4% -> 2% of each run, Pallas kernels for 31% -> 41%
where the time goes in v3:
time: 413 us; the launch traced here: 412 us
  Pallas kernels  381 us (92%)
  between operations  15.5 us (4%)
  local copies, waits for them, and re-layouts  11.8 us (3%)
    pallas_call x1, Pallas kernels, conv_forward(): pl.pallas_call(partial(conv_kernel, count, width), out_shape=(jax.ShapeDt...  108 us
    pallas_call x1, Pallas kernels, conv_backward(): pl.pallas_call(partial(conv_back_kernel, count, width), out_shape=(jax.Sh...  87.3 us
    pallas_call x1, Pallas kernels, attend_backward(): pl.pallas_call(attend_back_kernel, out_shape=(jax.ShapeDtypeStruct((group...  73 us
    pallas_call x1, Pallas kernels, cross_part(): pl.pallas_call(partial(cross_kernel, words), out_shape=(jax.ShapeDtypeStr...  41.9 us
    pallas_call x1, Pallas kernels, gather_inputs(): pl.pallas_call(partial(gather_kernel, count), out_shape=(jax.ShapeDtypeSt...  37.1 us
    pallas_call x1, Pallas kernels, attend_forward(): pl.pallas_call(attend_kernel, out_shape=(flat, flat, flat, jax.ShapeDtype...  21.6 us
    pallas_call x1, Pallas kernels, finish(): pl.pallas_call(finish_kernel, out_shape=(out(owned, channels),) * 6 + (ou...  8.29 us
  transfers between devices with their start and end apart: 2, of which 0 were waited for; matrix products, arithmetic and copies ran while one was open for 2% of the time, Pallas kernels for 41%

profile of v3, /device:TPU:0, one launch (start us, length us, event | category | flops | bytes accessed | tf_op | source)
XLA Modules:
  0.0 412.0 jit_solution(11751257784254740852)
XLA Ops:
  7.9 1.3 pad_convert_fusion.select_ref
  9.2 1.3 fusion.1.styled_ref
  10.5 0.5 broadcast_in_dim.40.label_ref
  11.0 3.7 prepare.1
  14.8 0.7 all-gather.5.cloned.1.call-update
  15.5 3.5 gather_fusion
  19.0 0.2 gather.12
  19.2 0.1 broadcast_select_fusion
  19.5 0.8 copy.52
  20.2 0.2 copy.46
  20.4 0.8 pad.18.rgb_weight_ref
  22.0 1.4 copy.44
  23.4 0.7 pad.19.rgb_cotangent_ref
  24.0 37.1 %gather_inputs.1 = (bf16[8,4,256,128]{3,2,1,0:T(8,128)(2,1)}, bf16[8,9,128,256]{3,2,1,0:T(8,128)(2,1)}, f32[8,8,128]{2,1,0:T(8,128)}, f32[8,256]{1,0:T(8,128)}) custom-call(f32[8,8,128]{2,1,0:T(8,128)} %get-tuple-element.80.style_ref, bf16[2,9,128,256]{3,2,1,0:T(8,128)(2,1)} %bitcast.44, bf16[8,256,128]{2,1,0:T(8,128)(2,1)} %get-tuple-element.81.parts_ref), custom_call_target="tpu_custom_call" | custom-call | tf_op jit(solution)/shard_map/gather_inputs/pallas_call | solution.py:258
  61.2 108.1 %conv_forward.1 = (bf16[256,1024]{1,0:T(8,128)(2,1)}, bf16[1024,256]{1,0:T(8,128)(2,1)}, f32[256,1024]{1,0:T(8,128)}, bf16[4,256,1024]{2,1,0:T(8,128)(2,1)}) custom-call(bf16[8,1024,128]{2,1,0:T(8,128)(2,1)} %bitcast.41, bf16[8,9,128,256]{3,2,1,0:T(8,128)(2,1)} %get-tuple-element.83.kernel_ref.kernel_from, bf16[256,1024]{1,0:T(8,128)(2,1)} %bitcast.50, ...), custom_call_target="tpu_custom_call" | custom-call | tf_op jit(solution)/shard_map/conv_forward/pallas_call | solution.py:566
  169.4 21.6 %attend_forward.1 = (bf16[1024,256]{1,0:T(8,128)(2,1)}, bf16[1024,256]{1,0:T(8,128)(2,1)}, bf16[1024,256]{1,0:T(8,128)(2,1)}, f32[1024,128]{1,0:T(8,128)}, bf16[...) custom-call(bf16[4,256,1024]{2,1,0:T(8,128)(2,1)} %get-tuple-element.84.normed_ref.normed_from, ...), custom_call_target="tpu_custom_call" | custom-call | tf_op jit(solution)/shard_map/attend_forward/pallas_call | solution.py:758
  191.0 0.5 broadcast_in_dim.44.penalty_ref
  191.5 41.9 %cross_part.1 = (f32[256,1024]{1,0:T(8,128)}, f32[256,128]{1,0:T(8,128)}, bf16[1024,256]{1,0:T(8,128)(2,1)}, bf16[4,128,512]{2,1,0:T(8,128)(2,1)}, f32[256,1024]...) custom-call(bf16[4,256,256]{2,1,0:T(8,128)(2,1)} %get-tuple-element., ...), custom_call_target="tpu_custom_call" | custom-call | tf_op jit(solution)/shard_map/cross_part/pallas_call | solution.py:1039
  233.4 73.0 %attend_backward.1 = (bf16[4,128,384]{2,1,0:T(8,128)(2,1)}, bf16[128,1152]{1,0:T(8,128)(2,1)}, bf16[128,512]{1,0:T(8,128)(2,1)}, f32[256,1024]{1,0:T(8,128)}, bf...) custom-call(bf16[4,256,256]{2,1,0:T(8,128)(2,1)} %get-tuple-element.95.grad_ref, ...), custom_call_target="tpu_custom_call" | custom-call | tf_op jit(solution)/shard_map/attend_backward/pallas_call | solution.py:1602
  306.4 87.3 %conv_backward.1 = (f32[2,9,128,256]{3,2,1,0:T(8,128)}, bf16[4,128,384]{2,1,0:T(8,128)(2,1)}, bf16[4,128,1152]{2,1,0:T(8,128)(2,1)}, bf16[4,128,512]{2,1,0:T(8,1...) custom-call(bf16[8,1024,128]{2,1,0:T(8,128)(2,1)} %bitcast.42, ...), custom_call_target="tpu_custom_call" | custom-call | tf_op jit(solution)/shard_map/conv_backward/pallas_call | solution.py:2241
  393.8 0.7 copy.48
  394.5 8.3 %finish.1 = (f32[128,1024]{1,0:T(8,128)}, f32[128,1024]{1,0:T(8,128)}, f32[128,1024]{1,0:T(8,128)}, f32[128,1024]{1,0:T(8,128)}, f32[128,1024]{1,0:T(8,128)}, /*...) custom-call(f32[8,8,1024]{2,1,0:T(8,128)} %get-tuple-element.115.row, ...), custom_call_target="tpu_custom_call" | custom-call | tf_op jit(solution)/shard_map/finish/pallas_call | solution.py:2521
  402.8 1.0 copy.57
  403.8 1.4 copy.58
  (24 shorter events, 0.4 us)
Async XLA Ops:
  7.2 162.2 %all-gather.3.cloned.1.call-start = ((), (), s32[]{:S(2)}) async-start(), calls=%async_computation | async-start | bytes 2949120 | tf_op jit(solution)/shard_map/all_gather | solution.py:2602
  11.0 4.5 %copy-start.6 = (s32[1,77]{1,0:T(1,128)S(1)}, s32[1,77]{1,0:T(1,128)}, u32[]{:S(2)}) copy-start(s32[1,77]{1,0:T(1,128)} %param.27) | copy-start | bytes 928
  14.7 5.5 %copy-start.5 = (bf16[1024,3]{0,1:T(4,128)(2,1)S(1)}, bf16[1024,3]{0,1:T(4,128)(2,1)}, u32[]{:S(2)}) copy-start(bf16[1024,3]{0,1:T(4,128)(2,1)} %param.45) | copy-start | bytes 18436
  14.7 6.5 %copy-start.4 = (f32[1,3,8,32]{3,2,1,0:T(8,128)S(1)}, f32[1,3,8,32]{3,2,1,0:T(8,128)}, u32[]{:S(2)}) copy-start(f32[1,3,8,32]{3,2,1,0:T(8,128)} %param.47) | copy-start | bytes 9220
  14.7 7.3 %copy-start = (bf16[2,3,3,128,256]{4,3,2,1,0:T(8,128)(2,1)S(1)}, bf16[2,3,3,128,256]{4,3,2,1,0:T(8,128)(2,1)}, u32[]{:S(2)}) copy-start(bf16[2,3,3,128,256]{4,3,2,1,0:T(8,128)(2,1)} %param.31) | copy-start | bytes 3538948
  14.7 176.3 %all-gather.5.cloned.1.call-start = ((), (), s32[]{:S(2)}) async-start(), calls=%async_computation.1 | async-start | bytes 6488064 | tf_op jit(solution)/shard_map/all_gather | solution.py:2603
  306.4 87.4 %copy-start.3 = (f32[256,128]{1,0:T(8,128)S(1)}, f32[256,128]{1,0:T(8,128)}, u32[]{:S(2)}) copy-start(f32[256,128]{1,0:T(8,128)} %get-tuple-element.92) | copy-start | bytes 393220
  394.5 8.3 %copy-start.2 = (f32[256,1024]{1,0:T(8,128)S(1)}, f32[256,1024]{1,0:T(8,128)}, u32[]{:S(2)}) copy-start(f32[256,1024]{1,0:T(8,128)} %get-tuple-element.91) | copy-start | bytes 3145732
  394.5 9.3 %copy-start.1 = (f32[2,9,128,256]{3,2,1,0:T(8,128)S(1)}, f32[2,9,128,256]{3,2,1,0:T(8,128)}, u32[]{:S(2)}) copy-start(f32[2,9,128,256]{3,2,1,0:T(8,128)} %get-tuple-element.125) | copy-start | bytes 7077892
Sparse Core Ops, SparseCore 0:
  14.9 68.3 all-gather.2
  86.8 85.4 all-gather.4

commit v4 on v3

--- a/solution.py
+++ b/solution.py
@@ -378,57 +378,70 @@
                 )
         return acc
 
-    def pair_copy(step):
+    half = tokens // 2
+    per_half = PIX // 2
+
+    def half_of(h):
+        return pl.ds(h * half, half)
+
+    def pair_copy(step, h):
         return remote(
-            pair_out.at[lax.rem(step, slots)],
-            pair_in.at[step],
-            pair_send.at[step],
-            pair_recv.at[step],
+            pair_out.at[lax.rem(step, slots), half_of(h)],
+            pair_in.at[step, half_of(h)],
+            pair_send.at[step, h],
+            pair_recv.at[step, h],
             (partner, col),
         )
 
-    def line_copy(step, upward):
+    def line_copy(step, upward, h):
         group = group_of(step)
         if upward:
             slot, target = group, above
         else:
             slot, target = jnp.where(group == level - 1, groups, group), below
         return remote(
-            line_out.at[lax.rem(step, slots)],
-            line_in.at[slot],
-            line_send.at[step],
-            line_recv.at[slot],
+            line_out.at[lax.rem(step, slots), half_of(h)],
+            line_in.at[slot, half_of(h)],
+            line_send.at[step, h],
+            line_recv.at[slot, h],
             (target, col),
         )
 
-    def line_arrives(slot):
+    def line_arrives(slot, h):
         remote(
-            line_out.at[0], line_in.at[slot], line_send.at[0], line_recv.at[slot], (partner, col)
+            line_out.at[0, half_of(h)],
+            line_in.at[slot, half_of(h)],
+            line_send.at[0, h],
+            line_recv.at[slot, h],
+            (partner, col),
         ).wait_recv()
 
     def give(step):
         @pl.when(step >= slots)
         def _():
-            pair_copy(step - slots).wait_send()
+            for h in range(2):
+                pair_copy(step - slots, h).wait_send()
 
         stage(step)
         sample = sample_of(step)
-
-        def chunk(i):
-            start = pl.multiple_of(i * rows, rows)
-            pair_out[lax.rem(step, slots), pl.ds(start, rows), :] = rows_of(sample, start).astype(
-                halves
-            )
-
-        loop(PIX, chunk)
-        pair_copy(step).start()
+        for h in range(2):
+
+            def chunk(i, h=h):
+                start = pl.multiple_of(h * half + i * rows, rows)
+                pair_out[lax.rem(step, slots), pl.ds(start, rows), :] = rows_of(
+                    sample, start
+                ).astype(halves)
+
+            loop(per_half, chunk)
+            pair_copy(step, h).start()
 
     loop(groups, give)
 
     def keep(step):
         @pl.when(step >= slots)
         def _():
-            line_copy(step - slots, True).wait_send()
+            for h in range(2):
+                line_copy(step - slots, True, h).wait_send()
 
         stage(groups + step)
         group = group_of(step)
@@ -440,40 +453,41 @@
             total[pl.ds(start, rows), :] = rows_of(sample, start)
 
         loop(PIX, chunk)
-        pair_copy(step).wait_recv()
         passing = jnp.where(group > level, has_below, has_above)
-
-        @pl.when(passing)
-        def _():
-            line_arrives(group)
-
-            def add(i):
-                here = pl.ds(pl.multiple_of(i * rows, rows), rows)
-                line_out[out, here, :] = (
-                    total[here, :]
-                    + pair_in[step, here, :].astype(floats)
-                    + line_in[group, here, :].astype(floats)
-                ).astype(halves)
-
-            loop(PIX, add)
-
-        @pl.when(jnp.logical_not(passing))
-        def _():
-            def add(i):
-                here = pl.ds(pl.multiple_of(i * rows, rows), rows)
-                line_out[out, here, :] = (
-                    total[here, :] + pair_in[step, here, :].astype(floats)
-                ).astype(halves)
-
-            loop(PIX, add)
-
-        @pl.when(group > level)
-        def _():
-            line_copy(step, True).start()
-
-        @pl.when(group < level)
-        def _():
-            line_copy(step, False).start()
+        for h in range(2):
+            pair_copy(step, h).wait_recv()
+
+            @pl.when(passing)
+            def _(h=h):
+                line_arrives(group, h)
+
+                def add(i):
+                    here = pl.ds(pl.multiple_of(h * half + i * rows, rows), rows)
+                    line_out[out, here, :] = (
+                        total[here, :]
+                        + pair_in[step, here, :].astype(floats)
+                        + line_in[group, here, :].astype(floats)
+                    ).astype(halves)
+
+                loop(per_half, add)
+
+            @pl.when(jnp.logical_not(passing))
+            def _(h=h):
+                def add(i):
+                    here = pl.ds(pl.multiple_of(h * half + i * rows, rows), rows)
+                    line_out[out, here, :] = (
+                        total[here, :] + pair_in[step, here, :].astype(floats)
+                    ).astype(halves)
+
+                loop(per_half, add)
+
+            @pl.when(group > level)
+            def _(h=h):
+                line_copy(step, True, h).start()
+
+            @pl.when(group < level)
+            def _(h=h):
+                line_copy(step, False, h).start()
 
     loop(groups - 1, keep)
     last = groups - 1
@@ -484,45 +498,44 @@
         total[pl.ds(start, rows), :] = rows_of(row, start)
 
     loop(PIX, own_chunk)
-    pair_copy(last).wait_recv()
-    for known, slot in ((has_below, level), (has_above, groups)):
-
-        @pl.when(known)
-        def _(slot=slot):
-            line_arrives(slot)
-
-            def add(i):
-                here = pl.ds(pl.multiple_of(i * rows, rows), rows)
-                total[here, :] += line_in[slot, here, :].astype(floats)
-
-            loop(PIX, add)
-
-    def block_copy(turn):
-        target = (far, cross, near)[turn]
+    for h in range(2):
+        for known, slot in ((has_below, level), (has_above, groups)):
+
+            @pl.when(known)
+            def _(slot=slot, h=h):
+                line_arrives(slot, h)
+
+                def add(i):
+                    here = pl.ds(pl.multiple_of(h * half + i * rows, rows), rows)
+                    total[here, :] += line_in[slot, here, :].astype(floats)
+
+                loop(per_half, add)
+
+        pair_copy(last, h).wait_recv()
+
+    short = rows // 2
+    part = rows // 4
+
+    def block_copy(turn, i, origin=None):
+        here = pl.ds(i * short, short)
         return remote(
-            block_out.at[turn], block_in.at[col], block_send.at[turn], block_recv.at[turn], (row, target)
-        )
-
-    def block_arrives(turn):
-        origin = (far, cross, near)[turn]
-        remote(
-            block_out.at[turn], block_in.at[origin], block_send.at[turn], block_recv.at[turn], (row, near)
-        ).wait_recv()
-
-    for turn, target in enumerate((far, cross, near, col)):
-        here = pl.ds(pl.multiple_of(target * rows, rows), rows)
-        value = total[here, :] + pair_in[last, here, :].astype(floats)
-        rounded = value.astype(halves)
-        conv_own_ref[here, :] = rounded
-        if turn < 3:
-            block_out[turn] = rounded
-            block_copy(turn).start()
-        else:
-            block_in[col] = rounded
-    for turn in range(3):
-        block_arrives(turn)
-
-    part = rows // 4
+            block_out.at[turn, here],
+            block_in.at[col if origin is None else origin, here],
+            block_send.at[2 * turn + i],
+            block_recv.at[2 * turn + i],
+            (row, (far, cross, near)[turn]),
+        )
+
+    for i in range(2):
+        for turn, target in enumerate((far, cross, near, col)):
+            here = pl.ds(pl.multiple_of(target * rows + i * short, short), short)
+            rounded = (total[here, :] + pair_in[last, here, :].astype(floats)).astype(halves)
+            conv_own_ref[here, :] = rounded
+            if turn < 3:
+                block_out[turn, i * short : (i + 1) * short, :] = rounded
+                block_copy(turn, i).start()
+            else:
+                block_in[col, i * short : (i + 1) * short, :] = rounded
 
     def norm_rows(i):
         here = pl.ds(pl.multiple_of(i * part, part), part)
@@ -534,26 +547,34 @@
         mean = jnp.mean(hidden * hidden, -1, keepdims=True)
         normed_ref[col, here, :] = (hidden * lax.rsqrt(mean + 1e-06) * gain_ref[...]).astype(halves)
 
-    loop(4, norm_rows)
-    mine, theirs = normed_ref.at[col], normed_ref.at[far]
-    to_far = remote(mine, mine, norm_send.at[0], norm_recv.at[0], (row, far))
-    to_near = remote(mine, mine, norm_send.at[1], norm_recv.at[1], (row, near))
-    to_far.start()
-    to_near.start()
-    remote(mine, theirs, norm_send.at[0], norm_recv.at[0], (row, far)).wait_recv()
-    onward = remote(theirs, theirs, norm_send.at[2], norm_recv.at[2], (row, near))
-    onward.start()
-    remote(mine, normed_ref.at[near], norm_send.at[1], norm_recv.at[1], (row, near)).wait_recv()
-    remote(mine, normed_ref.at[cross], norm_send.at[2], norm_recv.at[2], (row, near)).wait_recv()
-    to_far.wait_send()
-    to_near.wait_send()
-    onward.wait_send()
-    for turn in range(3):
-        block_copy(turn).wait_send()
-    for step in range(max(0, groups - slots), groups):
-        pair_copy(step).wait_send()
-    for step in range(max(0, groups - 1 - slots), groups - 1):
-        line_copy(step, True).wait_send()
+    def norm_copy(hop, i, block):
+        source = normed_ref.at[block, pl.ds(i * short, short)]
+        index = 2 * hop + i
+        return remote(
+            source, source, norm_send.at[index], norm_recv.at[index], (row, far if hop == 0 else near)
+        )
+
+    for i in range(2):
+        for turn, origin in enumerate((far, cross, near)):
+            block_copy(turn, i, origin).wait_recv()
+        norm_rows(2 * i)
+        norm_rows(2 * i + 1)
+        norm_copy(0, i, col).start()
+        norm_copy(1, i, col).start()
+    for i in range(2):
+        norm_copy(0, i, far).wait_recv()
+        norm_copy(2, i, far).start()
+    for i in range(2):
+        norm_copy(1, i, near).wait_recv()
+        norm_copy(2, i, cross).wait_recv()
+        for hop, block in enumerate((col, col, far)):
+            norm_copy(hop, i, block).wait_send()
+        for turn in range(3):
+            block_copy(turn, i).wait_send()
+        for step in range(max(0, groups - slots), groups):
+            pair_copy(step, i).wait_send()
+        for step in range(max(0, groups - 1 - slots), groups - 1):
+            line_copy(step, True, i).wait_send()
 
 
 def conv_forward(images_all, kernels, own, gain, width):
@@ -584,14 +605,14 @@
             pltpu.VMEM((3, rows, channels), halves),
             pltpu.VMEM((PIX, rows, channels), halves),
             DMA((2,)),
-            DMA((groups,)),
-            DMA((groups,)),
-            DMA((groups,)),
-            DMA((groups + 1,)),
-            DMA((3,)),
-            DMA((3,)),
-            DMA((3,)),
-            DMA((3,)),
+            DMA((groups, 2)),
+            DMA((groups, 2)),
+            DMA((groups, 2)),
+            DMA((groups + 1, 2)),
+            DMA((6,)),
+            DMA((6,)),
+            DMA((6,)),
+            DMA((6,)),
         ],
         compiler_params=params(1),
         name="conv_forward",
@@ -1086,6 +1107,60 @@
     )
 
 
+def group_copy(turn, source, landed, send, recv):
+    row, col = lax.axis_index("dp"), lax.axis_index("pix")
+    near, far, cross = peers(col)
+    target = (far, cross, near)[turn]
+    return remote(source, landed.at[turn], send.at[turn], recv.at[turn], (row, target))
+
+
+def group_sum(source, landed, send, recv):
+    col = lax.axis_index("pix")
+    _, far, cross = peers(col)
+    for turn in range(3):
+        group_copy(turn, source, landed, send, recv).wait()
+    landed[3] = source[...]
+    total = None
+    for which in range(PIX):
+        turn = jnp.where(
+            which == col, 3, jnp.where(which == far, 0, jnp.where(which == cross, 1, 2))
+        )
+        total = landed[turn] if total is None else total + landed[turn]
+    return total
+
+
+def far_copy_of(k, total, everyone, send, recv):
+    row, col = lax.axis_index("dp"), lax.axis_index("pix")
+    other = lax.rem(row + k, everyone.shape[0])
+    return remote(total, everyone.at[row], send.at[k], recv.at[k], (other, col))
+
+
+def far_start(total, everyone, send, recv, sem):
+    row, count = lax.axis_index("dp"), everyone.shape[0]
+    pltpu.make_async_copy(total, everyone.at[row], sem).start()
+    lax.fori_loop(
+        1, count, lambda k, c: (far_copy_of(k, total, everyone, send, recv).start(), c)[1], 0
+    )
+
+
+def far_end(total, everyone, send, recv, sem):
+    row, col = lax.axis_index("dp"), lax.axis_index("pix")
+    count = everyone.shape[0]
+    pltpu.make_async_copy(total, everyone.at[row], sem).wait()
+
+    def arrive(k, carry):
+        origin = lax.rem(row - k + count, count)
+        remote(
+            total, everyone.at[origin], send.at[k], recv.at[k], (row, flip(col, 1))
+        ).wait_recv()
+        return carry
+
+    lax.fori_loop(1, count, arrive, 0)
+    lax.fori_loop(
+        1, count, lambda k, c: (far_copy_of(k, total, everyone, send, recv).wait_send(), c)[1], 0
+    )
+
+
 def attend_back_kernel(
     grad_ref,
     query_ref,
@@ -1105,12 +1180,17 @@
     grad_attn_ref,
     normed_two_ref,
     grad_cross_ref,
+    rows_ref,
     attention_ref,
     others_ref,
     text_owned_ref,
     grad_one_ref,
     grad_conv_ref,
+    last_ref,
+    rows_all_ref,
     small_ref,
+    rows_in,
+    rows_sum,
     normed_ref,
     weight_ref,
     hidden_ref,
@@ -1169,6 +1249,11 @@
     attention_recv,
     landed_send,
     landed_recv,
+    rows_send,
+    rows_recv,
+    far_rows_send,
+    far_rows_recv,
+    rows_sem,
     *reduce_sems,
 ):
     row, col = lax.axis_index("dp"), lax.axis_index("pix")
@@ -1191,17 +1276,9 @@
     ]
     for load in loads:
         load.start()
-    barrier = pltpu.get_barrier_semaphore()
-
-    def hello(step, carry):
-        other = 2 * lax.rem(level + step, groups) + side
-        pl.semaphore_signal(barrier, inc=1, device_id=(other, col), device_id_type=MESH)
-        return carry
-
-    lax.fori_loop(1, groups, hello, 0)
-    for other in ((partner, col), (row, near), (row, far), (row, cross)):
-        pl.semaphore_signal(barrier, inc=1, device_id=other, device_id_type=MESH)
-    pl.semaphore_wait(barrier, groups - 1 + 4)
+    greet(2 * groups, [(row, near), (row, far), (row, cross)])
+    rows_group = (rows_ref, rows_in, rows_send, rows_recv)
+    rows_far = (rows_sum, rows_all_ref, far_rows_send, far_rows_recv, rows_sem)
     rows, full = hidden_ref.shape
     tokens, width = query_ref.shape
     heads = width // HEAD_DIM
@@ -1266,9 +1343,16 @@
         return to_side, middle, finish
 
     sides = reduction(0, reduced_ref, side_in, level_out, level_in)
-    outs = reduction(1, out_grad, out_side_in, out_level_out, out_level_in)
-    word = reduction(2, words_grad, words_side_in, words_level_out, words_level_in)
+    word = reduction(1, words_grad, words_side_in, words_level_out, words_level_in)
+    outs = [
+        reduction(
+            2 + w, out_grad.at[w], out_side_in.at[w], out_level_out.at[w], out_level_in.at[w]
+        )
+        for w in range(2)
+    ]
     sides[0]().start()
+    for turn in range(3):
+        group_copy(turn, *rows_group).start()
 
     def near_copy(which):
         return remote(
@@ -1317,23 +1401,22 @@
             loop(PIX, add)
             far_copy(which).start()
 
-    def out_end():
-        for which in range(2):
-            far_copy(which).wait_recv()
-
-            def add(i, which=which):
-                here = row_tile(i)
-                value = (
-                    near_kept[which, 0, here, :]
-                    + near_in[which, 0, here, :].astype(floats)
-                    + far_in[which, here, :].astype(floats)
-                ).astype(halves)
-                out_grad[pl.ds(i * per_tile, per_tile), :, :, which * width : (which + 1) * width] = (
-                    value.reshape(per_tile, 2, owned, width)
-                )
-
-            loop(PIX, add)
-        outs[0]().start()
+    def out_end(which):
+        far_copy(which).wait_recv()
+
+        def add(i):
+            here = row_tile(i)
+            value = (
+                near_kept[which, 0, here, :]
+                + near_in[which, 0, here, :].astype(floats)
+                + far_in[which, here, :].astype(floats)
+            ).astype(halves)
+            out_grad[which, pl.ds(i * per_tile, per_tile)] = value.reshape(
+                per_tile, 2, owned, width
+            )
+
+        loop(PIX, add)
+        outs[which][0]().start()
 
     def words_grads():
         text_total = text_grad_ref[col, 0:used, :].astype(floats)
@@ -1416,8 +1499,13 @@
             for load in loads:
                 load.wait()
             weight_grads(0)
+            rows_sum[...] = group_sum(*rows_group)
+            far_start(*rows_far)
         if h == 2:
             word[1]()
+            out_end(0)
+        if h == 3:
+            out_end(1)
 
     grads[col] = grad_ref[col]
     totals[...] = jnp.transpose(total_ref[...])
@@ -1505,10 +1593,10 @@
     pair_copy(1).wait_recv()
     norm_grad(col, store_own)
 
-    out_end()
     weight_grads(1)
     attention_level()
-    outs[1]()
+    outs[0][1]()
+    outs[1][1]()
     small_ref[...] = jnp.zeros_like(small_ref)
     part = 64
 
@@ -1555,7 +1643,11 @@
         conv_copy(turn, 1).wait_send()
         grad_copy(turn).wait_send()
         text_copy(turn).wait_send()
-    others_ref[:, 0 : 2 * width] = outs[2]()
+    for j in range(8):
+        last_ref[j : j + 1, :] = small_ref[0:1, j * 128 : (j + 1) * 128]
+    far_end(*rows_far)
+    for w in range(2):
+        others_ref[:, w * width : (w + 1) * width] = outs[w][2]()
     others_ref[:, 2 * width : 3 * width] = sides[2]()
     total = attention_out[level].astype(floats)
     for k in range(1, groups):
@@ -1578,6 +1670,7 @@
 
 def attend_backward(
     words,
+    small,
     grad,
     query,
     key,
@@ -1607,11 +1700,15 @@
             jax.ShapeDtypeStruct((owned, 2 * width), halves),
             jax.ShapeDtypeStruct((rows, full), floats),
             jax.ShapeDtypeStruct((PIX, rows, width), halves),
-            jax.ShapeDtypeStruct((8, full), floats),
+            jax.ShapeDtypeStruct((8, 128), floats),
+            jax.ShapeDtypeStruct((2 * groups,) + small.shape, floats),
         ),
-        in_specs=[VMEM] * 5 + [ANY] * 5 + [VMEM] * 8,
-        out_specs=(VMEM,) * 6,
+        in_specs=[VMEM] * 5 + [ANY] * 5 + [VMEM] * 9,
+        out_specs=(VMEM,) * 6 + (ANY,),
         scratch_shapes=[
+            pltpu.VMEM((8, full), floats),
+            pltpu.VMEM((4,) + small.shape, floats),
+            pltpu.VMEM(small.shape, floats),
             pltpu.VMEM(normed.shape, halves),
             pltpu.VMEM((full, 3 * width), halves),
             pltpu.VMEM((rows, full), floats),
@@ -1640,10 +1737,10 @@
             pltpu.VMEM((groups, owned, width), halves),
             pltpu.VMEM((groups, owned, width), halves),
             pltpu.VMEM((groups, owned, width), halves),
-            pltpu.VMEM((groups, 2, owned, 2 * width), halves),
-            pltpu.VMEM((groups, owned, 2 * width), halves),
-            pltpu.VMEM((groups, owned, 2 * width), halves),
-            pltpu.VMEM((groups, owned, 2 * width), halves),
+            pltpu.VMEM((2, groups, 2, owned, width), halves),
+            pltpu.VMEM((2, groups, owned, width), halves),
+            pltpu.VMEM((2, groups, owned, width), halves),
+            pltpu.VMEM((2, groups, owned, width), halves),
             pltpu.VMEM((groups, 2, owned, 2 * width), halves),
             pltpu.VMEM((groups, owned, 2 * width), halves),
             pltpu.VMEM((groups, owned, 2 * width), halves),
@@ -1670,8 +1767,13 @@
             DMA((2, PIX)),
             DMA((groups,)),
             DMA((groups,)),
+            DMA((3,)),
+            DMA((3,)),
+            DMA((2 * groups,)),
+            DMA((2 * groups,)),
+            DMA,
         ]
-        + [DMA, DMA, DMA((groups,)), DMA((groups,))] * 3,
+        + [DMA, DMA, DMA((groups,)), DMA((groups,))] * 4,
         compiler_params=params(3),
         name="attend_backward",
     )(
@@ -1690,6 +1792,7 @@
         text_grads,
         reduced,
         *factors,
+        small,
     )
 
 
@@ -1706,13 +1809,11 @@
     attention_ref,
     others_ref,
     words_ref,
-    small_ref,
     last_ref,
     bank_grad_ref,
     attention_all,
     others_all,
     words_all,
-    rows_all_ref,
     stats_all_ref,
     image_grad_ref,
     grads_ref,
@@ -1720,10 +1821,7 @@
     bank_ref,
     table_sem,
     stats_ref,
-    rows_out,
-    rows_in,
     stats_in,
-    rows_sum,
     stats_sum,
     image_buf,
     padded_image,
@@ -1760,15 +1858,10 @@
     attention_recv,
     weight_send,
     weight_recv,
-    rows_send,
-    rows_recv,
     stats_send,
     stats_recv,
-    far_rows_send,
-    far_rows_recv,
     far_stats_send,
     far_stats_recv,
-    rows_sem,
     stats_sem,
 ):
     row, col = lax.axis_index("dp"), lax.axis_index("pix")
@@ -1807,48 +1900,7 @@
         for hop in range(3):
             weight_copy(which, hop).wait_send()
 
-    def group_copy(turn, source, landed, send, recv):
-        return remote(source, landed.at[turn], send.at[turn], recv.at[turn], (row, targets[turn]))
-
-    def group_sum(source, landed, send, recv):
-        for turn in range(3):
-            group_copy(turn, source, landed, send, recv).wait()
-        landed[3] = source[...]
-        total = None
-        for which in range(PIX):
-            turn = jnp.where(
-                which == col, 3, jnp.where(which == far, 0, jnp.where(which == cross, 1, 2))
-            )
-            total = landed[turn] if total is None else total + landed[turn]
-        return total
-
-    def far_copy(k, total, everyone, send, recv):
-        return remote(
-            total, everyone.at[row], send.at[k], recv.at[k], (lax.rem(row + k, count), col)
-        )
-
-    def far_start(total, everyone, send, recv, sem):
-        pltpu.make_async_copy(total, everyone.at[row], sem).start()
-        lax.fori_loop(
-            1, count, lambda k, c: (far_copy(k, total, everyone, send, recv).start(), c)[1], 0
-        )
-
-    def far_end(total, everyone, send, recv, sem):
-        pltpu.make_async_copy(total, everyone.at[row], sem).wait()
-
-        def arrive(k, carry):
-            origin = lax.rem(row - k + count, count)
-            remote(total, everyone.at[origin], send.at[k], recv.at[k], (row, near)).wait_recv()
-            return carry
-
-        lax.fori_loop(1, count, arrive, 0)
-        lax.fori_loop(
-            1, count, lambda k, c: (far_copy(k, total, everyone, send, recv).wait_send(), c)[1], 0
-        )
-
-    rows_group = (rows_out, rows_in, rows_send, rows_recv)
     stats_group = (stats_ref, stats_in, stats_send, stats_recv)
-    rows_far = (rows_sum, rows_all_ref, far_rows_send, far_rows_recv, rows_sem)
     stats_far = (stats_sum, stats_all_ref, far_stats_send, far_stats_recv, stats_sem)
 
     def attention_copy(k):
@@ -1880,11 +1932,12 @@
     has_below, has_above = level > 0, level < groups - 1
     reach = jnp.minimum(level, groups - 1 - level)
 
-    def line_block(origin, upward):
+    def line_block(origin, upward, source=None):
         block = grads_ref.at[2 * origin + side]
         sem = (up_send if upward else down_send).at[origin]
         target = jnp.minimum(row + 2, count - 1) if upward else jnp.maximum(row - 2, 0)
-        return remote(block, block, sem, level_recv.at[origin], (target, col))
+        source = block if source is None else source
+        return remote(source, block, sem, level_recv.at[origin], (target, col))
 
     def relay(k):
         origin = level_at(level, groups, k)
@@ -1903,9 +1956,10 @@
 
         pair_copy(k).start()
 
-    def pair_copy(k):
+    def pair_copy(k, source=None):
         block = grads_ref.at[2 * level_at(level, groups, k) + side]
-        return remote(block, block, pair_send.at[k], pair_recv.at[k], (partner, col))
+        source = block if source is None else source
+        return remote(source, block, pair_send.at[k], pair_recv.at[k], (partner, col))
 
     def sums_copy(k):
         return remote(
@@ -1924,17 +1978,16 @@
     own.start()
     for load in loads:
         load.start()
-    own.wait()
 
     @pl.when(has_above)
     def _():
-        line_block(level, True).start()
+        line_block(level, True, grad_ref).start()
 
     @pl.when(has_below)
     def _():
-        line_block(level, False).start()
-
-    pair_copy(0).start()
+        line_block(level, False, grad_ref).start()
+
+    pair_copy(0, grad_ref).start()
 
     def fetch(step):
         slot = lax.rem(step, 2)
@@ -1945,12 +1998,8 @@
     fetch(0).start()
     others_all[col] = others_ref[...]
     words_all[col] = words_ref[...]
-    rows_out[...] = small_ref[...]
-    rows_out[5:6, :] = last_ref[0:1, :]
     for which in (1, 2):
         weight_start(which)
-    for turn in range(3):
-        group_copy(turn, *rows_group).start()
     products = jnp.zeros((8, channels), floats)
 
     def add_product(i, total):
@@ -1964,10 +2013,11 @@
     sums_in[row] = sums_out[...]
     acc[...] = jnp.zeros_like(acc)
     stats_ref[...] = jnp.zeros_like(stats_ref)
-    for buffer, lanes in ((padded_image, depth), (padded_grad, channels)):
-        zeros = jnp.zeros((3, halo, lanes), halves)
-        buffer[:, 0:halo, :] = zeros
-        buffer[:, halo + tokens : halo + tokens + halo, :] = zeros
+    stats_ref[3 * count :, :] = last_ref[...]
+    for buffer in (padded_image, padded_grad):
+        zeros = jnp.zeros((halo, buffer.shape[1]), halves)
+        buffer[0:halo, :] = zeros
+        buffer[halo + tokens : halo + tokens + halo, :] = zeros
 
     def sums_arrive(k, carry):
         origin = lax.rem(row - k + count, count)
@@ -1976,12 +2026,15 @@
         ).wait_recv()
         return carry
 
-    def fill(buffer, source):
+    def fill(source):
         wide = source.astype(floats)
         place = lax.rem(lax.broadcasted_iota(jnp.int32, wide.shape, 0), width)
         here = slice(halo, halo + tokens)
-        buffer[0, here, :] = jnp.where(place == 0, 0.0, pltpu.roll(wide, 1, 0)).astype(halves)
-        buffer[2, here, :] = jnp.where(
+        padded_image[here, 0:depth] = jnp.where(
+            place == 0, 0.0, pltpu.roll(wide, 1, 0)
+        ).astype(halves)
+        padded_image[here, depth : 2 * depth] = source
+        padded_image[here, 2 * depth : 3 * depth] = jnp.where(
             place == width - 1, 0.0, pltpu.roll(wide, tokens - 1, 0)
         ).astype(halves)
 
@@ -2036,7 +2089,7 @@
             relay(distance + reach)
 
         load = pltpu.make_async_copy(
-            grads_ref.at[sample], padded_grad.at[1, centre, :], load_sem
+            grads_ref.at[sample], padded_grad.at[centre, :], load_sem
         )
         load.start()
         fetch(step).wait()
@@ -2045,13 +2098,9 @@
         def _():
             fetch(step + 1).start()
 
-        image = image_buf[lax.rem(step, 2)]
-        padded_image[1, centre, :] = image
-        fill(padded_image, image)
+        fill(image_buf[lax.rem(step, 2)])
         load.wait()
-        grad = padded_grad[1, centre, :]
-        fill(padded_grad, grad)
-        turned[...] = jnp.transpose(grad)
+        turned[...] = jnp.transpose(padded_grad[centre, :])
         slot = lax.rem(step, 2)
 
         @pl.when(step >= 2)
@@ -2060,14 +2109,19 @@
 
         def through(target):
             start = pl.multiple_of(target * rows, rows)
-            total = jnp.zeros((rows, depth), floats)
+            total = jnp.zeros((rows, 3 * depth), floats)
             for a in range(3):
-                for b in range(3):
-                    window = padded_grad[
-                        2 - b, pl.ds(pl.multiple_of(start + (2 - a) * width, 16), rows), :
-                    ]
-                    total = total + mul_nt(window, kernel_ref[sample, 3 * a + b])
-            return total
+                window = padded_grad[pl.ds(pl.multiple_of(start + (2 - a) * width, 16), rows), :]
+                taps = kernel_ref[sample, 3 * a : 3 * a + 3].reshape(3 * depth, channels)
+                total = total + mul_nt(window, taps)
+            place = lax.rem(lax.broadcasted_iota(jnp.int32, (rows, depth), 0), width)
+            after = pltpu.roll(total[:, 0:depth], rows - 1, 0)
+            before = pltpu.roll(total[:, 2 * depth : 3 * depth], 1, 0)
+            return (
+                total[:, depth : 2 * depth]
+                + jnp.where(place == width - 1, 0.0, after)
+                + jnp.where(place == 0, 0.0, before)
+            )
 
         def give(i):
             pixel_out[slot, i] = through(jnp.where(i == 0, near, cross)).astype(halves)
@@ -2095,9 +2149,10 @@
         by_first = jnp.zeros((1, depth), floats)
         by_second = jnp.zeros((1, depth), floats)
         for a in range(3):
+            three = mul(turned[...], padded_image[pl.ds(a * width, tokens), :])
             for b in range(3):
                 tap = 3 * a + b
-                found = mul(turned[...], padded_image[b, pl.ds(a * width, tokens), :])
+                found = three[:, b * depth : (b + 1) * depth]
                 one, two = bank_ref[0, tap].astype(floats), bank_ref[1, tap].astype(floats)
                 selected = first * one + second * two
                 modded = inverse * found - factor * (selected * scale)
@@ -2107,9 +2162,8 @@
                 acc[1, tap] += second * grad_selected
                 by_first = by_first + jnp.sum(grad_selected * one, 0, keepdims=True)
                 by_second = by_second + jnp.sum(grad_selected * two, 0, keepdims=True)
-        stats_ref[sample, 0:1, :depth] = by_scale
-        stats_ref[sample, 1:2, :depth] = by_first
-        stats_ref[sample, 2:3, :depth] = by_second
+        for k, line in enumerate((by_scale, by_first, by_second)):
+            stats_ref[pl.ds(k * count + sample, 1), :depth] = line
 
     def across(step):
         slot = lax.rem(step, 2)
@@ -2145,6 +2199,7 @@
 
     lax.fori_loop(1, count, sums_arrive, 0)
 
+    own.wait()
     for load in loads:
         load.wait()
 
@@ -2153,8 +2208,6 @@
         def _():
             for which in (1, 2):
                 weight_pass(which)
-            rows_sum[...] = group_sum(*rows_group)
-            far_start(*rows_far)
 
         @pl.when(step == count - 2)
         def _():
@@ -2207,7 +2260,6 @@
 
     lax.fori_loop(1, count, owner_arrives, 0)
     weight_pass(0)
-    far_end(*rows_far)
     far_end(*stats_far)
     for which in (1, 2, 0):
         weight_end(which)
@@ -2230,9 +2282,8 @@
     lax.fori_loop(1, count, lambda k, c: (sums_copy(k).wait_send(), c)[1], 0)
 
 
-def conv_backward(images_all, kernels, bank, styles, inverse, grad, conv, owned, rows_here, width):
+def conv_backward(images_all, kernels, bank, styles, inverse, grad, conv, owned, last, width):
     attention, others, words = owned
-    small, last = rows_here
     count, tokens, depth = images_all.shape
     channels = grad.shape[1]
     rows = tokens // PIX
@@ -2245,26 +2296,22 @@
             jax.ShapeDtypeStruct((PIX,) + attention.shape[1:], halves),
             jax.ShapeDtypeStruct((PIX,) + others.shape, halves),
             jax.ShapeDtypeStruct((PIX,) + words.shape, halves),
-            jax.ShapeDtypeStruct((count,) + small.shape, floats),
-            jax.ShapeDtypeStruct((count, count, 8, 128), floats),
+            jax.ShapeDtypeStruct((count, 3 * count + 8, 128), floats),
             jax.ShapeDtypeStruct((count,) + piece, halves),
             jax.ShapeDtypeStruct((count, tokens, channels), halves),
         ),
-        in_specs=[ANY] * 3 + [VMEM] * 9,
-        out_specs=(VMEM,) * 4 + (ANY,) * 4,
+        in_specs=[ANY] * 3 + [VMEM] * 8,
+        out_specs=(VMEM,) * 4 + (ANY,) * 3,
         scratch_shapes=[
             pltpu.VMEM(kernels.shape, halves),
             pltpu.VMEM(bank.shape, halves),
             DMA((2,)),
-            pltpu.VMEM((count, 8, 128), floats),
-            pltpu.VMEM(small.shape, floats),
-            pltpu.VMEM((4,) + small.shape, floats),
-            pltpu.VMEM((4, count, 8, 128), floats),
-            pltpu.VMEM(small.shape, floats),
-            pltpu.VMEM((count, 8, 128), floats),
+            pltpu.VMEM((3 * count + 8, 128), floats),
+            pltpu.VMEM((4, 3 * count + 8, 128), floats),
+            pltpu.VMEM((3 * count + 8, 128), floats),
             pltpu.VMEM((2, tokens, depth), halves),
-            pltpu.VMEM((3, tokens + 2 * width, depth), halves),
-            pltpu.VMEM((3, tokens + 2 * width, channels), halves),
+            pltpu.VMEM((tokens + 2 * width, 3 * depth), halves),
+            pltpu.VMEM((tokens + 2 * width, channels), halves),
             pltpu.VMEM((channels, tokens), halves),
             pltpu.VMEM((2, 9, channels, depth), floats),
             pltpu.VMEM((8, channels), floats),
@@ -2299,13 +2346,8 @@
             DMA((9,)),
             DMA((3,)),
             DMA((3,)),
-            DMA((3,)),
-            DMA((3,)),
             DMA((count,)),
             DMA((count,)),
-            DMA((count,)),
-            DMA((count,)),
-            DMA,
             DMA,
         ],
         compiler_params=params(4),
@@ -2321,7 +2363,6 @@
         attention,
         others,
         words,
-        small,
         last,
     )
 
@@ -2443,7 +2484,7 @@
     for d in range(count):
         lanes = slice(d * depth, (d + 1) * depth)
         grad_image_ref[:, lanes] = grad_one_ref[:, lanes] + image_parts_ref[d].astype(floats)
-        scaling[:, lanes] = stats_ref[d, :, 0, :][:, :depth]
+        scaling[:, lanes] = stats_ref[d, 0:count, 0:depth]
     for k, out in enumerate((grad_query_ref, grad_key_ref, grad_value_ref)):
         for p in range(2 * PIX):
             first = 3 * width + k * 128 if p % 2 == 0 else k * 128
@@ -2460,14 +2501,17 @@
     sums = rows_ref[0]
     for d in range(1, count):
         sums = sums + rows_ref[d]
-    gain_self_ref[...] = sums[5:6]
+    total = stats_ref[0, 3 * count :, :]
+    for d in range(1, count):
+        total = total + stats_ref[d, 3 * count :, :]
+    gain_self_ref[...] = total
     gain_cross_ref[...] = sums[0:1]
     rgb_weight_ref[...] = sums[2:5]
     mixing, grads = [], []
     for k in (1, 2):
-        total = stats_ref[0, :, k, :]
+        total = stats_ref[0, k * count : (k + 1) * count, :]
         for d in range(1, count):
-            total = total + stats_ref[d, :, k, :]
+            total = total + stats_ref[d, k * count : (k + 1) * count, :]
         grads.append(jnp.sum(total, -1, keepdims=True))
         mixing.append(styles_ref[:, k, :][:, 0:1])
     inner = grads[0] * mixing[0] + grads[1] * mixing[1]
@@ -2529,7 +2573,7 @@
             out(2, wide),
             out(wide, channels),
             out(wide, channels),
-            out(1, channels),
+            out(8, channels // 8),
             out(1, channels),
             out(3, channels),
         ),
@@ -2640,8 +2684,17 @@
         rgb_rows,
         penalty,
     )
-    attention_grads, others_owned, words_owned, grad_one, grad_conv, last = attend_backward(
+    (
+        attention_grads,
+        others_owned,
+        words_owned,
+        grad_one,
+        grad_conv,
+        last,
+        all_rows,
+    ) = attend_backward(
         words,
+        small,
         grad_attended,
         query,
         key,
@@ -2659,7 +2712,7 @@
         *factors,
     )
 
-    bank_grad, *gathered, all_rows, all_stats, image_parts, _ = conv_backward(
+    bank_grad, *gathered, all_stats, image_parts, _ = conv_backward(
         images_all,
         kernels,
         bank_turned,
@@ -2668,7 +2721,7 @@
         grad_conv.reshape(PIX * rows, quarter),
         conv_own,
         (attention_grads, others_owned, words_owned),
-        (small, last),
+        last,
         width,
     )
     (

time: 413 us -> 402 us (0.973)
  Pallas kernels: 381 us -> 370 us
    pallas_call x1, Pallas kernels: 87.3 us -> 79.5 us  [conv_backward(): pl.pallas_call(partial(conv_back_kernel, count, width), out_shape=(jax.Sh...]
    pallas_call x1, Pallas kernels: 108 us -> 103 us  [conv_forward(): pl.pallas_call(partial(conv_kernel, count, width), out_shape=(jax.ShapeDt...]
where the time goes in v4:
time: 402 us; the launch traced here: 401 us
  Pallas kernels  370 us (92%)
  between operations  15.5 us (4%)
  local copies, waits for them, and re-layouts  11.8 us (3%)
    pallas_call x1, Pallas kernels, conv_forward(): pl.pallas_call(partial(conv_kernel, count, width), out_shape=(jax.ShapeDt...  103 us
    pallas_call x1, Pallas kernels, conv_backward(): pl.pallas_call(partial(conv_back_kernel, count, width), out_shape=(jax.Sh...  79.5 us
    pallas_call x1, Pallas kernels, attend_backward(): pl.pallas_call(attend_back_kernel, out_shape=(jax.ShapeDtypeStruct((group...  74.2 us
    pallas_call x1, Pallas kernels, cross_part(): pl.pallas_call(partial(cross_kernel, words), out_shape=(jax.ShapeDtypeStr...  41.9 us
    pallas_call x1, Pallas kernels, gather_inputs(): pl.pallas_call(partial(gather_kernel, count), out_shape=(jax.ShapeDtypeSt...  37.1 us
    pallas_call x1, Pallas kernels, attend_forward(): pl.pallas_call(attend_kernel, out_shape=(flat, flat, flat, jax.ShapeDtype...  22.4 us
    pallas_call x1, Pallas kernels, finish(): pl.pallas_call(finish_kernel, out_shape=(out(owned, channels),) * 6 + (ou...  8.26 us
  transfers between devices with their start and end apart: 2, of which 0 were waited for; matrix products, arithmetic and copies ran while one was open for 2% of the time, Pallas kernels for 41%

profile of v4, /device:TPU:0, one launch (start us, length us, event | category | flops | bytes accessed | tf_op | source)
XLA Modules:
  0.0 401.2 jit_solution(7536728818153388074)
XLA Ops:
  7.9 1.3 pad_convert_fusion.select_ref
  9.2 1.3 fusion.1.styled_ref
  10.5 0.5 broadcast_in_dim.40.label_ref
  11.0 3.7 prepare.1
  14.8 0.7 all-gather.5.cloned.1.call-update
  15.5 3.5 gather_fusion
  19.1 0.2 gather.12
  19.3 0.1 broadcast_select_fusion
  19.5 0.8 copy.52
  20.2 0.2 copy.46
  20.4 0.8 pad.18.rgb_weight_ref
  22.0 1.4 copy.44
  23.4 0.7 pad.19.rgb_cotangent_ref
  24.1 37.1 %gather_inputs.1 = (bf16[8,4,256,128]{3,2,1,0:T(8,128)(2,1)}, bf16[8,9,128,256]{3,2,1,0:T(8,128)(2,1)}, f32[8,8,128]{2,1,0:T(8,128)}, f32[8,256]{1,0:T(8,128)}) custom-call(f32[8,8,128]{2,1,0:T(8,128)} %get-tuple-element.80.style_ref, bf16[2,9,128,256]{3,2,1,0:T(8,128)(2,1)} %bitcast.44, bf16[8,256,128]{2,1,0:T(8,128)(2,1)} %get-tuple-element.81.parts_ref), custom_call_target="tpu_custom_call" | custom-call | tf_op jit(solution)/shard_map/gather_inputs/pallas_call | solution.py:258
  61.2 103.3 %conv_forward.1 = (bf16[256,1024]{1,0:T(8,128)(2,1)}, bf16[1024,256]{1,0:T(8,128)(2,1)}, f32[256,1024]{1,0:T(8,128)}, bf16[4,256,1024]{2,1,0:T(8,128)(2,1)}) custom-call(bf16[8,1024,128]{2,1,0:T(8,128)(2,1)} %bitcast.41, bf16[8,9,128,256]{3,2,1,0:T(8,128)(2,1)} %get-tuple-element.83.kernel_ref.kernel_from, bf16[256,1024]{1,0:T(8,128)(2,1)} %bitcast.50, ...), custom_call_target="tpu_custom_call" | custom-call | tf_op jit(solution)/shard_map/conv_forward/pallas_call | solution.py:587
  164.5 22.4 %attend_forward.1 = (bf16[1024,256]{1,0:T(8,128)(2,1)}, bf16[1024,256]{1,0:T(8,128)(2,1)}, bf16[1024,256]{1,0:T(8,128)(2,1)}, f32[1024,128]{1,0:T(8,128)}, bf16[...) custom-call(bf16[4,256,1024]{2,1,0:T(8,128)(2,1)} %get-tuple-element.84.normed_ref.normed_from, ...), custom_call_target="tpu_custom_call" | custom-call | tf_op jit(solution)/shard_map/attend_forward/pallas_call | solution.py:779
  186.9 0.5 broadcast_in_dim.44.penalty_ref
  187.4 41.9 %cross_part.1 = (f32[256,1024]{1,0:T(8,128)}, f32[256,128]{1,0:T(8,128)}, bf16[1024,256]{1,0:T(8,128)(2,1)}, bf16[4,128,512]{2,1,0:T(8,128)(2,1)}, f32[256,1024]...) custom-call(bf16[4,256,256]{2,1,0:T(8,128)(2,1)} %get-tuple-element., ...), custom_call_target="tpu_custom_call" | custom-call | tf_op jit(solution)/shard_map/cross_part/pallas_call | solution.py:1060
  229.3 74.2 %attend_backward.1 = (bf16[4,128,384]{2,1,0:T(8,128)(2,1)}, bf16[128,1152]{1,0:T(8,128)(2,1)}, bf16[128,512]{1,0:T(8,128)(2,1)}, f32[256,1024]{1,0:T(8,128)}, bf...) custom-call(bf16[4,256,256]{2,1,0:T(8,128)(2,1)} %get-tuple-element.93.grad_ref, ...), custom_call_target="tpu_custom_call" | custom-call | tf_op jit(solution)/shard_map/attend_backward/pallas_call | solution.py:1695
  303.5 79.5 %conv_backward.1 = (f32[2,9,128,256]{3,2,1,0:T(8,128)}, bf16[4,128,384]{2,1,0:T(8,128)(2,1)}, bf16[4,128,1152]{2,1,0:T(8,128)(2,1)}, bf16[4,128,512]{2,1,0:T(8,1...) custom-call(bf16[8,1024,128]{2,1,0:T(8,128)(2,1)} %bitcast.42, ...), custom_call_target="tpu_custom_call" | custom-call | tf_op jit(solution)/shard_map/conv_backward/pallas_call | solution.py:2292
  383.0 0.7 copy.48
  383.7 8.3 %finish.1 = (f32[128,1024]{1,0:T(8,128)}, f32[128,1024]{1,0:T(8,128)}, f32[128,1024]{1,0:T(8,128)}, f32[128,1024]{1,0:T(8,128)}, f32[128,1024]{1,0:T(8,128)}, /*...) custom-call(f32[8,8,1024]{2,1,0:T(8,128)} %get-tuple-element.107.row, ...), custom_call_target="tpu_custom_call" | custom-call | tf_op jit(solution)/shard_map/finish/pallas_call | solution.py:2565
  392.0 1.0 copy.57
  392.9 1.4 copy.58
  (24 shorter events, 0.4 us)
Async XLA Ops:
  7.2 157.3 %all-gather.3.cloned.1.call-start = ((), (), s32[]{:S(2)}) async-start(), calls=%async_computation | async-start | bytes 2949120 | tf_op jit(solution)/shard_map/all_gather | solution.py:2646
  11.0 4.5 %copy-start.6 = (s32[1,77]{1,0:T(1,128)S(1)}, s32[1,77]{1,0:T(1,128)}, u32[]{:S(2)}) copy-start(s32[1,77]{1,0:T(1,128)} %param.27) | copy-start | bytes 928
  14.7 5.5 %copy-start.5 = (bf16[1024,3]{0,1:T(4,128)(2,1)S(1)}, bf16[1024,3]{0,1:T(4,128)(2,1)}, u32[]{:S(2)}) copy-start(bf16[1024,3]{0,1:T(4,128)(2,1)} %param.45) | copy-start | bytes 18436
  14.7 6.5 %copy-start.4 = (f32[1,3,8,32]{3,2,1,0:T(8,128)S(1)}, f32[1,3,8,32]{3,2,1,0:T(8,128)}, u32[]{:S(2)}) copy-start(f32[1,3,8,32]{3,2,1,0:T(8,128)} %param.47) | copy-start | bytes 9220
  14.7 7.3 %copy-start = (bf16[2,3,3,128,256]{4,3,2,1,0:T(8,128)(2,1)S(1)}, bf16[2,3,3,128,256]{4,3,2,1,0:T(8,128)(2,1)}, u32[]{:S(2)}) copy-start(bf16[2,3,3,128,256]{4,3,2,1,0:T(8,128)(2,1)} %param.31) | copy-start | bytes 3538948
  14.7 172.2 %all-gather.5.cloned.1.call-start = ((), (), s32[]{:S(2)}) async-start(), calls=%async_computation.1 | async-start | bytes 6488064 | tf_op jit(solution)/shard_map/all_gather | solution.py:2647
  303.5 79.5 %copy-start.3 = (f32[256,128]{1,0:T(8,128)S(1)}, f32[256,128]{1,0:T(8,128)}, u32[]{:S(2)}) copy-start(f32[256,128]{1,0:T(8,128)} %get-tuple-element.92) | copy-start | bytes 393220
  383.7 8.3 %copy-start.2 = (f32[256,1024]{1,0:T(8,128)S(1)}, f32[256,1024]{1,0:T(8,128)}, u32[]{:S(2)}) copy-start(f32[256,1024]{1,0:T(8,128)} %get-tuple-element.91) | copy-start | bytes 3145732
  383.7 9.3 %copy-start.1 = (f32[2,9,128,256]{3,2,1,0:T(8,128)S(1)}, f32[2,9,128,256]{3,2,1,0:T(8,128)}, u32[]{:S(2)}) copy-start(f32[2,9,128,256]{3,2,1,0:T(8,128)} %get-tuple-element.125) | copy-start | bytes 7077892
Sparse Core Ops, SparseCore 0:
  14.9 70.8 all-gather.2
  89.3 78.6 all-gather.4

commit v5 on v4

--- a/solution.py
+++ b/solution.py
@@ -280,13 +280,15 @@
     count,
     width,
     images_ref,
-    kernel_ref,
+    kernel_from,
     own_ref,
     gain_ref,
     conv_ref,
     conv_own_ref,
     hidden_ref,
     normed_ref,
+    kernel_ref,
+    kernel_sem,
     image_buf,
     padded,
     total,
@@ -319,6 +321,8 @@
     rows = tokens // PIX
     halo = width
 
+    load = pltpu.make_async_copy(kernel_from, kernel_ref, kernel_sem)
+    load.start()
     has_below, has_above = level > 0, level < groups - 1
     below, above = jnp.maximum(row - 2, 0), jnp.minimum(row + 2, count - 1)
 
@@ -347,6 +351,7 @@
             images_ref.at[sample_of(index)], image_buf.at[slot], image_sem.at[slot]
         )
 
+    load.wait()
     zeros = jnp.zeros((3, halo, depth), halves)
     padded[:, 0:halo, :] = zeros
     padded[:, halo + tokens : halo + tokens + halo, :] = zeros
@@ -592,9 +597,11 @@
             jax.ShapeDtypeStruct((rows, full), floats),
             jax.ShapeDtypeStruct((PIX, rows, full), halves),
         ),
-        in_specs=[ANY, VMEM, VMEM, VMEM],
+        in_specs=[ANY, ANY, VMEM, VMEM],
         out_specs=(VMEM, VMEM, VMEM, VMEM),
         scratch_shapes=[
+            pltpu.VMEM(kernels.shape, halves),
+            DMA,
             pltpu.VMEM((2, tokens, depth), halves),
             pltpu.VMEM((3, tokens + 2 * width, depth), halves),
             pltpu.VMEM(block, floats),
@@ -670,8 +677,8 @@
 
 
 def attend_kernel(
-    normed_ref,
-    weight_ref,
+    normed_from,
+    weight_from,
     text_ref,
     query_ref,
     key_ref,
@@ -679,6 +686,9 @@
     total_ref,
     attended_ref,
     text_out_ref,
+    normed_ref,
+    weight_ref,
+    load_sem,
     block_out,
     key_norm,
     block_send,
@@ -689,7 +699,15 @@
     row, col = lax.axis_index("dp"), lax.axis_index("pix")
     near, far, cross = peers(col)
     targets = (far, cross, near)
+    loads = [
+        pltpu.make_async_copy(weight_from, weight_ref, load_sem.at[0]),
+        pltpu.make_async_copy(normed_from, normed_ref, load_sem.at[1]),
+    ]
+    for load in loads:
+        load.start()
     greet_pixels(row, targets)
+    for load in loads:
+        load.wait()
     rows = normed_ref.shape[1]
     width = query_ref.shape[1]
     heads = width // HEAD_DIM
@@ -717,14 +735,14 @@
     ones = jnp.ones((8, HEAD_DIM), floats)
     for h in range(heads):
         key = key_ref[:, h * HEAD_DIM : (h + 1) * HEAD_DIM].astype(floats)
-        key_norm[h] = mul_nt(ones, key * key, highest)
+        key_norm[h] = score_scale * mul_nt(ones, key * key, highest)
 
     def attend(target, store):
         here = pl.ds(pl.multiple_of(target * rows, rows), rows)
         for h in range(heads):
             lanes = slice(h * HEAD_DIM, (h + 1) * HEAD_DIM)
             inner = mul_nt(query_ref[here, lanes], key_ref[:, lanes])
-            scores = score_scale * (2.0 * inner - key_norm[h, 0:1, :])
+            scores = (2.0 * score_scale) * inner - key_norm[h, 0:1, :]
             largest = jnp.max(scores, -1, keepdims=True)
             expanded = jnp.exp(scores - largest)
             summed = jnp.sum(expanded, -1, keepdims=True)
@@ -786,9 +804,12 @@
             jax.ShapeDtypeStruct((PIX, rows, width), halves),
             jax.ShapeDtypeStruct((PIX, text.shape[0], 2 * width), halves),
         ),
-        in_specs=[VMEM] * 3,
+        in_specs=[ANY, ANY, VMEM],
         out_specs=(VMEM,) * 6,
         scratch_shapes=[
+            pltpu.VMEM(normed.shape, halves),
+            pltpu.VMEM(weights.shape, halves),
+            DMA((2,)),
             pltpu.VMEM((4, rows, width), halves),
             pltpu.VMEM((heads, 8, tokens), floats),
             DMA((3,)),
@@ -805,7 +826,7 @@
     words,
     attended_ref,
     hidden_ref,
-    weight_ref,
+    weight_from,
     text_ref,
     gain_ref,
     rgb_scale_ref,
@@ -833,6 +854,8 @@
     grad_proj,
     grad_crossed,
     grad_norm,
+    weight_ref,
+    weight_sem,
     near_out,
     near_in,
     kept,
@@ -845,9 +868,18 @@
 ):
     row, col = lax.axis_index("dp"), lax.axis_index("pix")
     near, far, cross = peers(col)
-    greet_pixels(row, (near, far))
     rows, full = hidden_ref.shape
     tile = full // PIX
+    loads = []
+    for i in range(3):
+        lanes = pl.ds(i * tile, tile)
+        loads.append(
+            pltpu.make_async_copy(
+                weight_from.at[:, :, lanes], weight_ref.at[:, :, lanes], weight_sem.at[i]
+            )
+        )
+        loads[i].start()
+    greet_pixels(row, (near, far))
     score_scale = HEAD_DIM ** (-0.5)
     W_OUT, C_QUERY, C_OUT = (slice(i * tile, (i + 1) * tile) for i in range(3))
     part = 64
@@ -915,6 +947,7 @@
     def out_two(j):
         two[:, cols(j)] = hidden_ref[:, cols(j)] + mul(attended[...], weight_ref[j, :, W_OUT])
 
+    loads[0].wait()
     loop(PIX, out_two)
 
     def norm_two(i):
@@ -928,6 +961,7 @@
     def out_query(j):
         query[:, cols(j)] = mul(normed[...], weight_ref[j, :, C_QUERY]).astype(halves)
 
+    loads[1].wait()
     loop(PIX, out_query)
     slots = text_ref.shape[1]
     known = lax.broadcasted_iota(jnp.int32, (rows, slots), 1) < words
@@ -967,6 +1001,7 @@
         mixed[:, cols(j)] = blend
         rgb_ref[...] += mul(blend, rgb_weight_ref[cols(j), :])
 
+    loads[2].wait()
     loop(PIX, out_three)
     rgb_grad = rgb_cotangent_ref[...] + penalty_weight * penalty_ref[...] * rgb_ref[...]
 
@@ -992,6 +1027,7 @@
         grad_crossed[:, cols(j)] = times_transposed(grad_proj, j, C_OUT).astype(halves)
 
     loop(PIX, back_crossed)
+    pass_grad(0)
 
     def back_pair(pair):
         here = pl.ds(pl.multiple_of(pair * 128, 128), 128)
@@ -1019,7 +1055,6 @@
         back_pair(2 * i + 1)
 
     loop(full // 256, back_four)
-    pass_grad(0)
 
     def back_query(j):
         grad_norm[:, cols(j)] = times_transposed(grad_query, j, C_QUERY)
@@ -1069,7 +1104,7 @@
             jax.ShapeDtypeStruct((8, full), floats),
         )
         + (jax.ShapeDtypeStruct((rows, full), halves),) * 4,
-        in_specs=[VMEM] * 10,
+        in_specs=[VMEM, VMEM, ANY] + [VMEM] * 7,
         out_specs=(VMEM,) * 11,
         scratch_shapes=[
             wide,
@@ -1081,6 +1116,8 @@
             slim,
             slim,
             wide,
+            pltpu.VMEM(weights.shape, halves),
+            DMA((3,)),
             pltpu.VMEM((1, 2, full, tile), halves),
             pltpu.VMEM((1, 2, full, tile), halves),
             pltpu.VMEM((1, 2, full, tile), floats),
@@ -1506,6 +1543,7 @@
             out_end(0)
         if h == 3:
             out_end(1)
+            attention_level()
 
     grads[col] = grad_ref[col]
     totals[...] = jnp.transpose(total_ref[...])
@@ -1594,7 +1632,6 @@
     norm_grad(col, store_own)
 
     weight_grads(1)
-    attention_level()
     outs[0][1]()
     outs[1][1]()
     small_ref[...] = jnp.zeros_like(small_ref)
@@ -1819,6 +1856,7 @@
     grads_ref,
     kernel_ref,
     bank_ref,
+    bank_raw,
     table_sem,
     stats_ref,
     stats_in,
@@ -1972,7 +2010,7 @@
 
     loads = [
         pltpu.make_async_copy(kernel_from, kernel_ref, table_sem.at[0]),
-        pltpu.make_async_copy(bank_from, bank_ref, table_sem.at[1]),
+        pltpu.make_async_copy(bank_from, bank_raw, table_sem.at[1]),
     ]
     own = pltpu.make_async_copy(grad_ref, grads_ref.at[row], local_sem)
     own.start()
@@ -2203,6 +2241,12 @@
     for load in loads:
         load.wait()
 
+    def turn_bank(index):
+        i, j = lax.div(index, 9), lax.rem(index, 9)
+        bank_ref[i, j] = jnp.transpose(bank_raw[i, j].astype(floats)).astype(halves)
+
+    loop(18, turn_bank)
+
     def step_body(step):
         @pl.when(step == 2)
         def _():
@@ -2304,6 +2348,7 @@
         out_specs=(VMEM,) * 4 + (ANY,) * 3,
         scratch_shapes=[
             pltpu.VMEM(kernels.shape, halves),
+            pltpu.VMEM((2, 9, channels, depth), halves),
             pltpu.VMEM(bank.shape, halves),
             DMA((2,)),
             pltpu.VMEM((3 * count + 8, 128), floats),
@@ -2401,7 +2446,7 @@
     for k, source in enumerate((out_ref, cross_query_ref, cross_out_ref)):
         others_ref[:, k * width : (k + 1) * width] = source[:, mine]
     styled = styled_ref[...]
-    logits = jnp.sum(styled * select_ref[...], -1, keepdims=True)
+    logits = jnp.sum(styled * select_ref[...].astype(floats), -1, keepdims=True)
     first, second = logits[0:1], logits[1:2]
     largest = jnp.maximum(first, second)
     first, second = jnp.exp(first - largest), jnp.exp(second - largest)
@@ -2416,7 +2461,7 @@
     same = jnp.concatenate(
         [jnp.broadcast_to(first / total, (1, 128)), jnp.broadcast_to(second / total, (1, 128))]
         + [styled[:, k * 128 : (k + 1) * 128] for k in range(4)]
-        + [label_ref[...]],
+        + [jnp.full((1, 128), label_ref[0, 0].astype(floats))],
         axis=0,
     )
     for d in range(count):
@@ -2439,7 +2484,7 @@
             jax.ShapeDtypeStruct((1, channels), floats),
             jax.ShapeDtypeStruct((count, rows, channels // count), halves),
         ),
-        in_specs=[VMEM] * 14,
+        in_specs=[VMEM, pl.BlockSpec(memory_space=pltpu.SMEM)] + [VMEM] * 12,
         out_specs=(VMEM,) * 5,
         compiler_params=pltpu.CompilerParams(vmem_limit_bytes=VMEM_LIMIT),
         name="prepare",
@@ -2523,11 +2568,12 @@
     place = lax.broadcasted_iota(jnp.int32, (count, 128), 1)
     both = jnp.where(place == 0, logits[0], jnp.where(place == 1, logits[1], 0.0))
     grad_select_ref[...] = outer_sum(both, styled)[0:2]
+    select = select_ref[...].astype(floats)
     grad_styles = (
         exact(mul_nt, scaling[...], modulation_ref[...])
         + exact(mul_nt, rgb, rgb_modulation_ref[...])
-        + logits[0] * select_ref[0:1, :]
-        + logits[1] * select_ref[1:2, :]
+        + logits[0] * select[0:1]
+        + logits[1] * select[1:2]
     )
     styles_grad[...] = grad_styles
     grad_style_ref[...] = styles_grad[pl.ds(row, 1), :]
@@ -2630,8 +2676,8 @@
     owned, text_owned = w_query.shape[0], c_key.shape[0]
     class_row = jnp.take(class_table, labels, axis=0).astype(floats)
     styled = style_codes.astype(floats) + class_row
-    label = jnp.broadcast_to(labels.astype(floats).reshape(1, 1), (1, 128))
-    select_rows = jnp.pad(select_weight.T, ((0, 6), (0, 0))).astype(floats)
+    label = labels.reshape(1, 1)
+    select_rows = select_weight.T
     own = images.reshape(rows, channels)
     attention, others, style, rgb_scale, parts = prepare(
         styled,
@@ -2647,7 +2693,6 @@
     others = lax.all_gather(others, ("pix", "dp"), axis=0, tiled=True)
     others = others.reshape(PIX, channels, 3 * quarter)
     bank = conv_bank.reshape(2, 9, depth, quarter)
-    bank_turned = bank.transpose(0, 1, 3, 2)
     words = token_ids.shape[1]
     text = jnp.take(text_table, token_ids[0], axis=0)
     text = text.reshape(words, count, text_owned)
@@ -2715,7 +2760,7 @@
     bank_grad, *gathered, all_stats, image_parts, _ = conv_backward(
         images_all,
         kernels,
-        bank_turned,
+        bank,
         styles,
         inverse,
         grad_conv.reshape(PIX * rows, quarter),

time: 402 us -> 389 us (0.968)
  Pallas kernels: 370 us -> 359 us
    pallas_call x1, Pallas kernels: 103 us -> 97.7 us  [conv_forward(): pl.pallas_call(partial(conv_kernel, count, width), out_shape=(jax.ShapeDt...]
    pallas_call x1, Pallas kernels: 41.9 us -> 36.7 us  [cross_part(): pl.pallas_call(partial(cross_kernel, words), out_shape=(jax.ShapeDtypeStr...]
where the time goes in v5:
time: 389 us; the launch traced here: 388 us
  Pallas kernels  359 us (92%)
  between operations  15.5 us (4%)
  local copies, waits for them, and re-layouts  10.8 us (3%)
    pallas_call x1, Pallas kernels, conv_forward(): pl.pallas_call(partial(conv_kernel, count, width), out_shape=(jax.ShapeDt...  97.7 us
    pallas_call x1, Pallas kernels, conv_backward(): pl.pallas_call(partial(conv_back_kernel, count, width), out_shape=(jax.Sh...  81.7 us
    pallas_call x1, Pallas kernels, attend_backward(): pl.pallas_call(attend_back_kernel, out_shape=(jax.ShapeDtypeStruct((group...  70.7 us
    pallas_call x1, Pallas kernels, gather_inputs(): pl.pallas_call(partial(gather_kernel, count), out_shape=(jax.ShapeDtypeSt...  38.5 us
    pallas_call x1, Pallas kernels, cross_part(): pl.pallas_call(partial(cross_kernel, words), out_shape=(jax.ShapeDtypeStr...  36.7 us
    pallas_call x1, Pallas kernels, attend_forward(): pl.pallas_call(attend_kernel, out_shape=(flat, flat, flat, jax.ShapeDtype...  22 us
    pallas_call x1, Pallas kernels, finish(): pl.pallas_call(finish_kernel, out_shape=(out(owned, channels),) * 6 + (ou...  8.29 us
  transfers between devices with their start and end apart: 2, of which 0 were waited for; matrix products, arithmetic and copies ran while one was open for 2% of the time, Pallas kernels for 41%

profile of v5, /device:TPU:0, one launch (start us, length us, event | category | flops | bytes accessed | tf_op | source)
XLA Modules:
  0.0 388.1 jit_solution(9449254184222023681)
XLA Ops:
  7.2 0.0 all-gather.3.cloned.1.call-start
  7.9 1.3 fusion.1.styled_ref
  9.2 3.7 prepare.1
  12.9 0.0 all-gather.5.cloned.1.call-start
  13.0 0.7 all-gather.5.cloned.1.call-update
  14.4 3.6 gather_fusion
  17.9 0.2 gather.12
  18.1 0.2 broadcast_select_fusion
  18.3 0.8 copy.49
  19.1 0.1 copy.45
  19.2 0.2 copy.44
  19.4 0.8 pad.13.rgb_weight_ref
  20.2 0.7 pad.14.rgb_cotangent_ref
  20.9 38.5 %gather_inputs.1 = (bf16[8,4,256,128]{3,2,1,0:T(8,128)(2,1)}, bf16[8,9,128,256]{3,2,1,0:T(8,128)(2,1)}, f32[8,8,128]{2,1,0:T(8,128)}, f32[8,256]{1,0:T(8,128)}) custom-call(f32[8,8,128]{2,1,0:T(8,128)} %get-tuple-element.80.style_ref, bf16[2,9,128,256]{3,2,1,0:T(8,128)(2,1)} %bitcast.42, bf16[8,256,128]{2,1,0:T(8,128)(2,1)} %get-tuple-element.81.parts_ref), custom_call_target="tpu_custom_call" | custom-call | tf_op jit(solution)/shard_map/gather_inputs/pallas_call | solution.py:258
  59.4 97.7 %conv_forward.1 = (bf16[256,1024]{1,0:T(8,128)(2,1)}, bf16[1024,256]{1,0:T(8,128)(2,1)}, f32[256,1024]{1,0:T(8,128)}, bf16[4,256,1024]{2,1,0:T(8,128)(2,1)}) custom-call(bf16[8,1024,128]{2,1,0:T(8,128)(2,1)} %bitcast.39, bf16[8,9,128,256]{3,2,1,0:T(8,128)(2,1)} %get-tuple-element.83.kernel_from, bf16[256,1024]{1,0:T(8,128)(2,1)} %bitcast.48, f32[1,1024]{1,0:T(1,128)} %bitcast.56), custom_call_target="tpu_custom_call" | custom-call | tf_op jit(solution)/shard_map/conv_forward/pallas_call | solution.py:592
  157.1 22.0 %attend_forward.1 = (bf16[1024,256]{1,0:T(8,128)(2,1)}, bf16[1024,256]{1,0:T(8,128)(2,1)}, bf16[1024,256]{1,0:T(8,128)(2,1)}, f32[1024,128]{1,0:T(8,128)}, bf16[...) custom-call(bf16[4,256,1024]{2,1,0:T(8,128)(2,1)} %get-tuple-element.84.normed_from, ...), custom_call_target="tpu_custom_call" | custom-call | tf_op jit(solution)/shard_map/attend_forward/pallas_call | solution.py:797
  179.2 0.5 broadcast_in_dim.35.penalty_ref
  179.7 36.7 %cross_part.1 = (f32[256,1024]{1,0:T(8,128)}, f32[256,128]{1,0:T(8,128)}, bf16[1024,256]{1,0:T(8,128)(2,1)}, bf16[4,128,512]{2,1,0:T(8,128)(2,1)}, f32[256,1024]...) custom-call(bf16[4,256,256]{2,1,0:T(8,128)(2,1)} %get-tuple-element., ...), custom_call_target="tpu_custom_call" | custom-call | tf_op jit(solution)/shard_map/cross_part/pallas_call | solution.py:1095
  216.4 1.6 copy.46
  218.1 70.7 %attend_backward.1 = (bf16[4,128,384]{2,1,0:T(8,128)(2,1)}, bf16[128,1152]{1,0:T(8,128)(2,1)}, bf16[128,512]{1,0:T(8,128)(2,1)}, f32[256,1024]{1,0:T(8,128)}, bf...) custom-call(bf16[4,256,256]{2,1,0:T(8,128)(2,1)} %get-tuple-element.93.grad_ref, ...), custom_call_target="tpu_custom_call" | custom-call | tf_op jit(solution)/shard_map/attend_backward/pallas_call | solution.py:1732
  288.8 81.7 %conv_backward.1 = (f32[2,9,128,256]{3,2,1,0:T(8,128)}, bf16[4,128,384]{2,1,0:T(8,128)(2,1)}, bf16[4,128,1152]{2,1,0:T(8,128)(2,1)}, bf16[4,128,512]{2,1,0:T(8,1...) custom-call(bf16[8,1024,128]{2,1,0:T(8,128)(2,1)} %bitcast.40, ...), custom_call_target="tpu_custom_call" | custom-call | tf_op jit(solution)/shard_map/conv_backward/pallas_call | solution.py:2336
  370.6 8.3 %finish.1 = (f32[128,1024]{1,0:T(8,128)}, f32[128,1024]{1,0:T(8,128)}, f32[128,1024]{1,0:T(8,128)}, f32[128,1024]{1,0:T(8,128)}, f32[128,1024]{1,0:T(8,128)}, /*...) custom-call(f32[8,8,1024]{2,1,0:T(8,128)} %get-tuple-element.107.row, ...), custom_call_target="tpu_custom_call" | custom-call | tf_op jit(solution)/shard_map/finish/pallas_call | solution.py:2611
  378.9 1.0 copy.54
  379.8 1.4 copy.55
  (17 shorter events, 0.1 us)
Async XLA Ops:
  7.2 149.9 %all-gather.3.cloned.1.call-start = ((), (), s32[]{:S(2)}) async-start(), calls=%async_computation | async-start | bytes 2949120 | tf_op jit(solution)/shard_map/all_gather | solution.py:2692
  9.2 5.1 %copy-start.4 = (s32[1,77]{1,0:T(1,128)S(1)}, s32[1,77]{1,0:T(1,128)}, u32[]{:S(2)}) copy-start(s32[1,77]{1,0:T(1,128)} %param.27) | copy-start | bytes 928
  12.9 6.2 %copy-start.2 = (f32[1,3,8,32]{3,2,1,0:T(8,128)S(1)}, f32[1,3,8,32]{3,2,1,0:T(8,128)}, u32[]{:S(2)}) copy-start(f32[1,3,8,32]{3,2,1,0:T(8,128)} %param.47) | copy-start | bytes 9220
  12.9 6.3 %copy-start.3 = (bf16[1024,3]{0,1:T(4,128)(2,1)S(1)}, bf16[1024,3]{0,1:T(4,128)(2,1)}, u32[]{:S(2)}) copy-start(bf16[1024,3]{0,1:T(4,128)(2,1)} %param.45) | copy-start | bytes 18436
  12.9 166.2 %all-gather.5.cloned.1.call-start = ((), (), s32[]{:S(2)}) async-start(), calls=%async_computation.1 | async-start | bytes 6488064 | tf_op jit(solution)/shard_map/all_gather | solution.py:2693
  370.5 8.3 %copy-start.1 = (f32[256,1024]{1,0:T(8,128)S(1)}, f32[256,1024]{1,0:T(8,128)}, u32[]{:S(2)}) copy-start(f32[256,1024]{1,0:T(8,128)} %get-tuple-element.91) | copy-start | bytes 3145732
  370.5 9.3 %copy-start = (f32[2,9,128,256]{3,2,1,0:T(8,128)S(1)}, f32[2,9,128,256]{3,2,1,0:T(8,128)}, u32[]{:S(2)}) copy-start(f32[2,9,128,256]{3,2,1,0:T(8,128)} %get-tuple-element.125) | copy-start | bytes 7077892
Sparse Core Ops, SparseCore 0:
  13.0 74.6 all-gather.2
  91.2 74.1 all-gather.4
